TPU v7x, 512 devices: a whole 4x4x16 slice. The times are simulated.
512 devices in a mesh: pipe: 4 (over y_lo, core), ctx: 16 (over z), tp: 8 (over y_hi, x).
Axes of the slice: x: 4, y: 4 (y_hi: 2, y_lo: 2; y = y_hi * 2 + y_lo), z: 16, core: 2. Of those that a mesh axis runs over, the one named last changes fastest.
Arguments:
- section_in: bfloat16 [4, 4096, 4096], P('pipe', 'ctx', 'tp'), may hold values from -6 to 6
- stretch_order: int32 [32], replicated, may hold values from 0 to 31, each once
- norm_gain: float32 [4, 4096], P('pipe', 'tp'), may hold values from 0.25 to 1.75
- w_query: bfloat16 [4, 4096, 4096], P('pipe', 'ctx', 'tp'), may hold values from -1 to 1
- w_key: bfloat16 [4, 4096, 1024], P('pipe', 'ctx', 'tp'), may hold values from -1 to 1
- w_value: bfloat16 [4, 4096, 1024], P('pipe', 'ctx', 'tp'), may hold values from -0.09375 to 0.09375
- w_out: bfloat16 [4, 4096, 4096], P('pipe', 'tp', 'ctx'), may hold values from -0.375 to 0.375
Outputs:
- section_out: bfloat16 [4, 4096, 4096], P('pipe', 'ctx', 'tp')
Inputs may be any that keep to these rules, and one draw needn't show every extreme that they name: stretch_order holds each number of 0 to 2 * 16 - 1 once.
All inputs are finite; a program needn't handle non-finite values.
Results may differ from a plain program's by a relative error of at most 0.035.
Values may be sent and summed in bfloat16 or wider, within the bound.
No kernel may reach another device: no remote copies, remote signals or barrier semaphores. Data moves between devices by JAX's collectives and lax.ppermute only.
A program may use at most 64 MiB of HBM per device.

v0:
```python
import jax
import jax.numpy as jnp
from jax import lax
from jax.sharding import PartitionSpec as P

HD = 128


EPS = 1e-05
THETA = 500000.0


def passed_along(value, axis, by):
    length = lax.axis_size(axis)
    return lax.ppermute(value, axis, [(i, (i + by) % length) for i in range(length)])


def rotate(values, pos):
    half = values.shape[-1] // 2
    index = jnp.arange(half, dtype=jnp.float32)
    freq = THETA ** (-2.0 * index / values.shape[-1])
    angle = pos.astype(jnp.float32)[:, None] * freq[None, :]
    cosine = jnp.cos(angle)[:, None, :]
    sine = jnp.sin(angle)[:, None, :]
    first = values[..., :half]
    second = values[..., half:]
    return jnp.concatenate(
        [first * cosine - second * sine, second * cosine + first * sine], axis=-1
    )


def positions_of(stored, stretch_order, block):
    which = stored // block
    slots = jnp.arange(stretch_order.shape[0], dtype=jnp.int32)
    picked = jnp.sum(jnp.where(which[:, None] == slots[None, :], stretch_order[None, :], 0), axis=1)
    return picked * block + stored % block


def attend(state, query, query_pos, keys_values, key_pos):
    peak, total, accum = state
    scores = jnp.einsum(
        "qhd,kd->hqk", query, keys_values[0], preferred_element_type=jnp.float32
    ) * (1.0 / HD**0.5)
    allowed = key_pos[None, None, :] <= query_pos[None, :, None]
    scores = jnp.where(allowed, scores, -1e30)
    new_peak = jnp.maximum(peak, jnp.max(scores, axis=2))
    probs = jnp.where(allowed, jnp.exp(scores - new_peak[:, :, None]), 0.0)
    factor = jnp.exp(peak - new_peak)
    total = total * factor + jnp.sum(probs, axis=2)
    mixed = jnp.einsum(
        "hqk,kd->hqd",
        probs.astype(jnp.bfloat16),
        keys_values[1],
        preferred_element_type=jnp.float32,
    )
    accum = accum * factor[:, :, None] + mixed
    return (new_peak, total, accum)


def shards(section_in, stretch_order, norm_gain, w_query, w_key, w_value, w_out):
    hidden = section_in[0]
    rows = hidden.shape[0]
    block = rows // 2
    n_ctx = lax.axis_size("ctx")
    me = lax.axis_index("ctx")
    width = hidden.shape[1] * lax.axis_size("tp")
    local = hidden.astype(jnp.float32)
    squares = lax.psum(jnp.sum(local * local, axis=1), "tp")
    factor = lax.rsqrt(squares / width + EPS)
    part_normed = (local * factor[:, None] * norm_gain[0][None, :]).astype(jnp.bfloat16)
    normed = lax.all_gather(part_normed, "tp", axis=1, tiled=True)
    pieces = (
        lax.all_gather(w_query, "ctx", axis=1, tiled=True),
        lax.all_gather(w_key, "ctx", axis=1, tiled=True),
        lax.all_gather(w_value, "ctx", axis=1, tiled=True),
    )
    query_raw, key_raw, value_raw = tuple(
        (jnp.dot(normed, piece[0], preferred_element_type=jnp.float32) for piece in pieces)
    )
    heads = w_query.shape[2] // HD
    local_rows = jnp.arange(rows, dtype=jnp.int32)
    query_pos = positions_of(me * rows + local_rows, stretch_order, block)
    query = rotate(query_raw.reshape(rows, heads, HD), query_pos).astype(jnp.bfloat16)
    key = rotate(key_raw.reshape(rows, 1, HD), query_pos).astype(jnp.bfloat16)[:, 0, :]
    value = value_raw.astype(jnp.bfloat16)
    keys_values = jnp.stack([key, value], axis=0)
    state = (
        jnp.full((heads, rows), -1e30, jnp.float32),
        jnp.zeros((heads, rows), jnp.float32),
        jnp.zeros((heads, rows, HD), jnp.float32),
    )

    def cycle_turn(turn, carry):
        current, held = carry
        source = (me - turn) % n_ctx
        key_pos = positions_of(source * rows + local_rows, stretch_order, block)
        current = attend(current, query, query_pos, held, key_pos)
        held = passed_along(held, "ctx", 1)
        return (current, held)

    state, keys_values = lax.fori_loop(0, n_ctx - 1, cycle_turn, (state, keys_values))
    source = (me - (n_ctx - 1)) % n_ctx
    state = attend(
        state,
        query,
        query_pos,
        keys_values,
        positions_of(source * rows + local_rows, stretch_order, block),
    )
    peak, total, accum = state
    context = (
        (accum / total[:, :, None])
        .transpose(1, 0, 2)
        .reshape(rows, heads * HD)
        .astype(jnp.bfloat16)
    )
    terms = jnp.dot(
        context,
        lax.all_gather(w_out, "ctx", axis=2, tiled=True)[0],
        preferred_element_type=jnp.float32,
    )
    summed = lax.psum_scatter(
        terms.astype(jnp.bfloat16), "tp", scatter_dimension=1, tiled=True
    ).astype(jnp.float32)
    result = (hidden.astype(jnp.float32) + summed).astype(jnp.bfloat16)[None]
    return passed_along(result, "pipe", 1)


def solution(mesh):
    in_specs = (
        P("pipe", "ctx", "tp"),
        P(),
        P("pipe", "tp"),
        P("pipe", "ctx", "tp"),
        P("pipe", "ctx", "tp"),
        P("pipe", "ctx", "tp"),
        P("pipe", "tp", "ctx"),
    )
    out_specs = P("pipe", "ctx", "tp")
    return jax.shard_map(shards, mesh=mesh, in_specs=in_specs, out_specs=out_specs, check_vma=False)
```

profile of v0, /device:TPU:6, one launch (start us, length us, event | category | flops | bytes accessed | tf_op | source)
XLA Modules:
  0.0 565.0 jit_solution(10237172937348808350)
XLA Ops:
  8.4 20.6 %psum.7 = f32[256]{0:T(256)S(1)} all-reduce(f32[256]{0:T(256)S(1)} %fusion.31), channel_id=1, replica_groups=mesh['pipe'=4,'ctx'=16,'tp'=8] {'tp'}, use_global_device_ids=true, to_apply=%region_1.0 | all-reduce | flops 256 | bytes 2048 | tf_op jit(solution)/shard_map/psum | solution.py:68
  34.0 50.9 %all-gather.8.cloned.1.call-done = bf16[1,4096,128]{2,1,0:T(8,128)(2,1)} async-done(((bf16[1,256,128]{2,1,0:T(8,128)(2,1)}), bf16[1,4096,128]{2,1,0:T(8,128)(2,1)}) %all-gather.8.cloned.1.call-update) | async-done | bytes 1048592 | tf_op jit(solution)/shard_map/all_gather | solution.py:74
  85.0 72.6 %all-gather.6.cloned.1.call-done = bf16[256,4096]{1,0:T(8,128)(2,1)} async-done(((bf16[256,512]{1,0:T(8,128)(2,1)}), bf16[256,4096]{1,0:T(8,128)(2,1)}) %all-gather.6.cloned.1.call-update) | async-done | bytes 2097168 | tf_op jit(solution)/shard_map/all_gather | solution.py:71
  157.6 2.8 convolution_bitcast_fusion
  160.8 69.2 %all-gather.10.cloned.1.call-done = bf16[1,4096,128]{2,1,0:T(8,128)(2,1)} async-done(((bf16[1,256,128]{2,1,0:T(8,128)(2,1)}), bf16[1,4096,128]{2,1,0:T(8,128)(2,1)}) %all-gather.10.cloned.1.call-update) | async-done | bytes 1048592 | tf_op jit(solution)/shard_map/all_gather | solution.py:75
  232.1 75.5 %all-gather.12.cloned.1.call-done = bf16[1,4096,512]{2,1,0:T(8,128)(2,1)} async-done(((bf16[1,256,512]{2,1,0:T(8,128)(2,1)}), bf16[1,4096,512]{2,1,0:T(8,128)(2,1)}) %all-gather.12.cloned.1.call-update) | async-done | bytes 4194320 | tf_op jit(solution)/shard_map/all_gather | solution.py:73
  307.6 6.4 %copy.19 = bf16[512,4096]{1,0:T(8,128)(2,1)} copy(bf16[512,4096]{0,1:T(8,128)(2,1)} %bitcast.74) | data formatting | bytes 8388608 | tf_op jit(solution)/shard_map/dot_general | solution.py:78
  314.0 3.5 fusion.20
  317.8 135.2 %while.23 = (s32[]{:T(128)}, f32[4,256]{1,0:T(4,128)S(1)}, f32[4,256]{1,0:T(4,128)S(1)}, f32[4,256,128]{2,1,0:T(8,128)S(1)}, bf16[2,256,128]{2,1,0:T(8,128)(2,1)...) while((s32[]{:T(128)}, f32[4,256]{1,0:T(4,128)S(1)}, ...), condition=%wide.region_7.8_spmd.clone, body=%wide.region_3.7_spmd.clone.sunk | while | flops 137072912 | bytes 5709254 | solution.py:101
  317.8 3.3 collective-permute-start
  322.5 4.4 collective-permute-done
  326.8 4.4 collective-permute-start
  332.6 4.7 collective-permute-done
  337.3 3.0 collective-permute-start
  341.7 6.3 %collective-permute-done = bf16[2,256,128]{2,1,0:T(8,128)(2,1)S(1)} collective-permute-done((bf16[2,256,128]{2,1,0:T(8,128)(2,1)S(1)}, bf16[2,256,128]{2,1,0:T(8,128)(2,1)S(1)}, u32[]{:S(2)}, u32[]{:S(2)}) %collective-permute-start) | collective-permute-done | bytes 131104 | tf_op jit(solution)/shard_map/while/body/eval_jaxpr/ppermute | solution.py:15
  351.3 5.3 collective-permute-done
  356.7 3.8 collective-permute-start
  361.8 6.3 %collective-permute-done = bf16[2,256,128]{2,1,0:T(8,128)(2,1)S(1)} collective-permute-done((bf16[2,256,128]{2,1,0:T(8,128)(2,1)S(1)}, bf16[2,256,128]{2,1,0:T(8,128)(2,1)S(1)}, u32[]{:S(2)}, u32[]{:S(2)}) %collective-permute-start) | collective-permute-done | bytes 131104 | tf_op jit(solution)/shard_map/while/body/eval_jaxpr/ppermute | solution.py:15
  371.4 5.7 %collective-permute-done = bf16[2,256,128]{2,1,0:T(8,128)(2,1)S(1)} collective-permute-done((bf16[2,256,128]{2,1,0:T(8,128)(2,1)S(1)}, bf16[2,256,128]{2,1,0:T(8,128)(2,1)S(1)}, u32[]{:S(2)}, u32[]{:S(2)}) %collective-permute-start) | collective-permute-done | bytes 131104 | tf_op jit(solution)/shard_map/while/body/eval_jaxpr/ppermute | solution.py:15
  381.0 4.4 collective-permute-done
  388.7 7.3 %collective-permute-done = bf16[2,256,128]{2,1,0:T(8,128)(2,1)S(1)} collective-permute-done((bf16[2,256,128]{2,1,0:T(8,128)(2,1)S(1)}, bf16[2,256,128]{2,1,0:T(8,128)(2,1)S(1)}, u32[]{:S(2)}, u32[]{:S(2)}) %collective-permute-start) | collective-permute-done | bytes 131104 | tf_op jit(solution)/shard_map/while/body/eval_jaxpr/ppermute | solution.py:15
  399.3 4.8 collective-permute-done
  404.1 3.7 collective-permute-start
  409.2 3.3 collective-permute-done
  416.4 4.2 collective-permute-done
  424.6 4.1 collective-permute-done
  432.0 4.8 collective-permute-done
  440.1 4.8 collective-permute-done
  448.2 4.8 collective-permute-done
  454.2 4.8 convolution_convert_fusion
  459.0 89.7 %reduce-scatter.2.cloned.1.call-done = bf16[256,512]{1,0:T(8,128)(2,1)} async-done(((bf16[256,4096]{1,0:T(8,128)(2,1)}), bf16[256,512]{1,0:T(8,128)(2,1)}) %reduce-scatter.2.cloned.1.call-update) | async-done | bytes 262160 | tf_op jit(solution)/shard_map/reduce_scatter | solution.py:122
  551.6 5.8 %collective-permute-done.1 = bf16[1,256,512]{2,1,0:T(8,128)(2,1)S(1)} collective-permute-done((bf16[1,256,512]{2,1,0:T(8,128)(2,1)S(1)}, bf16[1,256,512]{2,1,0:T(8,128)(2,1)S(1)}, u32[]{:S(2)}, u32[]{:S(2)}) %collective-permute-start.1) | collective-permute-done | bytes 262176 | tf_op jit(solution)/shard_map/ppermute | solution.py:15
  (224 shorter events, 54.9 us)
Async XLA Ops:
  6.5 78.4 %all-gather.8.cloned.1.call-start = ((), (), s32[]{:S(2)}) async-start(), calls=%async_computation.2 | async-start | bytes 1114112 | tf_op jit(solution)/shard_map/all_gather | solution.py:74
  7.3 150.3 %all-gather.6.cloned.1.call-start = ((), (), s32[]{:S(2)}) async-start(), calls=%async_computation.1 | async-start | bytes 2359296 | tf_op jit(solution)/shard_map/all_gather | solution.py:71
  30.8 199.1 %all-gather.10.cloned.1.call-start = ((), (), s32[]{:S(2)}) async-start(), calls=%async_computation.3 | async-start | bytes 1114112 | tf_op jit(solution)/shard_map/all_gather | solution.py:75
  31.5 276.1 %all-gather.12.cloned.1.call-start = ((), (), s32[]{:S(2)}) async-start(), calls=%async_computation.4 | async-start | bytes 4456448 | tf_op jit(solution)/shard_map/all_gather | solution.py:73
  32.1 422.1 %all-gather.14.cloned.1.call-start = ((), (), s32[]{:S(2)}) async-start(), calls=%async_computation.5 | async-start | bytes 4456448 | tf_op jit(solution)/shard_map/all_gather | solution.py:119
  32.7 516.0 %reduce-scatter.2.cloned.1.call-start = ((), (), s32[]{:S(2)}) async-start(), calls=%async_computation.6 | async-start | bytes 2359296 | tf_op jit(solution)/shard_map/reduce_scatter | solution.py:122
  157.6 72.3 %copy-start = (bf16[256,4096]{1,0:T(8,128)(2,1)S(1)}, bf16[256,4096]{1,0:T(8,128)(2,1)}, u32[]{:S(2)}) copy-start(bf16[256,4096]{1,0:T(8,128)(2,1)} %all-gather.6.cloned.1.call-done) | copy-start | bytes 6291460
  314.0 3.8 copy-start.2
  317.8 9.0 %collective-permute-start = (bf16[2,256,128]{2,1,0:T(8,128)(2,1)S(1)}, bf16[2,256,128]{2,1,0:T(8,128)(2,1)S(1)}, u32[]{:S(2)}, u32[]{:S(2)}) collective-permute-start(bf16[2,256,128]{2,1,0:T(8,128)(2,1)S(1)} %copy.39), channel_id=1, source_target_pairs={{0,8},{8,16},{16,24},{24,32},{32,40},{40,48},{48,56},{56,64},{64,7... | collective-permute-start | bytes 393224 | tf_op jit(solution)/shard_map/while/body/eval_jaxpr/ppermute | solution.py:15
  326.8 10.4 %collective-permute-start = (bf16[2,256,128]{2,1,0:T(8,128)(2,1)S(1)}, bf16[2,256,128]{2,1,0:T(8,128)(2,1)S(1)}, u32[]{:S(2)}, u32[]{:S(2)}) collective-permute-start(bf16[2,256,128]{2,1,0:T(8,128)(2,1)S(1)} %copy.39), channel_id=1, source_target_pairs={{0,8},{8,16},{16,24},{24,32},{32,40},{40,48},{48,56},{56,64},{64,7... | collective-permute-start | bytes 393224 | tf_op jit(solution)/shard_map/while/body/eval_jaxpr/ppermute | solution.py:15
  337.3 10.7 %collective-permute-start = (bf16[2,256,128]{2,1,0:T(8,128)(2,1)S(1)}, bf16[2,256,128]{2,1,0:T(8,128)(2,1)S(1)}, u32[]{:S(2)}, u32[]{:S(2)}) collective-permute-start(bf16[2,256,128]{2,1,0:T(8,128)(2,1)S(1)} %copy.39), channel_id=1, source_target_pairs={{0,8},{8,16},{16,24},{24,32},{32,40},{40,48},{48,56},{56,64},{64,7... | collective-permute-start | bytes 393224 | tf_op jit(solution)/shard_map/while/body/eval_jaxpr/ppermute | solution.py:15
  348.0 8.6 %collective-permute-start = (bf16[2,256,128]{2,1,0:T(8,128)(2,1)S(1)}, bf16[2,256,128]{2,1,0:T(8,128)(2,1)S(1)}, u32[]{:S(2)}, u32[]{:S(2)}) collective-permute-start(bf16[2,256,128]{2,1,0:T(8,128)(2,1)S(1)} %copy.39), channel_id=1, source_target_pairs={{0,8},{8,16},{16,24},{24,32},{32,40},{40,48},{48,56},{56,64},{64,7... | collective-permute-start | bytes 393224 | tf_op jit(solution)/shard_map/while/body/eval_jaxpr/ppermute | solution.py:15
  356.7 11.4 %collective-permute-start = (bf16[2,256,128]{2,1,0:T(8,128)(2,1)S(1)}, bf16[2,256,128]{2,1,0:T(8,128)(2,1)S(1)}, u32[]{:S(2)}, u32[]{:S(2)}) collective-permute-start(bf16[2,256,128]{2,1,0:T(8,128)(2,1)S(1)} %copy.39), channel_id=1, source_target_pairs={{0,8},{8,16},{16,24},{24,32},{32,40},{40,48},{48,56},{56,64},{64,7... | collective-permute-start | bytes 393224 | tf_op jit(solution)/shard_map/while/body/eval_jaxpr/ppermute | solution.py:15
  368.1 8.9 %collective-permute-start = (bf16[2,256,128]{2,1,0:T(8,128)(2,1)S(1)}, bf16[2,256,128]{2,1,0:T(8,128)(2,1)S(1)}, u32[]{:S(2)}, u32[]{:S(2)}) collective-permute-start(bf16[2,256,128]{2,1,0:T(8,128)(2,1)S(1)} %copy.39), channel_id=1, source_target_pairs={{0,8},{8,16},{16,24},{24,32},{32,40},{40,48},{48,56},{56,64},{64,7... | collective-permute-start | bytes 393224 | tf_op jit(solution)/shard_map/while/body/eval_jaxpr/ppermute | solution.py:15
  377.1 8.4 %collective-permute-start = (bf16[2,256,128]{2,1,0:T(8,128)(2,1)S(1)}, bf16[2,256,128]{2,1,0:T(8,128)(2,1)S(1)}, u32[]{:S(2)}, u32[]{:S(2)}) collective-permute-start(bf16[2,256,128]{2,1,0:T(8,128)(2,1)S(1)} %copy.39), channel_id=1, source_target_pairs={{0,8},{8,16},{16,24},{24,32},{32,40},{40,48},{48,56},{56,64},{64,7... | collective-permute-start | bytes 393224 | tf_op jit(solution)/shard_map/while/body/eval_jaxpr/ppermute | solution.py:15
  385.5 10.6 %collective-permute-start = (bf16[2,256,128]{2,1,0:T(8,128)(2,1)S(1)}, bf16[2,256,128]{2,1,0:T(8,128)(2,1)S(1)}, u32[]{:S(2)}, u32[]{:S(2)}) collective-permute-start(bf16[2,256,128]{2,1,0:T(8,128)(2,1)S(1)} %copy.39), channel_id=1, source_target_pairs={{0,8},{8,16},{16,24},{24,32},{32,40},{40,48},{48,56},{56,64},{64,7... | collective-permute-start | bytes 393224 | tf_op jit(solution)/shard_map/while/body/eval_jaxpr/ppermute | solution.py:15
  396.0 8.1 %collective-permute-start = (bf16[2,256,128]{2,1,0:T(8,128)(2,1)S(1)}, bf16[2,256,128]{2,1,0:T(8,128)(2,1)S(1)}, u32[]{:S(2)}, u32[]{:S(2)}) collective-permute-start(bf16[2,256,128]{2,1,0:T(8,128)(2,1)S(1)} %copy.39), channel_id=1, source_target_pairs={{0,8},{8,16},{16,24},{24,32},{32,40},{40,48},{48,56},{56,64},{64,7... | collective-permute-start | bytes 393224 | tf_op jit(solution)/shard_map/while/body/eval_jaxpr/ppermute | solution.py:15
  404.1 8.4 %collective-permute-start = (bf16[2,256,128]{2,1,0:T(8,128)(2,1)S(1)}, bf16[2,256,128]{2,1,0:T(8,128)(2,1)S(1)}, u32[]{:S(2)}, u32[]{:S(2)}) collective-permute-start(bf16[2,256,128]{2,1,0:T(8,128)(2,1)S(1)} %copy.39), channel_id=1, source_target_pairs={{0,8},{8,16},{16,24},{24,32},{32,40},{40,48},{48,56},{56,64},{64,7... | collective-permute-start | bytes 393224 | tf_op jit(solution)/shard_map/while/body/eval_jaxpr/ppermute | solution.py:15
  412.6 8.1 %collective-permute-start = (bf16[2,256,128]{2,1,0:T(8,128)(2,1)S(1)}, bf16[2,256,128]{2,1,0:T(8,128)(2,1)S(1)}, u32[]{:S(2)}, u32[]{:S(2)}) collective-permute-start(bf16[2,256,128]{2,1,0:T(8,128)(2,1)S(1)} %copy.39), channel_id=1, source_target_pairs={{0,8},{8,16},{16,24},{24,32},{32,40},{40,48},{48,56},{56,64},{64,7... | collective-permute-start | bytes 393224 | tf_op jit(solution)/shard_map/while/body/eval_jaxpr/ppermute | solution.py:15
  420.6 8.1 %collective-permute-start = (bf16[2,256,128]{2,1,0:T(8,128)(2,1)S(1)}, bf16[2,256,128]{2,1,0:T(8,128)(2,1)S(1)}, u32[]{:S(2)}, u32[]{:S(2)}) collective-permute-start(bf16[2,256,128]{2,1,0:T(8,128)(2,1)S(1)} %copy.39), channel_id=1, source_target_pairs={{0,8},{8,16},{16,24},{24,32},{32,40},{40,48},{48,56},{56,64},{64,7... | collective-permute-start | bytes 393224 | tf_op jit(solution)/shard_map/while/body/eval_jaxpr/ppermute | solution.py:15
  428.7 8.1 %collective-permute-start = (bf16[2,256,128]{2,1,0:T(8,128)(2,1)S(1)}, bf16[2,256,128]{2,1,0:T(8,128)(2,1)S(1)}, u32[]{:S(2)}, u32[]{:S(2)}) collective-permute-start(bf16[2,256,128]{2,1,0:T(8,128)(2,1)S(1)} %copy.39), channel_id=1, source_target_pairs={{0,8},{8,16},{16,24},{24,32},{32,40},{40,48},{48,56},{56,64},{64,7... | collective-permute-start | bytes 393224 | tf_op jit(solution)/shard_map/while/body/eval_jaxpr/ppermute | solution.py:15
  436.8 8.1 %collective-permute-start = (bf16[2,256,128]{2,1,0:T(8,128)(2,1)S(1)}, bf16[2,256,128]{2,1,0:T(8,128)(2,1)S(1)}, u32[]{:S(2)}, u32[]{:S(2)}) collective-permute-start(bf16[2,256,128]{2,1,0:T(8,128)(2,1)S(1)} %copy.39), channel_id=1, source_target_pairs={{0,8},{8,16},{16,24},{24,32},{32,40},{40,48},{48,56},{56,64},{64,7... | collective-permute-start | bytes 393224 | tf_op jit(solution)/shard_map/while/body/eval_jaxpr/ppermute | solution.py:15
  444.9 8.1 %collective-permute-start = (bf16[2,256,128]{2,1,0:T(8,128)(2,1)S(1)}, bf16[2,256,128]{2,1,0:T(8,128)(2,1)S(1)}, u32[]{:S(2)}, u32[]{:S(2)}) collective-permute-start(bf16[2,256,128]{2,1,0:T(8,128)(2,1)S(1)} %copy.39), channel_id=1, source_target_pairs={{0,8},{8,16},{16,24},{24,32},{32,40},{40,48},{48,56},{56,64},{64,7... | collective-permute-start | bytes 393224 | tf_op jit(solution)/shard_map/while/body/eval_jaxpr/ppermute | solution.py:15
  459.0 89.7 %copy-start.1 = (bf16[1,256,512]{2,1,0:T(8,128)(2,1)S(1)}, bf16[1,256,512]{2,1,0:T(8,128)(2,1)}, u32[]{:S(2)}) copy-start(bf16[1,256,512]{2,1,0:T(8,128)(2,1)} %param.9) | copy-start | bytes 786436
  549.7 7.7 %collective-permute-start.1 = (bf16[1,256,512]{2,1,0:T(8,128)(2,1)S(1)}, bf16[1,256,512]{2,1,0:T(8,128)(2,1)S(1)}, u32[]{:S(2)}, u32[]{:S(2)}) collective-permute-start(bf16[1,256,512]{2,1,0:T(8,128)(2,1)S(1)} %fusion.39), channel_id=1, source_target_pairs={{0,128},{128,256},{256,384},{384,0},{1,129},{129,257},{257,385},{3... | collective-permute-start | bytes 786440 | tf_op jit(solution)/shard_map/ppermute | solution.py:15
Sparse Core Ops, SparseCore 0:
  9.4 75.4 all-gather.7
  88.0 69.5 all-gather.5
  159.7 70.2 all-gather.9
  231.9 75.6 all-gather.11
  309.4 105.0 all-gather.13
  459.2 89.4 reduce-scatter.1
where the time goes:
time: 566 us; the launch traced here: 565 us
  waiting for transfers between devices  441 us (78%)
  starting transfers between devices  41.5 us (7%)
  matrix products  26.2 us (5%)
  blocking collectives  20.6 us (4%)
  between operations  13.7 us (2%)
  other arithmetic  12.6 us (2%)
  local copies, waits for them, and re-layouts  7.89 us (1%)
    reduce_scatter x1, waiting for transfers between devices, shards(): lax.psum_scatter(terms.astype(jnp.bfloat16), 'tp', scatter_dimension=1, t...  89.7 us
    ppermute x16, waiting for transfers between devices, passed_along(): lax.ppermute(value, axis, [(i, (i + by) % length) for i in range(length)])  81 us
    all_gather x1, waiting for transfers between devices, shards(): lax.all_gather(w_query, 'ctx', axis=1, tiled=True)  75.5 us
    all_gather x1, waiting for transfers between devices, shards(): normed = lax.all_gather(part_normed, 'tp', axis=1, tiled=True)  72.6 us
    all_gather x1, waiting for transfers between devices, shards(): lax.all_gather(w_value, 'ctx', axis=1, tiled=True)  69.2 us
    all_gather x1, waiting for transfers between devices, shards(): lax.all_gather(w_key, 'ctx', axis=1, tiled=True)  50.9 us
    ppermute x16, starting transfers between devices, passed_along(): lax.ppermute(value, axis, [(i, (i + by) % length) for i in range(length)])  41.3 us
    psum x1, blocking collectives, shards(): squares = lax.psum(jnp.sum(local * local, axis=1), 'tp')  20.6 us
  transfers between devices with their start and end apart: 22, of which 21 were waited for; matrix products, arithmetic and copies ran while one was open for 7% of the time, Pallas kernels for 0%

commit v1 on v0

--- a/solution.py
+++ b/solution.py
@@ -59,30 +59,34 @@
 
 def shards(section_in, stretch_order, norm_gain, w_query, w_key, w_value, w_out):
     hidden = section_in[0]
-    rows = hidden.shape[0]
+    rows, part = hidden.shape
     block = rows // 2
     n_ctx = lax.axis_size("ctx")
+    n_tp = lax.axis_size("tp")
     me = lax.axis_index("ctx")
-    width = hidden.shape[1] * lax.axis_size("tp")
+    width = part * n_tp
+    heads = w_query.shape[2] // HD
+    w_mine = jnp.concatenate([w_query[0], w_key[0], w_value[0]], axis=1)
+    w_all = lax.all_gather(w_mine, "ctx", axis=0, tiled=True)
     local = hidden.astype(jnp.float32)
     squares = lax.psum(jnp.sum(local * local, axis=1), "tp")
     factor = lax.rsqrt(squares / width + EPS)
     part_normed = (local * factor[:, None] * norm_gain[0][None, :]).astype(jnp.bfloat16)
-    normed = lax.all_gather(part_normed, "tp", axis=1, tiled=True)
-    pieces = (
-        lax.all_gather(w_query, "ctx", axis=1, tiled=True),
-        lax.all_gather(w_key, "ctx", axis=1, tiled=True),
-        lax.all_gather(w_value, "ctx", axis=1, tiled=True),
+    w_out_mine, part_normed = lax.optimization_barrier((w_out[0], part_normed))
+    w_out_all = lax.all_gather(w_out_mine, "ctx", axis=0, tiled=False)
+    normed = lax.all_to_all(
+        jnp.broadcast_to(part_normed[None], (n_tp, rows, part)), "tp", 0, 0
     )
-    query_raw, key_raw, value_raw = tuple(
-        (jnp.dot(normed, piece[0], preferred_element_type=jnp.float32) for piece in pieces)
-    )
-    heads = w_query.shape[2] // HD
+    normed = normed.transpose(1, 0, 2).reshape(rows, width)
+    raw = jnp.dot(normed, w_all, preferred_element_type=jnp.float32)
     local_rows = jnp.arange(rows, dtype=jnp.int32)
     query_pos = positions_of(me * rows + local_rows, stretch_order, block)
-    query = rotate(query_raw.reshape(rows, heads, HD), query_pos).astype(jnp.bfloat16)
-    key = rotate(key_raw.reshape(rows, 1, HD), query_pos).astype(jnp.bfloat16)[:, 0, :]
-    value = value_raw.astype(jnp.bfloat16)
+    turned = rotate(raw[:, : (heads + 1) * HD].reshape(rows, heads + 1, HD), query_pos).astype(
+        jnp.bfloat16
+    )
+    query = turned[:, :heads]
+    key = turned[:, heads]
+    value = raw[:, (heads + 1) * HD :].astype(jnp.bfloat16)
     keys_values = jnp.stack([key, value], axis=0)
     state = (
         jnp.full((heads, rows), -1e30, jnp.float32),
@@ -90,23 +94,23 @@
         jnp.zeros((heads, rows, HD), jnp.float32),
     )
 
-    def cycle_turn(turn, carry):
-        current, held = carry
-        source = (me - turn) % n_ctx
-        key_pos = positions_of(source * rows + local_rows, stretch_order, block)
-        current = attend(current, query, query_pos, held, key_pos)
-        held = passed_along(held, "ctx", 1)
-        return (current, held)
+    def pos_of(source):
+        return positions_of((source % n_ctx) * rows + local_rows, stretch_order, block)
 
-    state, keys_values = lax.fori_loop(0, n_ctx - 1, cycle_turn, (state, keys_values))
-    source = (me - (n_ctx - 1)) % n_ctx
-    state = attend(
-        state,
-        query,
-        query_pos,
-        keys_values,
-        positions_of(source * rows + local_rows, stretch_order, block),
-    )
+    up = down = keys_values
+    held, held_pos = keys_values, query_pos
+    for turn in range(1, n_ctx // 2 + 1):
+        last = turn == n_ctx // 2
+        new_up = passed_along(up, "ctx", 1)
+        new_down = down if last else passed_along(down, "ctx", -1)
+        state = attend(state, query, query_pos, held, held_pos)
+        up, down, state = lax.optimization_barrier((new_up, new_down, state))
+        if last:
+            held, held_pos = up, pos_of(me - turn)
+        else:
+            held = jnp.concatenate([up, down], axis=1)
+            held_pos = jnp.concatenate([pos_of(me - turn), pos_of(me + turn)])
+    state = attend(state, query, query_pos, held, held_pos)
     peak, total, accum = state
     context = (
         (accum / total[:, :, None])
@@ -114,14 +118,14 @@
         .reshape(rows, heads * HD)
         .astype(jnp.bfloat16)
     )
-    terms = jnp.dot(
-        context,
-        lax.all_gather(w_out, "ctx", axis=2, tiled=True)[0],
-        preferred_element_type=jnp.float32,
-    )
-    summed = lax.psum_scatter(
-        terms.astype(jnp.bfloat16), "tp", scatter_dimension=1, tiled=True
-    ).astype(jnp.float32)
+    terms = jnp.einsum(
+        "rk,ckn->crn", context, w_out_all, preferred_element_type=jnp.float32
+    ).astype(jnp.bfloat16)
+    per = n_ctx // n_tp
+    terms = terms.reshape(n_tp, per, rows, part // per)
+    parts = lax.all_to_all(terms, "tp", 0, 0)
+    summed = jnp.sum(parts.astype(jnp.float32), axis=0)
+    summed = summed.transpose(1, 0, 2).reshape(rows, part)
     result = (hidden.astype(jnp.float32) + summed).astype(jnp.bfloat16)[None]
     return passed_along(result, "pipe", 1)
 

time: 566 us -> 247 us (0.44)
  waiting for transfers between devices: 441 us -> 82.4 us
  blocking collectives: 20.6 us -> 47 us
  starting transfers between devices: 41.5 us -> 65 us
  matrix products: 26.2 us -> 18.7 us
    all_gather x5 -> x2, waiting for transfers between devices: 268 us -> 37 us  [the longest x1 37 us: shards(): w_all = lax.all_gather(w_mine, 'ctx', axis=0, tiled=True)]
    reduce_scatter x1 -> x0, waiting for transfers between devices: 89.7 us -> none  [shards(): lax.psum_scatter(terms.astype(jnp.bfloat16), 'tp', scatter_dimension=1, t...]
    ppermute x16, waiting for transfers between devices: 81 us -> 27.4 us  [passed_along(): lax.ppermute(value, axis, [(i, (i + by) % length) for i in range(length)])]
    all_to_all x0 -> x1, blocking collectives: none -> 26.4 us  [shards(): parts = lax.all_to_all(terms, 'tp', 0, 0)]
    all_to_all x0 -> x1, waiting for transfers between devices: none -> 17.2 us  [shards(): lax.all_to_all(jnp.broadcast_to(part_normed[None], (n_tp, rows, part)), '...]
    ppermute x16, starting transfers between devices: 41.3 us -> 57.1 us  [passed_along(): lax.ppermute(value, axis, [(i, (i + by) % length) for i in range(length)])]
    all_to_all x0 -> x1, starting transfers between devices: none -> 7.89 us  [shards(): lax.all_to_all(jnp.broadcast_to(part_normed[None], (n_tp, rows, part)), '...]
    dot_general x1 -> x0, local copies, waits for them, and re-layouts: 6.4 us -> none  [shards(): jnp.dot(normed, piece[0], preferred_element_type=jnp.float32)]
  transfers between devices with their start and end apart: 22 -> 19, of which waited for: 21 -> 16; matrix products, arithmetic and copies ran while one was open for 7% -> 12% of each run, Pallas kernels for 0% -> 0%
where the time goes in v1:
time: 247 us; the launch traced here: 245 us
  waiting for transfers between devices  82.4 us (33%)
  starting transfers between devices  65 us (26%)
  blocking collectives  47 us (19%)
  matrix products  18.7 us (8%)
  between operations  14.6 us (6%)
  other arithmetic  13.1 us (5%)
  local copies, waits for them, and re-layouts  4.3 us (2%)
    ppermute x16, starting transfers between devices, passed_along(): lax.ppermute(value, axis, [(i, (i + by) % length) for i in range(length)])  57.1 us
    all_gather x1, waiting for transfers between devices, shards(): w_all = lax.all_gather(w_mine, 'ctx', axis=0, tiled=True)  37 us
    ppermute x16, waiting for transfers between devices, passed_along(): lax.ppermute(value, axis, [(i, (i + by) % length) for i in range(length)])  27.4 us
    all_to_all x1, blocking collectives, shards(): parts = lax.all_to_all(terms, 'tp', 0, 0)  26.4 us
    psum x1, blocking collectives, shards(): squares = lax.psum(jnp.sum(local * local, axis=1), 'tp')  20.6 us
    all_to_all x1, waiting for transfers between devices, shards(): lax.all_to_all(jnp.broadcast_to(part_normed[None], (n_tp, rows, part)), '...  17.2 us
    all_to_all x1, starting transfers between devices, shards(): lax.all_to_all(jnp.broadcast_to(part_normed[None], (n_tp, rows, part)), '...  7.89 us
    dot_general x9, matrix products, attend(): jnp.einsum('hqk,kd->hqd', probs.astype(jnp.bfloat16), keys_values[1], pre...  6.61 us
  transfers between devices with their start and end apart: 19, of which 16 were waited for; matrix products, arithmetic and copies ran while one was open for 12% of the time, Pallas kernels for 0%

profile of v1, /device:TPU:6, one launch (start us, length us, event | category | flops | bytes accessed | tf_op | source)
XLA Modules:
  0.0 245.1 jit_solution(14082239146654438249)
XLA Ops:
  6.5 1.8 pad_maximum_fusion
  9.5 20.6 %psum.7 = f32[256]{0:T(256)S(1)} all-reduce(f32[256]{0:T(256)S(1)} %fusion.52), channel_id=1, replica_groups=mesh['pipe'=4,'ctx'=16,'tp'=8] {'tp'}, use_global_device_ids=true, to_apply=%region_1.0 | all-reduce | flops 256 | bytes 2048 | tf_op jit(solution)/shard_map/psum | solution.py:72
  32.7 7.9 %all-to-all-start = ((bf16[8,256,512]{1,2,0:T(8,128)(2,1)}), bf16[8,256,512]{1,2,0:T(8,128)(2,1)S(1)}, u32[]{:S(2)}, u32[]{:S(2)}) async-start(bf16[8,256,512]{1,2,0:T(8,128)(2,1)} %broadcast_in_dim.282), calls=%async_computation | async-start | bytes 4194304 | tf_op jit(solution)/shard_map/all_to_all | solution.py:77
  45.9 17.2 %all-to-all-done = bf16[8,256,512]{1,2,0:T(8,128)(2,1)S(1)} async-done(((bf16[8,256,512]{1,2,0:T(8,128)(2,1)}), bf16[8,256,512]{1,2,0:T(8,128)(2,1)S(1)}, u32[]{:S(2)}, u32[]{:S(2)}) %all-to-all-start) | async-done | bytes 2097184 | tf_op jit(solution)/shard_map/all_to_all | solution.py:77
  63.1 37.0 %all-gather.4.cloned.1.call-done = bf16[4096,768]{1,0:T(8,128)(2,1)} async-done(((bf16[256,768]{1,0:T(8,128)(2,1)}), bf16[4096,768]{1,0:T(8,128)(2,1)}) %all-gather.4.cloned.1.call-update) | async-done | bytes 6291472 | tf_op jit(solution)/shard_map/all_gather | solution.py:70
  100.0 4.6 %fusion.159 = f32[256,768]{1,0:T(8,128)S(1)} fusion(bf16[256,4096]{0,1:T(8,128)(2,1)S(1)} %bitcast.252, bf16[4096,768]{1,0:T(8,128)(2,1)} %all-gather.4.cloned.1.call-done), kind=kOutput, calls=%fused_computation.379 | convolution fusion | flops 1610612736 | bytes 9175040 | tf_op jit(solution)/shard_map/dot_general | solution.py:81
  106.1 2.8 %collective-permute-start = (bf16[2,256,128]{2,1,0:T(8,128)(2,1)S(1)}, bf16[2,256,128]{2,1,0:T(8,128)(2,1)S(1)}, u32[]{:S(2)}, u32[]{:S(2)}) collective-permute-start(bf16[2,256,128]{2,1,0:T(8,128)(2,1)S(1)} %pad_maximum_fusion.2), channel_id=1, source_target_pairs={{0,8},{8,16},{16,24},{24,32},{32,40},{40,48},{48,56},{56,64},{64,7... | collective-permute-start | bytes 393224 | tf_op jit(solution)/shard_map/ppermute | solution.py:15
  108.9 4.3 %collective-permute-start.1 = (bf16[2,256,128]{2,1,0:T(8,128)(2,1)S(1)}, bf16[2,256,128]{2,1,0:T(8,128)(2,1)S(1)}, u32[]{:S(2)}, u32[]{:S(2)}) collective-permute-start(bf16[2,256,128]{2,1,0:T(8,128)(2,1)S(1)} %pad_maximum_fusion.2), channel_id=1, source_target_pairs={{0,120},{8,0},{16,8},{24,16},{32,24},{40,32},{48,40},{56,48},{64,5... | collective-permute-start | bytes 393224 | tf_op jit(solution)/shard_map/ppermute | solution.py:15
  114.2 2.7 %collective-permute-done.1 = bf16[2,256,128]{2,1,0:T(8,128)(2,1)S(1)} collective-permute-done((bf16[2,256,128]{2,1,0:T(8,128)(2,1)S(1)}, bf16[2,256,128]{2,1,0:T(8,128)(2,1)S(1)}, u32[]{:S(2)}, u32[]{:S(2)}) %collective-permute-start.1) | collective-permute-done | bytes 131104 | tf_op jit(solution)/shard_map/ppermute | solution.py:15
  117.0 1.9 collective-permute-start.2
  118.9 5.6 %collective-permute-start.3 = (bf16[2,256,128]{2,1,0:T(8,128)(2,1)S(1)}, bf16[2,256,128]{2,1,0:T(8,128)(2,1)S(1)}, u32[]{:S(2)}, u32[]{:S(2)}) collective-permute-start(bf16[2,256,128]{2,1,0:T(8,128)(2,1)S(1)} %collective-permute-done.1), channel_id=1, source_target_pairs={{0,120},{8,0},{16,8},{24,16},{32,24},{40,32},{48,40},{56,48},{64,5... | collective-permute-start | bytes 393224 | tf_op jit(solution)/shard_map/ppermute | solution.py:15
  126.4 1.6 collective-permute-done.2
  129.3 1.9 collective-permute-start.4
  131.3 5.6 %collective-permute-start.5 = (bf16[2,256,128]{2,1,0:T(8,128)(2,1)S(1)}, bf16[2,256,128]{2,1,0:T(8,128)(2,1)S(1)}, u32[]{:S(2)}, u32[]{:S(2)}) collective-permute-start(bf16[2,256,128]{2,1,0:T(8,128)(2,1)S(1)} %collective-permute-done.3), channel_id=1, source_target_pairs={{0,120},{8,0},{16,8},{24,16},{32,24},{40,32},{48,40},{56,48},{64,5... | collective-permute-start | bytes 393224 | tf_op jit(solution)/shard_map/ppermute | solution.py:15
  140.7 4.2 %collective-permute-start.6 = (bf16[2,256,128]{2,1,0:T(8,128)(2,1)S(1)}, bf16[2,256,128]{2,1,0:T(8,128)(2,1)S(1)}, u32[]{:S(2)}, u32[]{:S(2)}) collective-permute-start(bf16[2,256,128]{2,1,0:T(8,128)(2,1)S(1)} %collective-permute-done.4), channel_id=1, source_target_pairs={{0,8},{8,16},{16,24},{24,32},{32,40},{40,48},{48,56},{56,64},{64,7... | collective-permute-start | bytes 393224 | tf_op jit(solution)/shard_map/ppermute | solution.py:15
  144.9 3.5 %collective-permute-start.7 = (bf16[2,256,128]{2,1,0:T(8,128)(2,1)S(1)}, bf16[2,256,128]{2,1,0:T(8,128)(2,1)S(1)}, u32[]{:S(2)}, u32[]{:S(2)}) collective-permute-start(bf16[2,256,128]{2,1,0:T(8,128)(2,1)S(1)} %collective-permute-done.5), channel_id=1, source_target_pairs={{0,120},{8,0},{16,8},{24,16},{32,24},{40,32},{48,40},{56,48},{64,5... | collective-permute-start | bytes 393224 | tf_op jit(solution)/shard_map/ppermute | solution.py:15
  151.3 1.9 collective-permute-done.7
  153.3 4.1 %collective-permute-start.8 = (bf16[2,256,128]{2,1,0:T(8,128)(2,1)S(1)}, bf16[2,256,128]{2,1,0:T(8,128)(2,1)S(1)}, u32[]{:S(2)}, u32[]{:S(2)}) collective-permute-start(bf16[2,256,128]{2,1,0:T(8,128)(2,1)S(1)} %collective-permute-done.6), channel_id=1, source_target_pairs={{0,8},{8,16},{16,24},{24,32},{32,40},{40,48},{48,56},{56,64},{64,7... | collective-permute-start | bytes 393224 | tf_op jit(solution)/shard_map/ppermute | solution.py:15
  157.4 3.1 %collective-permute-start.9 = (bf16[2,256,128]{2,1,0:T(8,128)(2,1)S(1)}, bf16[2,256,128]{2,1,0:T(8,128)(2,1)S(1)}, u32[]{:S(2)}, u32[]{:S(2)}) collective-permute-start(bf16[2,256,128]{2,1,0:T(8,128)(2,1)S(1)} %collective-permute-done.7), channel_id=1, source_target_pairs={{0,120},{8,0},{16,8},{24,16},{32,24},{40,32},{48,40},{56,48},{64,5... | collective-permute-start | bytes 393224 | tf_op jit(solution)/shard_map/ppermute | solution.py:15
  163.9 3.3 %collective-permute-done.9 = bf16[2,256,128]{2,1,0:T(8,128)(2,1)S(1)} collective-permute-done((bf16[2,256,128]{2,1,0:T(8,128)(2,1)S(1)}, bf16[2,256,128]{2,1,0:T(8,128)(2,1)S(1)}, u32[]{:S(2)}, u32[]{:S(2)}) %collective-permute-start.9) | collective-permute-done | bytes 131104 | tf_op jit(solution)/shard_map/ppermute | solution.py:15
  167.2 3.3 %collective-permute-start.10 = (bf16[2,256,128]{2,1,0:T(8,128)(2,1)S(1)}, bf16[2,256,128]{2,1,0:T(8,128)(2,1)S(1)}, u32[]{:S(2)}, u32[]{:S(2)}) collective-permute-start(bf16[2,256,128]{2,1,0:T(8,128)(2,1)S(1)} %collective-permute-done.8), channel_id=1, source_target_pairs={{0,8},{8,16},{16,24},{24,32},{32,40},{40,48},{48,56},{56,64},{64,7... | collective-permute-start | bytes 393224 | tf_op jit(solution)/shard_map/ppermute | solution.py:15
  170.6 3.7 %collective-permute-start.11 = (bf16[2,256,128]{2,1,0:T(8,128)(2,1)S(1)}, bf16[2,256,128]{2,1,0:T(8,128)(2,1)S(1)}, u32[]{:S(2)}, u32[]{:S(2)}) collective-permute-start(bf16[2,256,128]{2,1,0:T(8,128)(2,1)S(1)} %collective-permute-done.9), channel_id=1, source_target_pairs={{0,120},{8,0},{16,8},{24,16},{32,24},{40,32},{48,40},{56,48},{64,5... | collective-permute-start | bytes 393224 | tf_op jit(solution)/shard_map/ppermute | solution.py:15
  176.2 1.9 collective-permute-done.10
  178.5 4.0 %collective-permute-start.12 = (bf16[2,256,128]{2,1,0:T(8,128)(2,1)S(1)}, bf16[2,256,128]{2,1,0:T(8,128)(2,1)S(1)}, u32[]{:S(2)}, u32[]{:S(2)}) collective-permute-start(bf16[2,256,128]{2,1,0:T(8,128)(2,1)S(1)} %collective-permute-done.10), channel_id=1, source_target_pairs={{0,8},{8,16},{16,24},{24,32},{32,40},{40,48},{48,56},{56,64},{64,7... | collective-permute-start | bytes 393224 | tf_op jit(solution)/shard_map/ppermute | solution.py:15
  182.5 3.0 %collective-permute-start.13 = (bf16[2,256,128]{2,1,0:T(8,128)(2,1)S(1)}, bf16[2,256,128]{2,1,0:T(8,128)(2,1)S(1)}, u32[]{:S(2)}, u32[]{:S(2)}) collective-permute-start(bf16[2,256,128]{2,1,0:T(8,128)(2,1)S(1)} %collective-permute-done.11), channel_id=1, source_target_pairs={{0,120},{8,0},{16,8},{24,16},{32,24},{40,32},{48,40},{56,48},{64,5... | collective-permute-start | bytes 393224 | tf_op jit(solution)/shard_map/ppermute | solution.py:15
  187.5 2.1 collective-permute-done.13
  189.6 4.1 %collective-permute-start.14 = (bf16[2,256,128]{2,1,0:T(8,128)(2,1)S(1)}, bf16[2,256,128]{2,1,0:T(8,128)(2,1)S(1)}, u32[]{:S(2)}, u32[]{:S(2)}) collective-permute-start(bf16[2,256,128]{2,1,0:T(8,128)(2,1)S(1)} %collective-permute-done.12), channel_id=1, source_target_pairs={{0,8},{8,16},{16,24},{24,32},{32,40},{40,48},{48,56},{56,64},{64,7... | collective-permute-start | bytes 393224 | tf_op jit(solution)/shard_map/ppermute | solution.py:15
  195.7 2.0 collective-permute-done.14
  198.9 3.5 %convolution_convert_fusion = bf16[16,256,256]{2,1,0:T(8,128)(2,1)S(1)} fusion(bf16[16,512,256]{2,1,0:T(8,128)(2,1)} %bitcast.263, bf16[256,512,1]{0,1,2:T(8,128)(2,1)S(1)} %bitcast.259), kind=kOutput, calls=%fused_computation.15 | convolution fusion | flops 1074790400 | bytes 6553600 | tf_op jit(solution)/shard_map/rk,ckn->crn/dot_general | solution.py:121
  202.4 26.4 %all_to_all.10 = bf16[8,2,256,256]{2,3,1,0:T(8,128)(2,1)S(1)} all-to-all(bf16[8,2,256,256]{2,3,1,0:T(8,128)(2,1)S(1)} %bitcast.255), channel_id=1, replica_groups=mesh['pipe'=4,'ctx'=16,'tp'=8] {'tp'}, dimensions={0} | all-to-all | bytes 4194304 | tf_op jit(solution)/shard_map/all_to_all | solution.py:126
  229.9 1.9 collective-permute-start.15
  231.8 5.8 %collective-permute-done.15 = bf16[1,256,512]{2,1,0:T(8,128)(2,1)S(1)} collective-permute-done((bf16[1,256,512]{2,1,0:T(8,128)(2,1)S(1)}, bf16[1,256,512]{2,1,0:T(8,128)(2,1)S(1)}, u32[]{:S(2)}, u32[]{:S(2)}) %collective-permute-start.15) | collective-permute-done | bytes 262176 | tf_op jit(solution)/shard_map/ppermute | solution.py:15
  (154 shorter events, 33.1 us)
Async XLA Ops:
  6.5 93.5 %all-gather.4.cloned.1.call-start = ((), (), s32[]{:S(2)}) async-start(), calls=%async_computation.2 | async-start | bytes 6684672 | tf_op jit(solution)/shard_map/all_gather | solution.py:70
  32.7 9.2 %copy-start.12 = (s32[32]{0:T(128)S(1)}, s32[32]{0:T(128)}, u32[]{:S(2)}) copy-start(s32[32]{0:T(128)} %param.8) | copy-start | bytes 388
  32.7 30.3 %all-to-all-start = ((bf16[8,256,512]{1,2,0:T(8,128)(2,1)}), bf16[8,256,512]{1,2,0:T(8,128)(2,1)S(1)}, u32[]{:S(2)}, u32[]{:S(2)}) async-start(bf16[8,256,512]{1,2,0:T(8,128)(2,1)} %broadcast_in_dim.282), calls=%async_computation | async-start | bytes 4194304 | tf_op jit(solution)/shard_map/all_to_all | solution.py:77
  40.6 158.3 %all-gather.6.cloned.1.call-start = ((), (), s32[]{:S(2)}) async-start(), calls=%async_computation.3 | async-start | bytes 4456448 | tf_op jit(solution)/shard_map/all_gather | solution.py:76
  104.7 0.9 copy-start.10
  104.7 1.0 copy-start.11
  105.7 7.5 %copy-start.8 = (pred[256,256]{0,1:T(8,128)(4,1)S(1)}, pred[256,256]{0,1:T(8,128)(4,1)}, u32[]{:S(2)}) copy-start(pred[256,256]{0,1:T(8,128)(4,1)} %get-tuple-element.136) | copy-start | bytes 196612
  106.1 8.1 %collective-permute-start = (bf16[2,256,128]{2,1,0:T(8,128)(2,1)S(1)}, bf16[2,256,128]{2,1,0:T(8,128)(2,1)S(1)}, u32[]{:S(2)}, u32[]{:S(2)}) collective-permute-start(bf16[2,256,128]{2,1,0:T(8,128)(2,1)S(1)} %pad_maximum_fusion.2), channel_id=1, source_target_pairs={{0,8},{8,16},{16,24},{24,32},{32,40},{40,48},{48,56},{56,64},{64,7... | collective-permute-start | bytes 393224 | tf_op jit(solution)/shard_map/ppermute | solution.py:15
  108.9 8.0 %collective-permute-start.1 = (bf16[2,256,128]{2,1,0:T(8,128)(2,1)S(1)}, bf16[2,256,128]{2,1,0:T(8,128)(2,1)S(1)}, u32[]{:S(2)}, u32[]{:S(2)}) collective-permute-start(bf16[2,256,128]{2,1,0:T(8,128)(2,1)S(1)} %pad_maximum_fusion.2), channel_id=1, source_target_pairs={{0,120},{8,0},{16,8},{24,16},{32,24},{40,32},{48,40},{56,48},{64,5... | collective-permute-start | bytes 393224 | tf_op jit(solution)/shard_map/ppermute | solution.py:15
  113.2 11.3 %copy-start.7 = (pred[256,512]{0,1:T(8,128)(4,1)S(1)}, pred[256,512]{0,1:T(8,128)(4,1)}, u32[]{:S(2)}) copy-start(pred[256,512]{0,1:T(8,128)(4,1)} %get-tuple-element.134) | copy-start | bytes 393220
  117.0 11.0 %collective-permute-start.2 = (bf16[2,256,128]{2,1,0:T(8,128)(2,1)S(1)}, bf16[2,256,128]{2,1,0:T(8,128)(2,1)S(1)}, u32[]{:S(2)}, u32[]{:S(2)}) collective-permute-start(bf16[2,256,128]{2,1,0:T(8,128)(2,1)S(1)} %collective-permute-done), channel_id=1, source_target_pairs={{0,8},{8,16},{16,24},{24,32},{32,40},{40,48},{48,56},{56,64},{64,7... | collective-permute-start | bytes 393224 | tf_op jit(solution)/shard_map/ppermute | solution.py:15
  118.9 10.4 %collective-permute-start.3 = (bf16[2,256,128]{2,1,0:T(8,128)(2,1)S(1)}, bf16[2,256,128]{2,1,0:T(8,128)(2,1)S(1)}, u32[]{:S(2)}, u32[]{:S(2)}) collective-permute-start(bf16[2,256,128]{2,1,0:T(8,128)(2,1)S(1)} %collective-permute-done.1), channel_id=1, source_target_pairs={{0,120},{8,0},{16,8},{24,16},{32,24},{40,32},{48,40},{56,48},{64,5... | collective-permute-start | bytes 393224 | tf_op jit(solution)/shard_map/ppermute | solution.py:15
  125.6 11.3 %copy-start.6 = (pred[256,512]{0,1:T(8,128)(4,1)S(1)}, pred[256,512]{0,1:T(8,128)(4,1)}, u32[]{:S(2)}) copy-start(pred[256,512]{0,1:T(8,128)(4,1)} %get-tuple-element.135) | copy-start | bytes 393220
  129.3 10.4 %collective-permute-start.4 = (bf16[2,256,128]{2,1,0:T(8,128)(2,1)S(1)}, bf16[2,256,128]{2,1,0:T(8,128)(2,1)S(1)}, u32[]{:S(2)}, u32[]{:S(2)}) collective-permute-start(bf16[2,256,128]{2,1,0:T(8,128)(2,1)S(1)} %collective-permute-done.2), channel_id=1, source_target_pairs={{0,8},{8,16},{16,24},{24,32},{32,40},{40,48},{48,56},{56,64},{64,7... | collective-permute-start | bytes 393224 | tf_op jit(solution)/shard_map/ppermute | solution.py:15
  131.3 9.5 %collective-permute-start.5 = (bf16[2,256,128]{2,1,0:T(8,128)(2,1)S(1)}, bf16[2,256,128]{2,1,0:T(8,128)(2,1)S(1)}, u32[]{:S(2)}, u32[]{:S(2)}) collective-permute-start(bf16[2,256,128]{2,1,0:T(8,128)(2,1)S(1)} %collective-permute-done.3), channel_id=1, source_target_pairs={{0,120},{8,0},{16,8},{24,16},{32,24},{40,32},{48,40},{56,48},{64,5... | collective-permute-start | bytes 393224 | tf_op jit(solution)/shard_map/ppermute | solution.py:15
  138.0 10.5 %copy-start.5 = (pred[256,512]{0,1:T(8,128)(4,1)S(1)}, pred[256,512]{0,1:T(8,128)(4,1)}, u32[]{:S(2)}) copy-start(pred[256,512]{0,1:T(8,128)(4,1)} %get-tuple-element.130) | copy-start | bytes 393220
  140.7 10.6 %collective-permute-start.6 = (bf16[2,256,128]{2,1,0:T(8,128)(2,1)S(1)}, bf16[2,256,128]{2,1,0:T(8,128)(2,1)S(1)}, u32[]{:S(2)}, u32[]{:S(2)}) collective-permute-start(bf16[2,256,128]{2,1,0:T(8,128)(2,1)S(1)} %collective-permute-done.4), channel_id=1, source_target_pairs={{0,8},{8,16},{16,24},{24,32},{32,40},{40,48},{48,56},{56,64},{64,7... | collective-permute-start | bytes 393224 | tf_op jit(solution)/shard_map/ppermute | solution.py:15
  144.9 8.4 %collective-permute-start.7 = (bf16[2,256,128]{2,1,0:T(8,128)(2,1)S(1)}, bf16[2,256,128]{2,1,0:T(8,128)(2,1)S(1)}, u32[]{:S(2)}, u32[]{:S(2)}) collective-permute-start(bf16[2,256,128]{2,1,0:T(8,128)(2,1)S(1)} %collective-permute-done.5), channel_id=1, source_target_pairs={{0,120},{8,0},{16,8},{24,16},{32,24},{40,32},{48,40},{56,48},{64,5... | collective-permute-start | bytes 393224 | tf_op jit(solution)/shard_map/ppermute | solution.py:15
  149.5 11.0 %copy-start.4 = (pred[256,512]{0,1:T(8,128)(4,1)S(1)}, pred[256,512]{0,1:T(8,128)(4,1)}, u32[]{:S(2)}) copy-start(pred[256,512]{0,1:T(8,128)(4,1)} %get-tuple-element.131) | copy-start | bytes 393220
  153.3 10.6 %collective-permute-start.8 = (bf16[2,256,128]{2,1,0:T(8,128)(2,1)S(1)}, bf16[2,256,128]{2,1,0:T(8,128)(2,1)S(1)}, u32[]{:S(2)}, u32[]{:S(2)}) collective-permute-start(bf16[2,256,128]{2,1,0:T(8,128)(2,1)S(1)} %collective-permute-done.6), channel_id=1, source_target_pairs={{0,8},{8,16},{16,24},{24,32},{32,40},{40,48},{48,56},{56,64},{64,7... | collective-permute-start | bytes 393224 | tf_op jit(solution)/shard_map/ppermute | solution.py:15
  157.4 9.8 %collective-permute-start.9 = (bf16[2,256,128]{2,1,0:T(8,128)(2,1)S(1)}, bf16[2,256,128]{2,1,0:T(8,128)(2,1)S(1)}, u32[]{:S(2)}, u32[]{:S(2)}) collective-permute-start(bf16[2,256,128]{2,1,0:T(8,128)(2,1)S(1)} %collective-permute-done.7), channel_id=1, source_target_pairs={{0,120},{8,0},{16,8},{24,16},{32,24},{40,32},{48,40},{56,48},{64,5... | collective-permute-start | bytes 393224 | tf_op jit(solution)/shard_map/ppermute | solution.py:15
  161.6 12.7 %copy-start.3 = (pred[256,512]{0,1:T(8,128)(4,1)S(1)}, pred[256,512]{0,1:T(8,128)(4,1)}, u32[]{:S(2)}) copy-start(pred[256,512]{0,1:T(8,128)(4,1)} %get-tuple-element.132) | copy-start | bytes 393220
  167.2 10.9 %collective-permute-start.10 = (bf16[2,256,128]{2,1,0:T(8,128)(2,1)S(1)}, bf16[2,256,128]{2,1,0:T(8,128)(2,1)S(1)}, u32[]{:S(2)}, u32[]{:S(2)}) collective-permute-start(bf16[2,256,128]{2,1,0:T(8,128)(2,1)S(1)} %collective-permute-done.8), channel_id=1, source_target_pairs={{0,8},{8,16},{16,24},{24,32},{32,40},{40,48},{48,56},{56,64},{64,7... | collective-permute-start | bytes 393224 | tf_op jit(solution)/shard_map/ppermute | solution.py:15
  170.6 7.9 %collective-permute-start.11 = (bf16[2,256,128]{2,1,0:T(8,128)(2,1)S(1)}, bf16[2,256,128]{2,1,0:T(8,128)(2,1)S(1)}, u32[]{:S(2)}, u32[]{:S(2)}) collective-permute-start(bf16[2,256,128]{2,1,0:T(8,128)(2,1)S(1)} %collective-permute-done.9), channel_id=1, source_target_pairs={{0,120},{8,0},{16,8},{24,16},{32,24},{40,32},{48,40},{56,48},{64,5... | collective-permute-start | bytes 393224 | tf_op jit(solution)/shard_map/ppermute | solution.py:15
  175.4 10.2 %copy-start.2 = (pred[256,512]{0,1:T(8,128)(4,1)S(1)}, pred[256,512]{0,1:T(8,128)(4,1)}, u32[]{:S(2)}) copy-start(pred[256,512]{0,1:T(8,128)(4,1)} %get-tuple-element.133) | copy-start | bytes 393220
  178.5 9.0 %collective-permute-start.12 = (bf16[2,256,128]{2,1,0:T(8,128)(2,1)S(1)}, bf16[2,256,128]{2,1,0:T(8,128)(2,1)S(1)}, u32[]{:S(2)}, u32[]{:S(2)}) collective-permute-start(bf16[2,256,128]{2,1,0:T(8,128)(2,1)S(1)} %collective-permute-done.10), channel_id=1, source_target_pairs={{0,8},{8,16},{16,24},{24,32},{32,40},{40,48},{48,56},{56,64},{64,7... | collective-permute-start | bytes 393224 | tf_op jit(solution)/shard_map/ppermute | solution.py:15
  182.5 7.1 %collective-permute-start.13 = (bf16[2,256,128]{2,1,0:T(8,128)(2,1)S(1)}, bf16[2,256,128]{2,1,0:T(8,128)(2,1)S(1)}, u32[]{:S(2)}, u32[]{:S(2)}) collective-permute-start(bf16[2,256,128]{2,1,0:T(8,128)(2,1)S(1)} %collective-permute-done.11), channel_id=1, source_target_pairs={{0,120},{8,0},{16,8},{24,16},{32,24},{40,32},{48,40},{56,48},{64,5... | collective-permute-start | bytes 393224 | tf_op jit(solution)/shard_map/ppermute | solution.py:15
  186.7 7.1 %copy-start.1 = (pred[256,512]{0,1:T(8,128)(4,1)S(1)}, pred[256,512]{0,1:T(8,128)(4,1)}, u32[]{:S(2)}) copy-start(pred[256,512]{0,1:T(8,128)(4,1)} %get-tuple-element.129) | copy-start | bytes 393220
  189.6 8.1 %collective-permute-start.14 = (bf16[2,256,128]{2,1,0:T(8,128)(2,1)S(1)}, bf16[2,256,128]{2,1,0:T(8,128)(2,1)S(1)}, u32[]{:S(2)}, u32[]{:S(2)}) collective-permute-start(bf16[2,256,128]{2,1,0:T(8,128)(2,1)S(1)} %collective-permute-done.12), channel_id=1, source_target_pairs={{0,8},{8,16},{16,24},{24,32},{32,40},{40,48},{48,56},{56,64},{64,7... | collective-permute-start | bytes 393224 | tf_op jit(solution)/shard_map/ppermute | solution.py:15
  194.9 2.8 %copy-start.9 = (pred[256,256]{0,1:T(8,128)(4,1)S(1)}, pred[256,256]{0,1:T(8,128)(4,1)}, u32[]{:S(2)}) copy-start(pred[256,256]{0,1:T(8,128)(4,1)} %get-tuple-element.137) | copy-start | bytes 196612
  228.9 1.0 copy-start
  229.9 7.7 %collective-permute-start.15 = (bf16[1,256,512]{2,1,0:T(8,128)(2,1)S(1)}, bf16[1,256,512]{2,1,0:T(8,128)(2,1)S(1)}, u32[]{:S(2)}, u32[]{:S(2)}) collective-permute-start(bf16[1,256,512]{2,1,0:T(8,128)(2,1)S(1)} %fusion.55), channel_id=1, source_target_pairs={{0,128},{128,256},{256,384},{384,0},{1,129},{129,257},{257,385},{3... | collective-permute-start | bytes 786440 | tf_op jit(solution)/shard_map/ppermute | solution.py:15
Sparse Core Ops, SparseCore 0:
  9.4 90.5 all-gather.3
  102.1 80.9 all-gather.5

commit v2 on v1

v2 whole, which is shorter than its diff:
```python
import jax
import jax.numpy as jnp
from jax import lax
from jax.experimental import pallas as pl
from jax.experimental.pallas import tpu as pltpu
from jax.sharding import PartitionSpec as P

HD = 128


EPS = 1e-05
THETA = 500000.0


def passed_along(value, axis, by):
    length = lax.axis_size(axis)
    return lax.ppermute(value, axis, [(i, (i + by) % length) for i in range(length)])


def turning(pos):
    half = HD // 2
    index = jnp.arange(half, dtype=jnp.float32)
    freq = THETA ** (-2.0 * index / HD)
    angle = pos.astype(jnp.float32)[:, None] * freq[None, :]
    cosine = jnp.cos(angle)
    sine = jnp.sin(angle)
    return jnp.concatenate([cosine, cosine], axis=1), jnp.concatenate([-sine, sine], axis=1)


def rotate(values, pos):
    cosine, sine = turning(pos)
    half = HD // 2
    swapped = jnp.concatenate([values[:, half:], values[:, :half]], axis=1)
    return values * cosine + swapped * sine


def positions_of(stored, stretch_order, block):
    which = stored // block
    slots = jnp.arange(stretch_order.shape[0], dtype=jnp.int32)
    picked = jnp.sum(jnp.where(which[:, None] == slots[None, :], stretch_order[None, :], 0), axis=1)
    return picked * block + stored % block


TURN_KV = 4
LOW = -1e20
MASKED = -1e30
CHUNK = 512


def attend_kernel(order_ref, raw_ref, cosine_ref, sine_ref, query_pos_ref, kv_ref, out_ref, *scratch):
    query_ref, peak_ref, total_ref, accum_ref = scratch
    heads, rows, size = query_ref.shape
    keys = kv_ref.shape[0]
    block = keys // order_ref.shape[0]
    blocks = CHUNK // block
    rate = 1.4426950408889634 / size**0.5
    cosine = cosine_ref[...]
    sine = sine_ref[...]
    for head in range(heads):
        raw = raw_ref[:, head * size : (head + 1) * size]
        swapped = jnp.concatenate([raw[:, size // 2 :], raw[:, : size // 2]], axis=1)
        query_ref[head] = (raw * cosine + swapped * sine).astype(jnp.bfloat16)
    peak_ref[...] = jnp.full(peak_ref.shape, LOW, jnp.float32)
    total_ref[...] = jnp.zeros(total_ref.shape, jnp.float32)
    accum_ref[...] = jnp.zeros(accum_ref.shape, jnp.float32)
    query_pos = query_pos_ref[...]
    within = lax.broadcasted_iota(jnp.int32, (block, rows), 0)

    def chunk_step(chunk, carry):
        at = pl.multiple_of(chunk * CHUNK, CHUNK)
        key = kv_ref[pl.ds(at, CHUNK), :size]
        value = kv_ref[pl.ds(at, CHUNK), size:]
        allowed = jnp.concatenate(
            [within + order_ref[chunk * blocks + i] * block <= query_pos for i in range(blocks)],
            axis=0,
        )
        for head in range(heads):
            scores = lax.dot_general(
                key, query_ref[head], (((1,), (1,)), ((), ())), preferred_element_type=jnp.float32
            )
            scores = jnp.where(allowed, scores, MASKED)
            peak = peak_ref[head]
            new_peak = jnp.maximum(peak, jnp.max(scores, axis=0, keepdims=True))
            probs = jnp.exp2((scores - new_peak) * rate)
            fade = jnp.exp2((peak - new_peak) * rate)
            peak_ref[head] = new_peak
            total_ref[head] = total_ref[head] * fade + jnp.sum(probs, axis=0, keepdims=True)
            mixed = lax.dot_general(
                value,
                probs.astype(jnp.bfloat16),
                (((0,), (0,)), ((), ())),
                preferred_element_type=jnp.float32,
            )
            accum_ref[head] = accum_ref[head] * fade + mixed
        return carry

    lax.fori_loop(0, keys // CHUNK, chunk_step, 0)
    for head in range(heads):
        context = accum_ref[head] / total_ref[head]
        out_ref[:, head * size : (head + 1) * size] = context.T.astype(out_ref.dtype)


def attend_all(stretch_order, query_raw, query_pos, kv):
    rows, part = query_raw.shape
    heads = part // HD
    cosine, sine = turning(query_pos)
    vmem = pl.BlockSpec(memory_space=pltpu.VMEM)
    return pl.pallas_call(
        attend_kernel,
        out_shape=jax.ShapeDtypeStruct((rows, part), jnp.bfloat16),
        in_specs=[pl.BlockSpec(memory_space=pltpu.SMEM)] + [vmem] * 5,
        out_specs=vmem,
        scratch_shapes=[
            pltpu.VMEM((heads, rows, HD), jnp.bfloat16),
            pltpu.VMEM((heads, 1, rows), jnp.float32),
            pltpu.VMEM((heads, 1, rows), jnp.float32),
            pltpu.VMEM((heads, HD, rows), jnp.float32),
        ],
        compiler_params=pltpu.CompilerParams(vmem_limit_bytes=32 * 1024 * 1024),
        cost_estimate=pl.CostEstimate(
            flops=4 * rows * part * kv.shape[0],
            bytes_accessed=2 * kv.size,
            transcendentals=heads * rows * kv.shape[0],
        ),
    )(stretch_order, query_raw, cosine, sine, query_pos[None, :], kv)


def project_out_kernel(order_ref, context_ref, *refs):
    out_ref = refs[-1]
    depth = refs[0].shape[0] // 2
    packed = refs[0].shape[1]
    per = out_ref.shape[2] * out_ref.shape[0] // (len(refs) - 1)
    share = out_ref.shape[2] // per
    for turn, weights_ref in enumerate(refs[:-1]):
        total = None
        for i in range(packed // per):
            term = jnp.dot(
                context_ref[:, i * depth : (i + 1) * depth],
                weights_ref[-depth:, i * per : (i + 1) * per],
                preferred_element_type=jnp.float32,
            )
            total = term if total is None else total + term
        source = order_ref[turn]
        at = pl.multiple_of((source % share) * per, per)
        out_ref[source // share, :, pl.ds(at, per)] = total.astype(out_ref.dtype)


def project_out(context, held, order, n_tp):
    rows, part = context.shape
    vmem = pl.BlockSpec(memory_space=pltpu.VMEM)
    return pl.pallas_call(
        project_out_kernel,
        out_shape=jax.ShapeDtypeStruct((n_tp, rows, part), jnp.bfloat16),
        in_specs=[pl.BlockSpec(memory_space=pltpu.SMEM)] + [vmem] * (1 + len(held)),
        out_specs=vmem,
        compiler_params=pltpu.CompilerParams(vmem_limit_bytes=32 * 1024 * 1024),
        cost_estimate=pl.CostEstimate(
            flops=2 * rows * part * part * n_tp,
            bytes_accessed=4 * part * part * n_tp,
            transcendentals=0,
        ),
    )(jnp.stack(order).astype(jnp.int32), context, *held)


def shards(section_in, stretch_order, norm_gain, w_query, w_key, w_value, w_out):
    hidden = section_in[0]
    rows, part = hidden.shape
    block = rows // 2
    n_ctx = lax.axis_size("ctx")
    n_tp = lax.axis_size("tp")
    me = lax.axis_index("ctx")
    width = part * n_tp
    depth = w_query.shape[1]
    heads = w_query.shape[2] // HD
    span = w_out.shape[2]
    w_kv = lax.all_gather(
        jnp.concatenate([w_key[0], w_value[0]], axis=1), "ctx", axis=0, tiled=True
    )
    fold = part // span
    folded = [w_out[0, i * depth : (i + 1) * depth] for i in range(fold)]
    pack = jnp.concatenate([w_query[0], jnp.concatenate(folded, axis=1)], axis=0)
    gain = norm_gain[0]
    high = lax.reduce_precision(gain, 8, 7)
    middle = lax.reduce_precision(gain - high, 8, 7)
    low = gain - high - middle
    extra = jnp.zeros((16, part), jnp.float32)
    extra = extra.at[0].set(high).at[1].set(middle).at[2].set(low)
    payload = jnp.concatenate([hidden, extra.astype(jnp.bfloat16)], axis=0)
    spread = lax.all_to_all(
        jnp.broadcast_to(payload[None], (n_tp,) + payload.shape), "tp", 0, 0
    ).astype(jnp.float32)
    whole = spread[:, :rows]
    gains = spread[:, rows] + spread[:, rows + 1] + spread[:, rows + 2]
    squares = jnp.sum(whole * whole, axis=(0, 2))
    factor = lax.rsqrt(squares / width + EPS)
    normed = (whole * factor[None, :, None] * gains[:, None, :]).astype(jnp.bfloat16)
    normed = normed.transpose(1, 0, 2).reshape(rows, width)

    local_rows = jnp.arange(rows, dtype=jnp.int32)
    query_pos = positions_of(me * rows + local_rows, stretch_order, block)

    def query_term(source, weights):
        at = (source % n_ctx) * depth
        columns = lax.dynamic_slice(normed, (0, at), (rows, depth))
        return jnp.dot(columns, weights, preferred_element_type=jnp.float32)

    query_raw = query_term(me, pack[:depth])
    held = {0: pack}
    up = down = pack
    half = n_ctx // 2
    for turn in range(1, half):
        up = passed_along(up, "ctx", 1)
        down = passed_along(down, "ctx", -1)
        if turn == TURN_KV:
            up, down, w_kv, normed = lax.optimization_barrier((up, down, w_kv, normed))
            raw = jnp.dot(normed, w_kv, preferred_element_type=jnp.float32)
            key = rotate(raw[:, :HD], query_pos)
            keys_values = jnp.concatenate([key, raw[:, HD:]], axis=1).astype(jnp.bfloat16)
            all_kv = lax.all_gather(keys_values, "ctx", axis=0, tiled=True)
        if turn == TURN_KV + 1:
            up, down, _ = lax.optimization_barrier((up, down, keys_values))
        query_raw = query_raw + query_term(me - turn, up[:depth])
        query_raw = query_raw + query_term(me + turn, down[:depth])
        held[turn] = up
        held[n_ctx - turn] = down
    last_query = passed_along(up[:depth], "ctx", 1)
    held[half] = passed_along(down[depth:], "ctx", -1)
    query_raw = query_raw + query_term(me - half, last_query)
    context = attend_all(stretch_order, query_raw, query_pos, all_kv)
    order = [(me - turn) % n_ctx for turn in range(n_ctx)]
    terms = project_out(context, [held[turn] for turn in range(n_ctx)], order, n_tp)
    parts = lax.all_to_all(terms, "tp", 0, 0)
    summed = jnp.sum(parts.astype(jnp.float32), axis=0)
    result = (hidden.astype(jnp.float32) + summed).astype(jnp.bfloat16)[None]
    return passed_along(result, "pipe", 1)


def solution(mesh):
    in_specs = (
        P("pipe", "ctx", "tp"),
        P(),
        P("pipe", "tp"),
        P("pipe", "ctx", "tp"),
        P("pipe", "ctx", "tp"),
        P("pipe", "ctx", "tp"),
        P("pipe", "tp", "ctx"),
    )
    out_specs = P("pipe", "ctx", "tp")
    return jax.shard_map(shards, mesh=mesh, in_specs=in_specs, out_specs=out_specs, check_vma=False)
```

time: 247 us -> 257 us (1.040)
  blocking collectives: 47 us -> 26.1 us
  Pallas kernels: 0 us -> 17.6 us
  starting transfers between devices: 65 us -> 75 us
  local copies, waits for them, and re-layouts: 4.3 us -> 11.8 us
  matrix products: 18.7 us -> 12.6 us
  waiting for transfers between devices: 82.4 us -> 85.6 us
    ppermute x16 -> x17, waiting for transfers between devices: 27.4 us -> 85.2 us  [passed_along(): lax.ppermute(value, axis, [(i, (i + by) % length) for i in range(length)])]
    all_gather x2, waiting for transfers between devices: 37 us -> 0.33 us  [the longest x1 0.31 us: shards(): all_kv = lax.all_gather(keys_values, 'ctx', axis=0, tiled=True)]
    psum x1 -> x0, blocking collectives: 20.6 us -> none  [shards(): squares = lax.psum(jnp.sum(local * local, axis=1), 'tp')]
    pallas_call x0 -> x2, Pallas kernels: none -> 17.6 us  [the longest x1 15.1 us: attend_all(): pl.pallas_call(attend_kernel, out_shape=jax.ShapeDtypeStruct((rows, part)...]
    all_to_all x1, waiting for transfers between devices: 17.2 us -> 0.01 us  [shards(): lax.all_to_all(jnp.broadcast_to(payload[None], (n_tp,) + payload.shape),...]
    ppermute x16 -> x17, starting transfers between devices: 57.1 us -> 64.8 us  [passed_along(): lax.ppermute(value, axis, [(i, (i + by) % length) for i in range(length)])]
    dot_general x20 -> x17, matrix products: 18.7 us -> 12.6 us  [the longest x16 9.62 us: query_term(): return jnp.dot(columns, weights, preferred_element_type=jnp.float32)]
    transpose x0 -> x1, local copies, waits for them, and re-layouts: none -> 4.3 us  [shards(): normed = normed.transpose(1, 0, 2).reshape(rows, width)]
  transfers between devices with their start and end apart: 19 -> 20, of which waited for: 16 -> 11; matrix products, arithmetic and copies ran while one was open for 12% -> 9% of each run, Pallas kernels for 0% -> 6%
where the time goes in v2:
time: 257 us; the launch traced here: 255 us
  waiting for transfers between devices  85.6 us (33%)
  starting transfers between devices  75 us (29%)
  blocking collectives  26.1 us (10%)
  Pallas kernels  17.6 us (7%)
  between operations  14.5 us (6%)
  matrix products  12.6 us (5%)
  local copies, waits for them, and re-layouts  11.8 us (5%)
  other arithmetic  11.6 us (5%)
    ppermute x17, waiting for transfers between devices, passed_along(): lax.ppermute(value, axis, [(i, (i + by) % length) for i in range(length)])  85.2 us
    ppermute x17, starting transfers between devices, passed_along(): lax.ppermute(value, axis, [(i, (i + by) % length) for i in range(length)])  64.8 us
    all_to_all x1, blocking collectives, shards(): parts = lax.all_to_all(terms, 'tp', 0, 0)  26.1 us
    pallas_call x1, Pallas kernels, attend_all(): pl.pallas_call(attend_kernel, out_shape=jax.ShapeDtypeStruct((rows, part)...  15.1 us
    all_to_all x1, starting transfers between devices, shards(): lax.all_to_all(jnp.broadcast_to(payload[None], (n_tp,) + payload.shape),...  10.2 us
    dot_general x16, matrix products, query_term(): return jnp.dot(columns, weights, preferred_element_type=jnp.float32)  9.62 us
  transfers between devices with their start and end apart: 20, of which 11 were waited for; matrix products, arithmetic and copies ran while one was open for 9% of the time, Pallas kernels for 6%

profile of v2, /device:TPU:6, one launch (start us, length us, event | category | flops | bytes accessed | tf_op | source)
XLA Modules:
  0.0 254.7 jit_solution(11516979106473871589)
XLA Ops:
  11.5 10.2 %all-to-all-start = ((bf16[8,272,512]{2,1,0:T(8,128)(2,1)}), bf16[8,272,512]{2,1,0:T(8,128)(2,1)}, u32[]{:S(2)}, u32[]{:S(2)}) async-start(bf16[8,272,512]{2,1,0:T(8,128)(2,1)} %broadcast_in_dim.10), calls=%async_computation | async-start | bytes 4456448 | tf_op jit(solution)/shard_map/all_to_all | solution.py:189
  21.8 8.7 %collective-permute-start.1 = (bf16[512,512]{1,0:T(8,128)(2,1)S(1)}, bf16[512,512]{1,0:T(8,128)(2,1)S(1)}, u32[]{:S(2)}, u32[]{:S(2)}) collective-permute-start(bf16[512,512]{1,0:T(8,128)(2,1)S(1)} %maximum_maximum_fusion.refs_0_), channel_id=1, source_target_pairs={{0,120},{8,0},{16,8},{24,16},{32,24},{40,32},{48,40},{56,48},{64,5... | collective-permute-start | bytes 1572872 | tf_op jit(solution)/shard_map/ppermute | solution.py:17
  30.5 1.9 collective-permute-start
  32.5 14.3 %collective-permute-done.1.refs_15_ = bf16[512,512]{1,0:T(8,128)(2,1)S(1)} collective-permute-done((bf16[512,512]{1,0:T(8,128)(2,1)S(1)}, bf16[512,512]{1,0:T(8,128)(2,1)S(1)}, u32[]{:S(2)}, u32[]{:S(2)}) %collective-permute-start.1) | collective-permute-done | bytes 524320 | tf_op jit(solution)/shard_map/ppermute | solution.py:17
  46.7 5.6 %collective-permute-start.3 = (bf16[512,512]{1,0:T(8,128)(2,1)S(1)}, bf16[512,512]{1,0:T(8,128)(2,1)S(1)}, u32[]{:S(2)}, u32[]{:S(2)}) collective-permute-start(bf16[512,512]{1,0:T(8,128)(2,1)S(1)} %collective-permute-done.1.refs_15_), channel_id=1, source_target_pairs={{0,120},{8,0},{16,8},{24,16},{32,24},{40,32},{48,40},{56,48},{64,5... | collective-permute-start | bytes 1572872 | tf_op jit(solution)/shard_map/ppermute | solution.py:17
  52.5 1.9 collective-permute-start.2
  55.1 15.5 %collective-permute-done.3.refs_14_ = bf16[512,512]{1,0:T(8,128)(2,1)S(1)} collective-permute-done((bf16[512,512]{1,0:T(8,128)(2,1)S(1)}, bf16[512,512]{1,0:T(8,128)(2,1)S(1)}, u32[]{:S(2)}, u32[]{:S(2)}) %collective-permute-start.3) | collective-permute-done | bytes 524320 | tf_op jit(solution)/shard_map/ppermute | solution.py:17
  70.6 5.6 %collective-permute-start.5 = (bf16[512,512]{1,0:T(8,128)(2,1)S(1)}, bf16[512,512]{1,0:T(8,128)(2,1)S(1)}, u32[]{:S(2)}, u32[]{:S(2)}) collective-permute-start(bf16[512,512]{1,0:T(8,128)(2,1)S(1)} %collective-permute-done.3.refs_14_), channel_id=1, source_target_pairs={{0,120},{8,0},{16,8},{24,16},{32,24},{40,32},{48,40},{56,48},{64,5... | collective-permute-start | bytes 1572872 | tf_op jit(solution)/shard_map/ppermute | solution.py:17
  76.2 1.9 collective-permute-start.4
  78.2 15.8 %collective-permute-done.4.refs_3_ = bf16[512,512]{1,0:T(8,128)(2,1)S(1)} collective-permute-done((bf16[512,512]{1,0:T(8,128)(2,1)S(1)}, bf16[512,512]{1,0:T(8,128)(2,1)S(1)}, u32[]{:S(2)}, u32[]{:S(2)}) %collective-permute-start.4) | collective-permute-done | bytes 524320 | tf_op jit(solution)/shard_map/ppermute | solution.py:17
  94.0 1.9 collective-permute-start.6
  95.9 5.1 %collective-permute-start.7 = (bf16[512,512]{1,0:T(8,128)(2,1)S(1)}, bf16[512,512]{1,0:T(8,128)(2,1)}, u32[]{:S(2)}, u32[]{:S(2)}) collective-permute-start(bf16[512,512]{1,0:T(8,128)(2,1)S(1)} %collective-permute-done.5.refs_13_), channel_id=1, source_target_pairs={{0,120},{8,0},{16,8},{24,16},{32,24},{40,32},{48,40},{56,48},{64,5... | collective-permute-start | bytes 1572872 | tf_op jit(solution)/shard_map/ppermute | solution.py:17
  101.1 2.9 %copy_convert_fusion = f32[8,272,512]{2,0,1:T(8,128)S(1)} fusion(bf16[8,272,512]{2,1,0:T(8,128)(2,1)} %all-to-all-done), kind=kLoop, calls=%fused_computation.3 | loop fusion | flops 1114112 | bytes 6684672 | tf_op jit(solution)/shard_map/convert_element_type | solution.py:191
  106.8 4.3 %copy.29 = bf16[256,8,512]{0,2,1:T(8,128)(2,1)} copy(bf16[256,8,512]{2,1,0:T(8,128)(2,1)} %fusion) | data formatting | bytes 4194304 | tf_op jit(solution)/shard_map/transpose | solution.py:197
  111.2 3.0 %fusion.70 = f32[256,256]{1,0:T(8,128)S(1)} fusion(bf16[256,4096]{0,1:T(8,128)(2,1)} %bitcast.39, bf16[4096,256]{1,0:T(8,128)(2,1)} %all-gather.3.cloned.1.call-done), kind=kOutput, calls=%fused_computation.117 | convolution fusion | flops 536870912 | bytes 4456448 | tf_op jit(solution)/shard_map/dot_general | solution.py:216
  120.1 1.9 collective-permute-start.8
  122.1 5.1 %collective-permute-start.9 = (bf16[512,512]{1,0:T(8,128)(2,1)}, bf16[512,512]{1,0:T(8,128)(2,1)S(1)}, u32[]{:S(2)}, u32[]{:S(2)}) collective-permute-start(bf16[512,512]{1,0:T(8,128)(2,1)} %collective-permute-done.7.refs_12_), channel_id=1, source_target_pairs={{0,120},{8,0},{16,8},{24,16},{32,24},{40,32},{48,40},{56,48},{64,5... | collective-permute-start | bytes 1572872 | tf_op jit(solution)/shard_map/ppermute | solution.py:17
  127.8 7.4 %collective-permute-done.8.refs_5_ = bf16[512,512]{1,0:T(8,128)(2,1)S(1)} collective-permute-done((bf16[512,512]{1,0:T(8,128)(2,1)}, bf16[512,512]{1,0:T(8,128)(2,1)S(1)}, u32[]{:S(2)}, u32[]{:S(2)}) %collective-permute-start.8) | collective-permute-done | bytes 524320 | tf_op jit(solution)/shard_map/ppermute | solution.py:17
  135.2 4.2 %collective-permute-done.9.refs_11_ = bf16[512,512]{1,0:T(8,128)(2,1)S(1)} collective-permute-done((bf16[512,512]{1,0:T(8,128)(2,1)}, bf16[512,512]{1,0:T(8,128)(2,1)S(1)}, u32[]{:S(2)}, u32[]{:S(2)}) %collective-permute-start.9) | collective-permute-done | bytes 524320 | tf_op jit(solution)/shard_map/ppermute | solution.py:17
  139.4 1.9 collective-permute-start.10
  141.6 5.5 %collective-permute-start.11 = (bf16[512,512]{1,0:T(8,128)(2,1)S(1)}, bf16[512,512]{1,0:T(8,128)(2,1)S(1)}, u32[]{:S(2)}, u32[]{:S(2)}) collective-permute-start(bf16[512,512]{1,0:T(8,128)(2,1)S(1)} %collective-permute-done.9.refs_11_), channel_id=1, source_target_pairs={{0,120},{8,0},{16,8},{24,16},{32,24},{40,32},{48,40},{56,48},{64,5... | collective-permute-start | bytes 1572872 | tf_op jit(solution)/shard_map/ppermute | solution.py:17
  149.5 8.8 %collective-permute-done.10.refs_6_ = bf16[512,512]{1,0:T(8,128)(2,1)S(1)} collective-permute-done((bf16[512,512]{1,0:T(8,128)(2,1)S(1)}, bf16[512,512]{1,0:T(8,128)(2,1)S(1)}, u32[]{:S(2)}, u32[]{:S(2)}) %collective-permute-start.10) | collective-permute-done | bytes 524320 | tf_op jit(solution)/shard_map/ppermute | solution.py:17
  158.3 1.9 collective-permute-start.12
  160.5 6.3 %collective-permute-start.13 = (bf16[512,512]{1,0:T(8,128)(2,1)S(1)}, bf16[512,512]{1,0:T(8,128)(2,1)S(1)}, u32[]{:S(2)}, u32[]{:S(2)}) collective-permute-start(bf16[512,512]{1,0:T(8,128)(2,1)S(1)} %collective-permute-done.11.refs_10_), channel_id=1, source_target_pairs={{0,120},{8,0},{16,8},{24,16},{32,24},{40,32},{48,40},{56,48},{64,5... | collective-permute-start | bytes 1572872 | tf_op jit(solution)/shard_map/ppermute | solution.py:17
  167.4 11.6 %collective-permute-done.12.refs_7_ = bf16[512,512]{1,0:T(8,128)(2,1)S(1)} collective-permute-done((bf16[512,512]{1,0:T(8,128)(2,1)S(1)}, bf16[512,512]{1,0:T(8,128)(2,1)S(1)}, u32[]{:S(2)}, u32[]{:S(2)}) %collective-permute-start.12) | collective-permute-done | bytes 524320 | tf_op jit(solution)/shard_map/ppermute | solution.py:17
  179.0 1.9 collective-permute-start.14
  181.9 5.5 %collective-permute-start.15 = (bf16[256,512]{1,0:T(8,128)(2,1)}, bf16[256,512]{1,0:T(8,128)(2,1)S(1)}, u32[]{:S(2)}, u32[]{:S(2)}) collective-permute-start(bf16[256,512]{1,0:T(8,128)(2,1)} %slice.166), channel_id=1, source_target_pairs={{0,120},{8,0},{16,8},{24,16},{32,24},{40,32},{48,40},{56,48},{64,5... | collective-permute-start | bytes 786440 | tf_op jit(solution)/shard_map/ppermute | solution.py:17
  194.6 15.1 %shard_map.73.context_ref = bf16[256,512]{1,0:T(8,128)(2,1)S(1)} custom-call(s32[32]{0:T(128)S(1)} %copy-done.17, f32[256,512]{1,0:T(8,128)S(1)} %copy-done.15, f32[256,128]{1,0:T(8,128)S(1)} %copy-done.16, f32[256,128]{1,0:T(8,128)S(1)} %get-tuple-element.54.sine_ref, s32[1,256]{1,0:T(1,128)S(1)} %fusion.62.query_pos_ref, bf16[4096,256]{1,0:T(8,128)(2,1)S(1)} %copy-done.18), custom_call_target="tpu_custom_call" | custom-call | flops 2147483648 | bytes 2097152 | tf_op jit(solution)/shard_map/pallas_call | solution.py:108
  209.8 2.5 shard_map.74
  212.3 26.1 %all_to_all.10 = bf16[8,256,512]{2,1,0:T(8,128)(2,1)S(1)} all-to-all(bf16[8,256,512]{2,1,0:T(8,128)(2,1)S(1)} %shard_map.74), channel_id=1, replica_groups=mesh['pipe'=4,'ctx'=16,'tp'=8] {'tp'}, dimensions={0} | all-to-all | bytes 4194304 | tf_op jit(solution)/shard_map/all_to_all | solution.py:232
  239.5 1.9 collective-permute-start.16
  241.4 5.8 %collective-permute-done.16 = bf16[1,256,512]{2,1,0:T(8,128)(2,1)S(1)} collective-permute-done((bf16[1,256,512]{2,1,0:T(8,128)(2,1)S(1)}, bf16[1,256,512]{2,1,0:T(8,128)(2,1)S(1)}, u32[]{:S(2)}, u32[]{:S(2)}) %collective-permute-start.16) | collective-permute-done | bytes 262176 | tf_op jit(solution)/shard_map/ppermute | solution.py:17
  (106 shorter events, 28.0 us)
Async XLA Ops:
  6.5 104.6 %all-gather.3.cloned.1.call-start = ((), (), s32[]{:S(2)}) async-start(), calls=%async_computation.2 | async-start | bytes 2228224 | tf_op jit(solution)/shard_map/all_gather | solution.py:176
  11.5 89.6 %all-to-all-start = ((bf16[8,272,512]{2,1,0:T(8,128)(2,1)}), bf16[8,272,512]{2,1,0:T(8,128)(2,1)}, u32[]{:S(2)}, u32[]{:S(2)}) async-start(bf16[8,272,512]{2,1,0:T(8,128)(2,1)} %broadcast_in_dim.10), calls=%async_computation | async-start | bytes 4456448 | tf_op jit(solution)/shard_map/all_to_all | solution.py:189
  21.7 33.2 %copy-start.17 = (s32[32]{0:T(128)S(1)}, s32[32]{0:T(128)}, u32[]{:S(2)}) copy-start(s32[32]{0:T(128)} %order_ref.1) | copy-start | bytes 388
  21.7 169.3 %all-gather.5.cloned.1.call-start = ((), (), s32[]{:S(2)}) async-start(), calls=%async_computation.3 | async-start | bytes 2228224 | tf_op jit(solution)/shard_map/all_gather | solution.py:219
  21.8 24.9 %collective-permute-start.1 = (bf16[512,512]{1,0:T(8,128)(2,1)S(1)}, bf16[512,512]{1,0:T(8,128)(2,1)S(1)}, u32[]{:S(2)}, u32[]{:S(2)}) collective-permute-start(bf16[512,512]{1,0:T(8,128)(2,1)S(1)} %maximum_maximum_fusion.refs_0_), channel_id=1, source_target_pairs={{0,120},{8,0},{16,8},{24,16},{32,24},{40,32},{48,40},{56,48},{64,5... | collective-permute-start | bytes 1572872 | tf_op jit(solution)/shard_map/ppermute | solution.py:17
  30.5 22.0 %collective-permute-start = (bf16[512,512]{1,0:T(8,128)(2,1)S(1)}, bf16[512,512]{1,0:T(8,128)(2,1)S(1)}, u32[]{:S(2)}, u32[]{:S(2)}) collective-permute-start(bf16[512,512]{1,0:T(8,128)(2,1)S(1)} %maximum_maximum_fusion.refs_0_), channel_id=1, source_target_pairs={{0,8},{8,16},{16,24},{24,32},{32,40},{40,48},{48,56},{56,64},{64,7... | collective-permute-start | bytes 1572872 | tf_op jit(solution)/shard_map/ppermute | solution.py:17
  46.7 80.5 %copy-start.6 = (bf16[512,512]{1,0:T(8,128)(2,1)}, bf16[512,512]{1,0:T(8,128)(2,1)S(1)}, u32[]{:S(2)}) copy-start(bf16[512,512]{1,0:T(8,128)(2,1)S(1)} %collective-permute-done.1.refs_15_) | copy-start | bytes 1572868
  46.7 23.8 %collective-permute-start.3 = (bf16[512,512]{1,0:T(8,128)(2,1)S(1)}, bf16[512,512]{1,0:T(8,128)(2,1)S(1)}, u32[]{:S(2)}, u32[]{:S(2)}) collective-permute-start(bf16[512,512]{1,0:T(8,128)(2,1)S(1)} %collective-permute-done.1.refs_15_), channel_id=1, source_target_pairs={{0,120},{8,0},{16,8},{24,16},{32,24},{40,32},{48,40},{56,48},{64,5... | collective-permute-start | bytes 1572872 | tf_op jit(solution)/shard_map/ppermute | solution.py:17
  52.5 23.7 %copy-start.8 = (bf16[512,512]{1,0:T(8,128)(2,1)}, bf16[512,512]{1,0:T(8,128)(2,1)S(1)}, u32[]{:S(2)}) copy-start(bf16[512,512]{1,0:T(8,128)(2,1)S(1)} %collective-permute-done.refs_1_) | copy-start | bytes 1572868
  52.5 23.7 %collective-permute-start.2 = (bf16[512,512]{1,0:T(8,128)(2,1)S(1)}, bf16[512,512]{1,0:T(8,128)(2,1)S(1)}, u32[]{:S(2)}, u32[]{:S(2)}) collective-permute-start(bf16[512,512]{1,0:T(8,128)(2,1)S(1)} %collective-permute-done.refs_1_), channel_id=1, source_target_pairs={{0,8},{8,16},{16,24},{24,32},{32,40},{40,48},{48,56},{56,64},{64,7... | collective-permute-start | bytes 1572872 | tf_op jit(solution)/shard_map/ppermute | solution.py:17
  70.6 25.3 %collective-permute-start.5 = (bf16[512,512]{1,0:T(8,128)(2,1)S(1)}, bf16[512,512]{1,0:T(8,128)(2,1)S(1)}, u32[]{:S(2)}, u32[]{:S(2)}) collective-permute-start(bf16[512,512]{1,0:T(8,128)(2,1)S(1)} %collective-permute-done.3.refs_14_), channel_id=1, source_target_pairs={{0,120},{8,0},{16,8},{24,16},{32,24},{40,32},{48,40},{56,48},{64,5... | collective-permute-start | bytes 1572872 | tf_op jit(solution)/shard_map/ppermute | solution.py:17
  76.2 17.8 %collective-permute-start.4 = (bf16[512,512]{1,0:T(8,128)(2,1)S(1)}, bf16[512,512]{1,0:T(8,128)(2,1)S(1)}, u32[]{:S(2)}, u32[]{:S(2)}) collective-permute-start(bf16[512,512]{1,0:T(8,128)(2,1)S(1)} %collective-permute-done.2.refs_2_), channel_id=1, source_target_pairs={{0,8},{8,16},{16,24},{24,32},{32,40},{40,48},{48,56},{56,64},{64,7... | collective-permute-start | bytes 1572872 | tf_op jit(solution)/shard_map/ppermute | solution.py:17
  94.0 47.3 %copy-start = (bf16[512,512]{1,0:T(8,128)(2,1)}, bf16[512,512]{1,0:T(8,128)(2,1)S(1)}, u32[]{:S(2)}) copy-start(bf16[512,512]{1,0:T(8,128)(2,1)S(1)} %collective-permute-done.4.refs_3_) | copy-start | bytes 1572868
  94.0 17.2 %collective-permute-start.6 = (bf16[512,512]{1,0:T(8,128)(2,1)S(1)}, bf16[512,512]{1,0:T(8,128)(2,1)}, u32[]{:S(2)}, u32[]{:S(2)}) collective-permute-start(bf16[512,512]{1,0:T(8,128)(2,1)S(1)} %collective-permute-done.4.refs_3_), channel_id=1, source_target_pairs={{0,8},{8,16},{16,24},{24,32},{32,40},{40,48},{48,56},{56,64},{64,7... | collective-permute-start | bytes 1572872 | tf_op jit(solution)/shard_map/ppermute | solution.py:17
  95.9 15.2 %collective-permute-start.7 = (bf16[512,512]{1,0:T(8,128)(2,1)S(1)}, bf16[512,512]{1,0:T(8,128)(2,1)}, u32[]{:S(2)}, u32[]{:S(2)}) collective-permute-start(bf16[512,512]{1,0:T(8,128)(2,1)S(1)} %collective-permute-done.5.refs_13_), channel_id=1, source_target_pairs={{0,120},{8,0},{16,8},{24,16},{32,24},{40,32},{48,40},{56,48},{64,5... | collective-permute-start | bytes 1572872 | tf_op jit(solution)/shard_map/ppermute | solution.py:17
  120.1 15.0 %collective-permute-start.8 = (bf16[512,512]{1,0:T(8,128)(2,1)}, bf16[512,512]{1,0:T(8,128)(2,1)S(1)}, u32[]{:S(2)}, u32[]{:S(2)}) collective-permute-start(bf16[512,512]{1,0:T(8,128)(2,1)} %collective-permute-done.6.refs_4_), channel_id=1, source_target_pairs={{0,8},{8,16},{16,24},{24,32},{32,40},{40,48},{48,56},{56,64},{64,7... | collective-permute-start | bytes 1572872 | tf_op jit(solution)/shard_map/ppermute | solution.py:17
  122.1 17.3 %collective-permute-start.9 = (bf16[512,512]{1,0:T(8,128)(2,1)}, bf16[512,512]{1,0:T(8,128)(2,1)S(1)}, u32[]{:S(2)}, u32[]{:S(2)}) collective-permute-start(bf16[512,512]{1,0:T(8,128)(2,1)} %collective-permute-done.7.refs_12_), channel_id=1, source_target_pairs={{0,120},{8,0},{16,8},{24,16},{32,24},{40,32},{48,40},{56,48},{64,5... | collective-permute-start | bytes 1572872 | tf_op jit(solution)/shard_map/ppermute | solution.py:17
  135.2 25.1 %copy-start.11 = (bf16[512,512]{1,0:T(8,128)(2,1)}, bf16[512,512]{1,0:T(8,128)(2,1)S(1)}, u32[]{:S(2)}) copy-start(bf16[512,512]{1,0:T(8,128)(2,1)S(1)} %collective-permute-done.8.refs_5_) | copy-start | bytes 1572868
  139.4 27.5 %copy-start.13 = (bf16[512,512]{1,0:T(8,128)(2,1)}, bf16[512,512]{1,0:T(8,128)(2,1)S(1)}, u32[]{:S(2)}) copy-start(bf16[512,512]{1,0:T(8,128)(2,1)S(1)} %collective-permute-done.9.refs_11_) | copy-start | bytes 1572868
  139.4 18.9 %collective-permute-start.10 = (bf16[512,512]{1,0:T(8,128)(2,1)S(1)}, bf16[512,512]{1,0:T(8,128)(2,1)S(1)}, u32[]{:S(2)}, u32[]{:S(2)}) collective-permute-start(bf16[512,512]{1,0:T(8,128)(2,1)S(1)} %collective-permute-done.8.refs_5_), channel_id=1, source_target_pairs={{0,8},{8,16},{16,24},{24,32},{32,40},{40,48},{48,56},{56,64},{64,7... | collective-permute-start | bytes 1572872 | tf_op jit(solution)/shard_map/ppermute | solution.py:17
  141.6 18.9 %collective-permute-start.11 = (bf16[512,512]{1,0:T(8,128)(2,1)S(1)}, bf16[512,512]{1,0:T(8,128)(2,1)S(1)}, u32[]{:S(2)}, u32[]{:S(2)}) collective-permute-start(bf16[512,512]{1,0:T(8,128)(2,1)S(1)} %collective-permute-done.9.refs_11_), channel_id=1, source_target_pairs={{0,120},{8,0},{16,8},{24,16},{32,24},{40,32},{48,40},{56,48},{64,5... | collective-permute-start | bytes 1572872 | tf_op jit(solution)/shard_map/ppermute | solution.py:17
  158.3 22.6 %copy-start.2 = (bf16[512,512]{1,0:T(8,128)(2,1)}, bf16[512,512]{1,0:T(8,128)(2,1)S(1)}, u32[]{:S(2)}) copy-start(bf16[512,512]{1,0:T(8,128)(2,1)S(1)} %collective-permute-done.10.refs_6_) | copy-start | bytes 1572868
  158.3 20.7 %collective-permute-start.12 = (bf16[512,512]{1,0:T(8,128)(2,1)S(1)}, bf16[512,512]{1,0:T(8,128)(2,1)S(1)}, u32[]{:S(2)}, u32[]{:S(2)}) collective-permute-start(bf16[512,512]{1,0:T(8,128)(2,1)S(1)} %collective-permute-done.10.refs_6_), channel_id=1, source_target_pairs={{0,8},{8,16},{16,24},{24,32},{32,40},{40,48},{48,56},{56,64},{64,7... | collective-permute-start | bytes 1572872 | tf_op jit(solution)/shard_map/ppermute | solution.py:17
  160.5 20.7 %copy-start.4 = (bf16[512,512]{1,0:T(8,128)(2,1)}, bf16[512,512]{1,0:T(8,128)(2,1)S(1)}, u32[]{:S(2)}) copy-start(bf16[512,512]{1,0:T(8,128)(2,1)S(1)} %collective-permute-done.11.refs_10_) | copy-start | bytes 1572868
  160.5 20.7 %collective-permute-start.13 = (bf16[512,512]{1,0:T(8,128)(2,1)S(1)}, bf16[512,512]{1,0:T(8,128)(2,1)S(1)}, u32[]{:S(2)}, u32[]{:S(2)}) collective-permute-start(bf16[512,512]{1,0:T(8,128)(2,1)S(1)} %collective-permute-done.11.refs_10_), channel_id=1, source_target_pairs={{0,120},{8,0},{16,8},{24,16},{32,24},{40,32},{48,40},{56,48},{64,5... | collective-permute-start | bytes 1572872 | tf_op jit(solution)/shard_map/ppermute | solution.py:17
  179.0 10.4 %collective-permute-start.14 = (bf16[256,512]{1,0:T(8,128)(2,1)S(1)}, bf16[256,512]{1,0:T(8,128)(2,1)S(1)}, u32[]{:S(2)}, u32[]{:S(2)}) collective-permute-start(bf16[256,512]{1,0:T(8,128)(2,1)S(1)} %slice.164), channel_id=1, source_target_pairs={{0,8},{8,16},{16,24},{24,32},{32,40},{40,48},{48,56},{56,64},{64,7... | collective-permute-start | bytes 786440 | tf_op jit(solution)/shard_map/ppermute | solution.py:17
  181.9 27.8 %collective-permute-start.15 = (bf16[256,512]{1,0:T(8,128)(2,1)}, bf16[256,512]{1,0:T(8,128)(2,1)S(1)}, u32[]{:S(2)}, u32[]{:S(2)}) collective-permute-start(bf16[256,512]{1,0:T(8,128)(2,1)} %slice.166), channel_id=1, source_target_pairs={{0,120},{8,0},{16,8},{24,16},{32,24},{40,32},{48,40},{56,48},{64,5... | collective-permute-start | bytes 786440 | tf_op jit(solution)/shard_map/ppermute | solution.py:17
  194.6 15.2 %copy-start.7 = (bf16[512,512]{1,0:T(8,128)(2,1)S(1)}, bf16[512,512]{1,0:T(8,128)(2,1)}, u32[]{:S(2)}) copy-start(bf16[512,512]{1,0:T(8,128)(2,1)} %copy-done.6) | copy-start | bytes 1572868
  194.6 15.2 %copy-start.10 = (bf16[512,512]{1,0:T(8,128)(2,1)S(1)}, bf16[512,512]{1,0:T(8,128)(2,1)}, u32[]{:S(2)}) copy-start(bf16[512,512]{1,0:T(8,128)(2,1)} %copy-done.8) | copy-start | bytes 1572868
  194.6 15.2 %copy-start.12 = (bf16[512,512]{1,0:T(8,128)(2,1)S(1)}, bf16[512,512]{1,0:T(8,128)(2,1)}, u32[]{:S(2)}) copy-start(bf16[512,512]{1,0:T(8,128)(2,1)} %copy-done.11) | copy-start | bytes 1572868
  194.6 15.2 %copy-start.14 = (bf16[512,512]{1,0:T(8,128)(2,1)S(1)}, bf16[512,512]{1,0:T(8,128)(2,1)}, u32[]{:S(2)}) copy-start(bf16[512,512]{1,0:T(8,128)(2,1)} %copy-done.13) | copy-start | bytes 1572868
  239.5 7.7 %collective-permute-start.16 = (bf16[1,256,512]{2,1,0:T(8,128)(2,1)S(1)}, bf16[1,256,512]{2,1,0:T(8,128)(2,1)S(1)}, u32[]{:S(2)}, u32[]{:S(2)}) collective-permute-start(bf16[1,256,512]{2,1,0:T(8,128)(2,1)S(1)} %fusion.6), channel_id=1, source_target_pairs={{0,128},{128,256},{256,384},{384,0},{1,129},{129,257},{257,385},{3... | collective-permute-start | bytes 786440 | tf_op jit(solution)/shard_map/ppermute | solution.py:17
  (11 other events, 77.7 us)
Sparse Core Ops, SparseCore 0:
  9.4 82.4 all-gather.2
  116.3 74.6 all-gather.4

commit v3 on v1

v3 whole, which is shorter than its diff:
```python
import functools

import jax
import jax.numpy as jnp
from jax import lax
from jax.experimental import pallas as pl
from jax.experimental.pallas import tpu as pltpu
from jax.sharding import PartitionSpec as P

HD = 128


EPS = 1e-05
THETA = 500000.0


def passed_along(value, axis, by):
    length = lax.axis_size(axis)
    return lax.ppermute(value, axis, [(i, (i + by) % length) for i in range(length)])


def turning(pos):
    half = HD // 2
    index = jnp.arange(half, dtype=jnp.float32)
    freq = THETA ** (-2.0 * index / HD)
    angle = pos.astype(jnp.float32)[:, None] * freq[None, :]
    cosine = jnp.cos(angle)
    sine = jnp.sin(angle)
    return jnp.concatenate([cosine, cosine], axis=1), jnp.concatenate([-sine, sine], axis=1)


def positions_of(stored, stretch_order, block):
    which = stored // block
    slots = jnp.arange(stretch_order.shape[0], dtype=jnp.int32)
    picked = jnp.sum(jnp.where(which[:, None] == slots[None, :], stretch_order[None, :], 0), axis=1)
    return picked * block + stored % block


LOW = -1e20
MASKED = -1e30
MIB = 1024 * 1024


def normalise_kernel(spread_ref, out_ref):
    n_tp = spread_ref.shape[0]
    rows = out_ref.shape[0]
    part = out_ref.shape[1] // n_tp
    squares = jnp.zeros((rows, 1), jnp.float32)
    for i in range(n_tp):
        values = spread_ref[i, :rows, :].astype(jnp.float32)
        squares = squares + jnp.sum(values * values, axis=1, keepdims=True)
    factor = lax.rsqrt(squares / out_ref.shape[1] + EPS)
    for i in range(n_tp):
        values = spread_ref[i, :rows, :].astype(jnp.float32)
        terms = spread_ref[i, rows:, :].astype(jnp.float32)
        gain = terms[0:1] + terms[1:2] + terms[2:3]
        out_ref[:, i * part : (i + 1) * part] = (values * factor * gain).astype(out_ref.dtype)


def normalise(spread, rows):
    n_tp, _, part = spread.shape
    vmem = pl.BlockSpec(memory_space=pltpu.VMEM)
    return pl.pallas_call(
        normalise_kernel,
        out_shape=jax.ShapeDtypeStruct((rows, n_tp * part), jnp.bfloat16),
        in_specs=[vmem],
        out_specs=vmem,
        compiler_params=pltpu.CompilerParams(vmem_limit_bytes=16 * MIB),
        cost_estimate=pl.CostEstimate(
            flops=6 * rows * n_tp * part, bytes_accessed=4 * rows * n_tp * part, transcendentals=rows
        ),
    )(spread)


def rotated(raw, cosine, sine):
    half = raw.shape[1] // 2
    swapped = jnp.concatenate([raw[:, half:], raw[:, :half]], axis=1)
    return raw * cosine + swapped * sine


def streamed_dot(normed_ref, weights_ref, first, buffer_ref, sems):
    pieces, depth, wide = buffer_ref.shape
    copies = [
        pltpu.make_async_copy(
            weights_ref.at[pl.ds(i * depth, depth), pl.ds(first, wide)], buffer_ref.at[i], sems.at[i]
        )
        for i in range(pieces)
    ]
    for copy in copies:
        copy.start()
    total = None
    for i, copy in enumerate(copies):
        copy.wait()
        term = jnp.dot(
            normed_ref[:, i * depth : (i + 1) * depth],
            buffer_ref[i],
            preferred_element_type=jnp.float32,
        )
        total = term if total is None else total + term
    return total


def key_value_kernel(first, normed_ref, cosine_ref, sine_ref, weights_ref, out_ref, buffer_ref, sems):
    total = streamed_dot(normed_ref, weights_ref, first, buffer_ref, sems)
    key = rotated(total[:, :HD], cosine_ref[...], sine_ref[...])
    out_ref[:, :HD] = key.astype(out_ref.dtype)
    out_ref[:, HD:] = total[:, HD:].astype(out_ref.dtype)


def query_kernel(first, normed_ref, cosine_ref, sine_ref, weights_ref, out_ref, buffer_ref, sems):
    total = streamed_dot(normed_ref, weights_ref, first, buffer_ref, sems)
    cosine, sine = cosine_ref[...], sine_ref[...]
    for head in range(out_ref.shape[0]):
        raw = total[:, head * HD : (head + 1) * HD]
        out_ref[head] = rotated(raw, cosine, sine).astype(out_ref.dtype)


def project(kernel, shape, wide, first, normed, cosine, sine, weights):
    rows, width = normed.shape
    pieces = 8
    vmem = pl.BlockSpec(memory_space=pltpu.VMEM)
    return pl.pallas_call(
        functools.partial(kernel, first),
        out_shape=jax.ShapeDtypeStruct(shape, jnp.bfloat16),
        in_specs=[vmem] * 3 + [pl.BlockSpec(memory_space=pltpu.HBM)],
        out_specs=vmem,
        scratch_shapes=[
            pltpu.VMEM((pieces, width // pieces, wide), jnp.bfloat16),
            pltpu.SemaphoreType.DMA((pieces,)),
        ],
        compiler_params=pltpu.CompilerParams(vmem_limit_bytes=16 * MIB),
        cost_estimate=pl.CostEstimate(
            flops=2 * rows * width * wide, bytes_accessed=2 * width * wide, transcendentals=0
        ),
    )(normed, cosine, sine, weights)


def attend_kernel(starts_ref, query_ref, query_pos_ref, peak_ref, total_ref, accum_ref, *refs):
    new_peak_ref, new_total_ref, new_accum_ref = refs[-3:]
    held = refs[:-3]
    heads, rows, size = query_ref.shape
    block = rows // 2
    rate = 1.4426950408889634 / size**0.5
    query_pos = query_pos_ref[...]
    within = lax.broadcasted_iota(jnp.int32, (block, rows), 0)
    key = jnp.concatenate([ref[:, :size] for ref in held], axis=0)
    value = jnp.concatenate([ref[:, size:] for ref in held], axis=0).T
    allowed = jnp.concatenate(
        [within + starts_ref[i] <= query_pos for i in range(2 * len(held))], axis=0
    )
    scores = [
        jnp.where(
            allowed,
            lax.dot_general(
                key,
                query_ref[head],
                (((1,), (1,)), ((), ())),
                preferred_element_type=jnp.float32,
            ),
            MASKED,
        )
        for head in range(heads)
    ]
    for head in range(heads):
        peak = peak_ref[head]
        new_peak = jnp.maximum(peak, jnp.max(scores[head], axis=0, keepdims=True))
        probs = jnp.exp2((scores[head] - new_peak) * rate)
        fade = jnp.exp2((peak - new_peak) * rate)
        mixed = jnp.dot(value, probs.astype(jnp.bfloat16), preferred_element_type=jnp.float32)
        new_total = total_ref[head] * fade + jnp.sum(probs, axis=0, keepdims=True)
        new_peak_ref[head] = new_peak
        new_total_ref[head] = new_total
        new_accum_ref[head] = accum_ref[head] * fade + mixed


def attend(starts, query, query_pos, state, held):
    heads, rows, _ = query.shape
    keys = rows * len(held)
    vmem = pl.BlockSpec(memory_space=pltpu.VMEM)
    return pl.pallas_call(
        attend_kernel,
        out_shape=[jax.ShapeDtypeStruct(part.shape, part.dtype) for part in state],
        in_specs=[pl.BlockSpec(memory_space=pltpu.SMEM)] + [vmem] * (5 + len(held)),
        out_specs=[vmem] * 3,
        compiler_params=pltpu.CompilerParams(vmem_limit_bytes=16 * MIB),
        cost_estimate=pl.CostEstimate(
            flops=4 * heads * rows * HD * keys,
            bytes_accessed=4 * HD * keys,
            transcendentals=heads * rows * keys,
        ),
    )(starts, query, query_pos, *state, *held)


def project_out_kernel(total_ref, accum_ref, weights_ref, out_ref, context_ref):
    blocks, depth, packed = weights_ref.shape
    heads, size, _ = accum_ref.shape
    per = out_ref.shape[0] * out_ref.shape[2] // blocks
    share = out_ref.shape[2] // per

    @pl.when(pl.program_id(0) == 0)
    def _():
        for head in range(heads):
            context = (accum_ref[head] / total_ref[head]).T
            context_ref[:, head * size : (head + 1) * size] = context.astype(context_ref.dtype)

    for at in range(blocks):
        total = None
        for i in range(packed // per):
            term = jnp.dot(
                context_ref[:, i * depth : (i + 1) * depth],
                weights_ref[at, :, i * per : (i + 1) * per],
                preferred_element_type=jnp.float32,
            )
            total = term if total is None else total + term
        column = (at % share) * per
        out_ref[at // share, :, column : column + per] = total.astype(out_ref.dtype)


def project_out(total, accum, packed, n_tp):
    heads, size, rows = accum.shape
    n_ctx, deep, wide = packed.shape
    part = heads * size
    steps = 4
    return pl.pallas_call(
        project_out_kernel,
        grid=(steps,),
        out_shape=jax.ShapeDtypeStruct((n_tp, rows, part), jnp.bfloat16),
        in_specs=[
            pl.BlockSpec(total.shape, lambda k: (0, 0, 0)),
            pl.BlockSpec(accum.shape, lambda k: (0, 0, 0)),
            pl.BlockSpec((n_ctx // steps, deep, wide), lambda k: (k, 0, 0)),
        ],
        out_specs=pl.BlockSpec((n_tp // steps, rows, part), lambda k: (k, 0, 0)),
        scratch_shapes=[pltpu.VMEM((rows, part), jnp.bfloat16)],
        compiler_params=pltpu.CompilerParams(
            dimension_semantics=("arbitrary",), vmem_limit_bytes=16 * MIB
        ),
        cost_estimate=pl.CostEstimate(
            flops=2 * rows * part * part * n_tp,
            bytes_accessed=4 * part * part * n_tp,
            transcendentals=0,
        ),
    )(total, accum, packed)


def shards(section_in, stretch_order, norm_gain, w_query, w_key, w_value, w_out):
    hidden = section_in[0]
    rows, part = hidden.shape
    block = rows // 2
    n_ctx = lax.axis_size("ctx")
    n_tp = lax.axis_size("tp")
    me = lax.axis_index("ctx")
    heads = w_query.shape[2] // HD
    depth = w_query.shape[1]
    span = w_out.shape[2]
    w_mine = jnp.concatenate([w_query[0], w_key[0], w_value[0]], axis=1)
    w_all = lax.all_gather(w_mine, "ctx", axis=0, tiled=True)
    gain = norm_gain[0]
    high = lax.reduce_precision(gain, 8, 7)
    middle = lax.reduce_precision(gain - high, 8, 7)
    low = gain - high - middle
    extra = jnp.zeros((16, part), jnp.float32)
    extra = extra.at[0].set(high).at[1].set(middle).at[2].set(low)
    payload = jnp.concatenate([hidden, extra.astype(jnp.bfloat16)], axis=0)
    spread = lax.all_to_all(
        jnp.broadcast_to(payload[None], (n_tp,) + payload.shape), "tp", 0, 0
    )
    normed = normalise(spread, rows)
    folded = [w_out[0, i * depth : (i + 1) * depth] for i in range(part // span)]
    w_out_mine, payload = lax.optimization_barrier((jnp.concatenate(folded, axis=1), payload))
    packed = lax.all_gather(w_out_mine, "ctx", axis=0, tiled=False)

    local_rows = jnp.arange(rows, dtype=jnp.int32)
    query_pos = positions_of(me * rows + local_rows, stretch_order, block)
    cosine, sine = turning(query_pos)
    query_pos = query_pos[None, :]

    def starts_of(turns):
        stored = jnp.stack([2 * ((me - turn) % n_ctx) + i for turn in turns for i in range(2)])
        return positions_of(stored * block, stretch_order, block)

    keys_values = project(
        key_value_kernel, (rows, 2 * HD), 2 * HD, part, normed, cosine, sine, w_all
    )
    after, _ = lax.optimization_barrier((normed, keys_values))
    query = project(
        query_kernel, (heads, rows, HD), part, 0, after, cosine, sine, w_all
    )
    state = (
        jnp.full((heads, 1, rows), LOW, jnp.float32),
        jnp.zeros((heads, 1, rows), jnp.float32),
        jnp.zeros((heads, HD, rows), jnp.float32),
    )
    half = n_ctx // 2
    up = down = keys_values
    held, turns = [keys_values], [0]
    for turn in range(1, half + 1):
        up = passed_along(up, "ctx", 1)
        if turn < half:
            down = passed_along(down, "ctx", -1)
        state = attend(starts_of(turns), query, query_pos, state, held)
        up, state = lax.optimization_barrier((up, state))
        held, turns = ([up, down], [turn, -turn]) if turn < half else ([up], [turn])
    state = attend(starts_of(turns), query, query_pos, state, held)
    terms = project_out(state[1], state[2], packed, n_tp)
    parts = lax.all_to_all(terms, "tp", 0, 0)
    summed = jnp.sum(parts.astype(jnp.float32), axis=0)
    result = (hidden.astype(jnp.float32) + summed).astype(jnp.bfloat16)[None]
    return passed_along(result, "pipe", 1)


def solution(mesh):
    in_specs = (
        P("pipe", "ctx", "tp"),
        P(),
        P("pipe", "tp"),
        P("pipe", "ctx", "tp"),
        P("pipe", "ctx", "tp"),
        P("pipe", "ctx", "tp"),
        P("pipe", "tp", "ctx"),
    )
    out_specs = P("pipe", "ctx", "tp")
    return jax.shard_map(shards, mesh=mesh, in_specs=in_specs, out_specs=out_specs, check_vma=False)
```

time: 247 us -> 237 us (0.960)
  Pallas kernels: 0 us -> 21.1 us
  matrix products: 18.7 us -> 0 us
  blocking collectives: 47 us -> 29.6 us
  other arithmetic: 13.1 us -> 5.54 us
  waiting for transfers between devices: 82.4 us -> 89.6 us
  local copies, waits for them, and re-layouts: 4.3 us -> 11.4 us
    pallas_call x0 -> x13, Pallas kernels: none -> 21.1 us  [the longest x9 14.1 us: attend(): pl.pallas_call(attend_kernel, out_shape=[jax.ShapeDtypeStruct(part.shape,...]
    psum x1 -> x0, blocking collectives: 20.6 us -> none  [shards(): squares = lax.psum(jnp.sum(local * local, axis=1), 'tp')]
    dot_general x20 -> x0, matrix products: 18.7 us -> none  [the longest x9 6.61 us: attend(): jnp.einsum('hqk,kd->hqd', probs.astype(jnp.bfloat16), keys_values[1], pre...]
    all_gather x1, waiting for transfers between devices: 37 us -> 48.7 us  [shards(): w_all = lax.all_gather(w_mine, 'ctx', axis=0, tiled=True)]
    ppermute x16, waiting for transfers between devices: 27.4 us -> 17.8 us  [passed_along(): lax.ppermute(value, axis, [(i, (i + by) % length) for i in range(length)])]
    unnamed x36 -> x13, local copies, waits for them, and re-layouts: 1.92 us -> 8.71 us
    all_to_all x1, waiting for transfers between devices: 17.2 us -> 23.1 us  [shards(): lax.all_to_all(jnp.broadcast_to(payload[None], (n_tp,) + payload.shape),...]
    reduce_sum x10 -> x0, other arithmetic: 5.26 us -> none  [the longest x9 4.18 us: attend(): total = total * factor + jnp.sum(probs, axis=2)]
  transfers between devices with their start and end apart: 19 -> 19, of which waited for: 16 -> 13; matrix products, arithmetic and copies ran while one was open for 12% -> 3% of each run, Pallas kernels for 0% -> 8%
where the time goes in v3:
time: 237 us; the launch traced here: 235 us
  waiting for transfers between devices  89.6 us (38%)
  starting transfers between devices  63.9 us (27%)
  blocking collectives  29.6 us (12%)
  Pallas kernels  21.1 us (9%)
  between operations  14.1 us (6%)
  local copies, waits for them, and re-layouts  11.4 us (5%)
  other arithmetic  5.54 us (2%)
    ppermute x16, starting transfers between devices, passed_along(): lax.ppermute(value, axis, [(i, (i + by) % length) for i in range(length)])  54.4 us
    all_gather x1, waiting for transfers between devices, shards(): w_all = lax.all_gather(w_mine, 'ctx', axis=0, tiled=True)  48.7 us
    all_to_all x1, blocking collectives, shards(): parts = lax.all_to_all(terms, 'tp', 0, 0)  29.6 us
    all_to_all x1, waiting for transfers between devices, shards(): lax.all_to_all(jnp.broadcast_to(payload[None], (n_tp,) + payload.shape),...  23.1 us
    ppermute x16, waiting for transfers between devices, passed_along(): lax.ppermute(value, axis, [(i, (i + by) % length) for i in range(length)])  17.8 us
    pallas_call x9, Pallas kernels, attend(): pl.pallas_call(attend_kernel, out_shape=[jax.ShapeDtypeStruct(part.shape,...  14.1 us
    all_to_all x1, starting transfers between devices, shards(): lax.all_to_all(jnp.broadcast_to(payload[None], (n_tp,) + payload.shape),...  9.51 us
    unnamed x13, local copies, waits for them, and re-layouts  8.71 us
  transfers between devices with their start and end apart: 19, of which 13 were waited for; matrix products, arithmetic and copies ran while one was open for 3% of the time, Pallas kernels for 8%

profile of v3, /device:TPU:6, one launch (start us, length us, event | category | flops | bytes accessed | tf_op | source)
XLA Modules:
  0.0 235.3 jit_solution(10509345974274988068)
XLA Ops:
  6.5 1.9 pad_maximum_fusion
  12.6 9.5 %all-to-all-start = ((bf16[8,272,512]{2,1,0:T(8,128)(2,1)}), bf16[8,272,512]{2,1,0:T(8,128)(2,1)S(1)}, u32[]{:S(2)}, u32[]{:S(2)}) async-start(bf16[8,272,512]{2,1,0:T(8,128)(2,1)} %broadcast_in_dim.116), calls=%async_computation | async-start | bytes 4456448 | tf_op jit(solution)/shard_map/all_to_all | solution.py:265
  24.2 23.1 %all-to-all-done.spread_ref = bf16[8,272,512]{2,1,0:T(8,128)(2,1)S(1)} async-done(((bf16[8,272,512]{2,1,0:T(8,128)(2,1)}), bf16[8,272,512]{2,1,0:T(8,128)(2,1)S(1)}, u32[]{:S(2)}, u32[]{:S(2)}) %all-to-all-start) | async-done | bytes 2228256 | tf_op jit(solution)/shard_map/all_to_all | solution.py:265
  48.7 1.6 copy-done.2
  51.4 48.7 %all-gather.4.cloned.1.call-done.weights_ref = bf16[4096,768]{1,0:T(8,128)(2,1)} async-done(((bf16[256,768]{1,0:T(8,128)(2,1)}), bf16[4096,768]{1,0:T(8,128)(2,1)}) %all-gather.4.cloned.1.call-update) | async-done | bytes 6291472 | tf_op jit(solution)/shard_map/all_gather | solution.py:257
  100.0 2.8 %copy-done = bf16[4096,768]{1,0:T(8,128)(2,1)S(1)} copy-done((bf16[4096,768]{1,0:T(8,128)(2,1)S(1)}, bf16[4096,768]{1,0:T(8,128)(2,1)}, u32[]{:S(2)}) %copy-start) | copy-done | bytes 6291480
  102.8 1.9 shard_map.74.refs_0_
  104.7 2.8 %collective-permute-start = (bf16[256,256]{1,0:T(8,128)(2,1)S(1)}, bf16[256,256]{1,0:T(8,128)(2,1)S(1)}, u32[]{:S(2)}, u32[]{:S(2)}) collective-permute-start(bf16[256,256]{1,0:T(8,128)(2,1)S(1)} %shard_map.74.refs_0_), channel_id=1, source_target_pairs={{0,8},{8,16},{16,24},{24,32},{32,40},{40,48},{48,56},{56,64},{64,7... | collective-permute-start | bytes 393224 | tf_op jit(solution)/shard_map/ppermute | solution.py:19
  107.5 4.3 %collective-permute-start.2 = (bf16[256,256]{1,0:T(8,128)(2,1)S(1)}, bf16[256,256]{1,0:T(8,128)(2,1)S(1)}, u32[]{:S(2)}, u32[]{:S(2)}) collective-permute-start(bf16[256,256]{1,0:T(8,128)(2,1)S(1)} %shard_map.74.refs_0_), channel_id=1, source_target_pairs={{0,120},{8,0},{16,8},{24,16},{32,24},{40,32},{48,40},{56,48},{64,5... | collective-permute-start | bytes 393224 | tf_op jit(solution)/shard_map/ppermute | solution.py:19
  111.8 2.2 shard_map.75.query_ref
  115.2 1.9 collective-permute-start.1
  117.2 5.1 %collective-permute-start.4 = (bf16[256,256]{1,0:T(8,128)(2,1)S(1)}, bf16[256,256]{1,0:T(8,128)(2,1)S(1)}, u32[]{:S(2)}, u32[]{:S(2)}) collective-permute-start(bf16[256,256]{1,0:T(8,128)(2,1)S(1)} %collective-permute-done.2.refs_1_), channel_id=1, source_target_pairs={{0,120},{8,0},{16,8},{24,16},{32,24},{40,32},{48,40},{56,48},{64,5... | collective-permute-start | bytes 393224 | tf_op jit(solution)/shard_map/ppermute | solution.py:19
  124.8 1.9 collective-permute-start.3
  126.7 5.2 %collective-permute-start.6 = (bf16[256,256]{1,0:T(8,128)(2,1)S(1)}, bf16[256,256]{1,0:T(8,128)(2,1)S(1)}, u32[]{:S(2)}, u32[]{:S(2)}) collective-permute-start(bf16[256,256]{1,0:T(8,128)(2,1)S(1)} %collective-permute-done.4.refs_1_), channel_id=1, source_target_pairs={{0,120},{8,0},{16,8},{24,16},{32,24},{40,32},{48,40},{56,48},{64,5... | collective-permute-start | bytes 393224 | tf_op jit(solution)/shard_map/ppermute | solution.py:19
  133.5 1.7 collective-permute-done.3.refs_0_
  135.3 1.9 collective-permute-start.5
  137.2 5.1 %collective-permute-start.8 = (bf16[256,256]{1,0:T(8,128)(2,1)S(1)}, bf16[256,256]{1,0:T(8,128)(2,1)S(1)}, u32[]{:S(2)}, u32[]{:S(2)}) collective-permute-start(bf16[256,256]{1,0:T(8,128)(2,1)S(1)} %collective-permute-done.6.refs_1_), channel_id=1, source_target_pairs={{0,120},{8,0},{16,8},{24,16},{32,24},{40,32},{48,40},{56,48},{64,5... | collective-permute-start | bytes 393224 | tf_op jit(solution)/shard_map/ppermute | solution.py:19
  144.3 1.9 collective-permute-start.7
  146.5 4.9 %collective-permute-start.10 = (bf16[256,256]{1,0:T(8,128)(2,1)S(1)}, bf16[256,256]{1,0:T(8,128)(2,1)S(1)}, u32[]{:S(2)}, u32[]{:S(2)}) collective-permute-start(bf16[256,256]{1,0:T(8,128)(2,1)S(1)} %collective-permute-done.8.refs_1_), channel_id=1, source_target_pairs={{0,120},{8,0},{16,8},{24,16},{32,24},{40,32},{48,40},{56,48},{64,5... | collective-permute-start | bytes 393224 | tf_op jit(solution)/shard_map/ppermute | solution.py:19
  153.0 1.8 collective-permute-done.7.refs_0_
  154.8 1.9 collective-permute-start.9
  157.3 5.6 %collective-permute-start.12 = (bf16[256,256]{1,0:T(8,128)(2,1)S(1)}, bf16[256,256]{1,0:T(8,128)(2,1)S(1)}, u32[]{:S(2)}, u32[]{:S(2)}) collective-permute-start(bf16[256,256]{1,0:T(8,128)(2,1)S(1)} %collective-permute-done.10.refs_1_), channel_id=1, source_target_pairs={{0,120},{8,0},{16,8},{24,16},{32,24},{40,32},{48,40},{56,48},{64,5... | collective-permute-start | bytes 393224 | tf_op jit(solution)/shard_map/ppermute | solution.py:19
  164.7 2.2 collective-permute-start.11
  168.4 5.8 %collective-permute-start.14 = (bf16[256,256]{1,0:T(8,128)(2,1)S(1)}, bf16[256,256]{1,0:T(8,128)(2,1)S(1)}, u32[]{:S(2)}, u32[]{:S(2)}) collective-permute-start(bf16[256,256]{1,0:T(8,128)(2,1)S(1)} %collective-permute-done.12.refs_1_), channel_id=1, source_target_pairs={{0,120},{8,0},{16,8},{24,16},{32,24},{40,32},{48,40},{56,48},{64,5... | collective-permute-start | bytes 393224 | tf_op jit(solution)/shard_map/ppermute | solution.py:19
  175.8 1.9 collective-permute-start.13
  179.5 4.7 %collective-permute-done.13.refs_0_ = bf16[256,256]{1,0:T(8,128)(2,1)S(1)} collective-permute-done((bf16[256,256]{1,0:T(8,128)(2,1)S(1)}, bf16[256,256]{1,0:T(8,128)(2,1)S(1)}, u32[]{:S(2)}, u32[]{:S(2)}) %collective-permute-start.13) | collective-permute-done | bytes 131104 | tf_op jit(solution)/shard_map/ppermute | solution.py:19
  184.2 1.7 shard_map.84
  185.9 2.2 copy-done.3
  188.1 2.0 shard_map.85
  190.1 29.6 %all_to_all.10 = bf16[8,256,512]{2,1,0:T(8,128)(2,1)S(1)} all-to-all(bf16[8,256,512]{2,1,0:T(8,128)(2,1)S(1)} %shard_map.85), channel_id=1, replica_groups=mesh['pipe'=4,'ctx'=16,'tp'=8] {'tp'}, dimensions={0} | all-to-all | bytes 4194304 | tf_op jit(solution)/shard_map/all_to_all | solution.py:306
  220.1 1.9 collective-permute-start.15
  222.0 5.8 %collective-permute-done.15 = bf16[1,256,512]{2,1,0:T(8,128)(2,1)S(1)} collective-permute-done((bf16[1,256,512]{2,1,0:T(8,128)(2,1)S(1)}, bf16[1,256,512]{2,1,0:T(8,128)(2,1)S(1)}, u32[]{:S(2)}, u32[]{:S(2)}) %collective-permute-start.15) | collective-permute-done | bytes 262176 | tf_op jit(solution)/shard_map/ppermute | solution.py:19
  (72 shorter events, 25.8 us)
Async XLA Ops:
  6.5 4.5 %copy-start.4 = (bf16[1,256,512]{2,1,0:T(8,128)(2,1)S(1)}, bf16[1,256,512]{2,1,0:T(8,128)(2,1)}, u32[]{:S(2)}) copy-start(bf16[1,256,512]{2,1,0:T(8,128)(2,1)} %param.13) | copy-start | bytes 786436
  6.5 93.5 %all-gather.4.cloned.1.call-start = ((), (), s32[]{:S(2)}) async-start(), calls=%async_computation.2 | async-start | bytes 6684672 | tf_op jit(solution)/shard_map/all_gather | solution.py:257
  8.4 177.5 %all-gather.6.cloned.1.call-start = ((), (), s32[]{:S(2)}) async-start(), calls=%async_computation.3 | async-start | bytes 4456448 | tf_op jit(solution)/shard_map/all_gather | solution.py:271
  12.6 10.3 %copy-start.5 = (s32[32]{0:T(128)S(1)}, s32[32]{0:T(128)}, u32[]{:S(2)}) copy-start(s32[32]{0:T(128)} %param.14) | copy-start | bytes 388
  12.6 34.7 %all-to-all-start = ((bf16[8,272,512]{2,1,0:T(8,128)(2,1)}), bf16[8,272,512]{2,1,0:T(8,128)(2,1)S(1)}, u32[]{:S(2)}, u32[]{:S(2)}) async-start(bf16[8,272,512]{2,1,0:T(8,128)(2,1)} %broadcast_in_dim.116), calls=%async_computation | async-start | bytes 4456448 | tf_op jit(solution)/shard_map/all_to_all | solution.py:265
  47.3 1.4 copy-start.1
  48.7 1.6 copy-start.2
  100.0 2.8 %copy-start = (bf16[4096,768]{1,0:T(8,128)(2,1)S(1)}, bf16[4096,768]{1,0:T(8,128)(2,1)}, u32[]{:S(2)}) copy-start(bf16[4096,768]{1,0:T(8,128)(2,1)} %all-gather.4.cloned.1.call-done.weights_ref) | copy-start | bytes 18874372
  104.7 10.5 %collective-permute-start = (bf16[256,256]{1,0:T(8,128)(2,1)S(1)}, bf16[256,256]{1,0:T(8,128)(2,1)S(1)}, u32[]{:S(2)}, u32[]{:S(2)}) collective-permute-start(bf16[256,256]{1,0:T(8,128)(2,1)S(1)} %shard_map.74.refs_0_), channel_id=1, source_target_pairs={{0,8},{8,16},{16,24},{24,32},{32,40},{40,48},{48,56},{56,64},{64,7... | collective-permute-start | bytes 393224 | tf_op jit(solution)/shard_map/ppermute | solution.py:19
  107.5 9.7 %collective-permute-start.2 = (bf16[256,256]{1,0:T(8,128)(2,1)S(1)}, bf16[256,256]{1,0:T(8,128)(2,1)S(1)}, u32[]{:S(2)}, u32[]{:S(2)}) collective-permute-start(bf16[256,256]{1,0:T(8,128)(2,1)S(1)} %shard_map.74.refs_0_), channel_id=1, source_target_pairs={{0,120},{8,0},{16,8},{24,16},{32,24},{40,32},{48,40},{56,48},{64,5... | collective-permute-start | bytes 393224 | tf_op jit(solution)/shard_map/ppermute | solution.py:19
  115.2 9.5 %collective-permute-start.1 = (bf16[256,256]{1,0:T(8,128)(2,1)S(1)}, bf16[256,256]{1,0:T(8,128)(2,1)S(1)}, u32[]{:S(2)}, u32[]{:S(2)}) collective-permute-start(bf16[256,256]{1,0:T(8,128)(2,1)S(1)} %collective-permute-done.refs_0_), channel_id=1, source_target_pairs={{0,8},{8,16},{16,24},{24,32},{32,40},{40,48},{48,56},{56,64},{64,7... | collective-permute-start | bytes 393224 | tf_op jit(solution)/shard_map/ppermute | solution.py:19
  117.2 9.5 %collective-permute-start.4 = (bf16[256,256]{1,0:T(8,128)(2,1)S(1)}, bf16[256,256]{1,0:T(8,128)(2,1)S(1)}, u32[]{:S(2)}, u32[]{:S(2)}) collective-permute-start(bf16[256,256]{1,0:T(8,128)(2,1)S(1)} %collective-permute-done.2.refs_1_), channel_id=1, source_target_pairs={{0,120},{8,0},{16,8},{24,16},{32,24},{40,32},{48,40},{56,48},{64,5... | collective-permute-start | bytes 393224 | tf_op jit(solution)/shard_map/ppermute | solution.py:19
  124.8 10.5 %collective-permute-start.3 = (bf16[256,256]{1,0:T(8,128)(2,1)S(1)}, bf16[256,256]{1,0:T(8,128)(2,1)S(1)}, u32[]{:S(2)}, u32[]{:S(2)}) collective-permute-start(bf16[256,256]{1,0:T(8,128)(2,1)S(1)} %collective-permute-done.1.refs_0_), channel_id=1, source_target_pairs={{0,8},{8,16},{16,24},{24,32},{32,40},{40,48},{48,56},{56,64},{64,7... | collective-permute-start | bytes 393224 | tf_op jit(solution)/shard_map/ppermute | solution.py:19
  126.7 10.5 %collective-permute-start.6 = (bf16[256,256]{1,0:T(8,128)(2,1)S(1)}, bf16[256,256]{1,0:T(8,128)(2,1)S(1)}, u32[]{:S(2)}, u32[]{:S(2)}) collective-permute-start(bf16[256,256]{1,0:T(8,128)(2,1)S(1)} %collective-permute-done.4.refs_1_), channel_id=1, source_target_pairs={{0,120},{8,0},{16,8},{24,16},{32,24},{40,32},{48,40},{56,48},{64,5... | collective-permute-start | bytes 393224 | tf_op jit(solution)/shard_map/ppermute | solution.py:19
  135.3 9.1 %collective-permute-start.5 = (bf16[256,256]{1,0:T(8,128)(2,1)S(1)}, bf16[256,256]{1,0:T(8,128)(2,1)S(1)}, u32[]{:S(2)}, u32[]{:S(2)}) collective-permute-start(bf16[256,256]{1,0:T(8,128)(2,1)S(1)} %collective-permute-done.3.refs_0_), channel_id=1, source_target_pairs={{0,8},{8,16},{16,24},{24,32},{32,40},{40,48},{48,56},{56,64},{64,7... | collective-permute-start | bytes 393224 | tf_op jit(solution)/shard_map/ppermute | solution.py:19
  137.2 9.3 %collective-permute-start.8 = (bf16[256,256]{1,0:T(8,128)(2,1)S(1)}, bf16[256,256]{1,0:T(8,128)(2,1)S(1)}, u32[]{:S(2)}, u32[]{:S(2)}) collective-permute-start(bf16[256,256]{1,0:T(8,128)(2,1)S(1)} %collective-permute-done.6.refs_1_), channel_id=1, source_target_pairs={{0,120},{8,0},{16,8},{24,16},{32,24},{40,32},{48,40},{56,48},{64,5... | collective-permute-start | bytes 393224 | tf_op jit(solution)/shard_map/ppermute | solution.py:19
  144.3 10.5 %collective-permute-start.7 = (bf16[256,256]{1,0:T(8,128)(2,1)S(1)}, bf16[256,256]{1,0:T(8,128)(2,1)S(1)}, u32[]{:S(2)}, u32[]{:S(2)}) collective-permute-start(bf16[256,256]{1,0:T(8,128)(2,1)S(1)} %collective-permute-done.5.refs_0_), channel_id=1, source_target_pairs={{0,8},{8,16},{16,24},{24,32},{32,40},{40,48},{48,56},{56,64},{64,7... | collective-permute-start | bytes 393224 | tf_op jit(solution)/shard_map/ppermute | solution.py:19
  146.5 10.8 %collective-permute-start.10 = (bf16[256,256]{1,0:T(8,128)(2,1)S(1)}, bf16[256,256]{1,0:T(8,128)(2,1)S(1)}, u32[]{:S(2)}, u32[]{:S(2)}) collective-permute-start(bf16[256,256]{1,0:T(8,128)(2,1)S(1)} %collective-permute-done.8.refs_1_), channel_id=1, source_target_pairs={{0,120},{8,0},{16,8},{24,16},{32,24},{40,32},{48,40},{56,48},{64,5... | collective-permute-start | bytes 393224 | tf_op jit(solution)/shard_map/ppermute | solution.py:19
  154.8 9.8 %collective-permute-start.9 = (bf16[256,256]{1,0:T(8,128)(2,1)S(1)}, bf16[256,256]{1,0:T(8,128)(2,1)S(1)}, u32[]{:S(2)}, u32[]{:S(2)}) collective-permute-start(bf16[256,256]{1,0:T(8,128)(2,1)S(1)} %collective-permute-done.7.refs_0_), channel_id=1, source_target_pairs={{0,8},{8,16},{16,24},{24,32},{32,40},{40,48},{48,56},{56,64},{64,7... | collective-permute-start | bytes 393224 | tf_op jit(solution)/shard_map/ppermute | solution.py:19
  157.3 11.1 %collective-permute-start.12 = (bf16[256,256]{1,0:T(8,128)(2,1)S(1)}, bf16[256,256]{1,0:T(8,128)(2,1)S(1)}, u32[]{:S(2)}, u32[]{:S(2)}) collective-permute-start(bf16[256,256]{1,0:T(8,128)(2,1)S(1)} %collective-permute-done.10.refs_1_), channel_id=1, source_target_pairs={{0,120},{8,0},{16,8},{24,16},{32,24},{40,32},{48,40},{56,48},{64,5... | collective-permute-start | bytes 393224 | tf_op jit(solution)/shard_map/ppermute | solution.py:19
  164.7 11.1 %collective-permute-start.11 = (bf16[256,256]{1,0:T(8,128)(2,1)S(1)}, bf16[256,256]{1,0:T(8,128)(2,1)S(1)}, u32[]{:S(2)}, u32[]{:S(2)}) collective-permute-start(bf16[256,256]{1,0:T(8,128)(2,1)S(1)} %collective-permute-done.9.refs_0_), channel_id=1, source_target_pairs={{0,8},{8,16},{16,24},{24,32},{32,40},{40,48},{48,56},{56,64},{64,7... | collective-permute-start | bytes 393224 | tf_op jit(solution)/shard_map/ppermute | solution.py:19
  168.4 9.5 %collective-permute-start.14 = (bf16[256,256]{1,0:T(8,128)(2,1)S(1)}, bf16[256,256]{1,0:T(8,128)(2,1)S(1)}, u32[]{:S(2)}, u32[]{:S(2)}) collective-permute-start(bf16[256,256]{1,0:T(8,128)(2,1)S(1)} %collective-permute-done.12.refs_1_), channel_id=1, source_target_pairs={{0,120},{8,0},{16,8},{24,16},{32,24},{40,32},{48,40},{56,48},{64,5... | collective-permute-start | bytes 393224 | tf_op jit(solution)/shard_map/ppermute | solution.py:19
  175.8 8.4 %collective-permute-start.13 = (bf16[256,256]{1,0:T(8,128)(2,1)S(1)}, bf16[256,256]{1,0:T(8,128)(2,1)S(1)}, u32[]{:S(2)}, u32[]{:S(2)}) collective-permute-start(bf16[256,256]{1,0:T(8,128)(2,1)S(1)} %collective-permute-done.11.refs_0_), channel_id=1, source_target_pairs={{0,8},{8,16},{16,24},{24,32},{32,40},{40,48},{48,56},{56,64},{64,7... | collective-permute-start | bytes 393224 | tf_op jit(solution)/shard_map/ppermute | solution.py:19
  185.9 2.2 copy-start.3
  220.1 7.7 %collective-permute-start.15 = (bf16[1,256,512]{2,1,0:T(8,128)(2,1)S(1)}, bf16[1,256,512]{2,1,0:T(8,128)(2,1)S(1)}, u32[]{:S(2)}, u32[]{:S(2)}) collective-permute-start(bf16[1,256,512]{2,1,0:T(8,128)(2,1)S(1)} %fusion), channel_id=1, source_target_pairs={{0,128},{128,256},{256,384},{384,0},{1,129},{129,257},{257,385},{3... | collective-permute-start | bytes 786440 | tf_op jit(solution)/shard_map/ppermute | solution.py:19
Sparse Core Ops, SparseCore 0:
  9.4 90.5 all-gather.3
  102.1 82.8 all-gather.5

commit v4 on v3

v4 whole, which is shorter than its diff:
```python
import functools

import jax
import jax.numpy as jnp
from jax import lax
from jax.experimental import pallas as pl
from jax.experimental.pallas import tpu as pltpu
from jax.sharding import PartitionSpec as P

HD = 128


EPS = 1e-05
THETA = 500000.0


def passed_along(value, axis, by):
    length = lax.axis_size(axis)
    return lax.ppermute(value, axis, [(i, (i + by) % length) for i in range(length)])


def turning(pos):
    half = HD // 2
    index = jnp.arange(half, dtype=jnp.float32)
    freq = THETA ** (-2.0 * index / HD)
    angle = pos.astype(jnp.float32)[:, None] * freq[None, :]
    cosine = jnp.cos(angle)
    sine = jnp.sin(angle)
    return jnp.concatenate([cosine, cosine], axis=1), jnp.concatenate([-sine, sine], axis=1)


def passed_on(value, by):
    n_pipe, n_ctx = lax.axis_size("pipe"), lax.axis_size("ctx")
    pairs = [
        (p * n_ctx + c, (p + 1) % n_pipe * n_ctx + (c + by) % n_ctx)
        for p in range(n_pipe)
        for c in range(n_ctx)
    ]
    return lax.ppermute(value, ("pipe", "ctx"), pairs)


def positions_of(stored, stretch_order, block):
    which = stored // block
    slots = jnp.arange(stretch_order.shape[0], dtype=jnp.int32)
    picked = jnp.sum(jnp.where(which[:, None] == slots[None, :], stretch_order[None, :], 0), axis=1)
    return picked * block + stored % block


LOW = -1e20
MASKED = -1e30
MIB = 1024 * 1024
ATTENDED = (3, 4, 5, 6, 7, 8)


def normalise_kernel(spread_ref, out_ref):
    n_tp = spread_ref.shape[0]
    rows = out_ref.shape[0]
    part = out_ref.shape[1] // n_tp
    squares = jnp.zeros((rows, 1), jnp.float32)
    for i in range(n_tp):
        values = spread_ref[i, :rows, :].astype(jnp.float32)
        squares = squares + jnp.sum(values * values, axis=1, keepdims=True)
    factor = lax.rsqrt(squares / out_ref.shape[1] + EPS)
    for i in range(n_tp):
        values = spread_ref[i, :rows, :].astype(jnp.float32)
        terms = spread_ref[i, rows:, :].astype(jnp.float32)
        gain = terms[0:1] + terms[1:2] + terms[2:3]
        out_ref[:, i * part : (i + 1) * part] = (values * factor * gain).astype(out_ref.dtype)


def normalise(spread, rows):
    n_tp, _, part = spread.shape
    vmem = pl.BlockSpec(memory_space=pltpu.VMEM)
    return pl.pallas_call(
        normalise_kernel,
        out_shape=jax.ShapeDtypeStruct((rows, n_tp * part), jnp.bfloat16),
        in_specs=[vmem],
        out_specs=vmem,
        compiler_params=pltpu.CompilerParams(vmem_limit_bytes=16 * MIB),
        cost_estimate=pl.CostEstimate(
            flops=6 * rows * n_tp * part, bytes_accessed=4 * rows * n_tp * part, transcendentals=rows
        ),
    )(spread)


def rotated(raw, cosine, sine):
    half = raw.shape[1] // 2
    swapped = jnp.concatenate([raw[:, half:], raw[:, :half]], axis=1)
    return raw * cosine + swapped * sine


def key_value_kernel(normed_ref, cosine_ref, sine_ref, weights_ref, out_ref):
    total = jnp.dot(normed_ref[...], weights_ref[...], preferred_element_type=jnp.float32)
    key = rotated(total[:, :HD], cosine_ref[...], sine_ref[...])
    out_ref[:, :HD] = key.astype(out_ref.dtype)
    out_ref[:, HD:] = total[:, HD:].astype(out_ref.dtype)


def query_kernel(normed_ref, cosine_ref, sine_ref, weights_ref, keys_values_ref, out_ref):
    total = jnp.dot(normed_ref[...], weights_ref[...], preferred_element_type=jnp.float32)
    cosine, sine = cosine_ref[...], sine_ref[...]
    skip = keys_values_ref.shape[1]
    out_ref[:, :skip] = keys_values_ref[...]
    for at in range(0, total.shape[1], HD):
        raw = total[:, at : at + HD]
        out_ref[:, skip + at : skip + at + HD] = rotated(raw, cosine, sine).astype(out_ref.dtype)


def project(kernel, wide, normed, cosine, sine, weights, *extras):
    rows, width = normed.shape
    vmem = pl.BlockSpec(memory_space=pltpu.VMEM)
    return pl.pallas_call(
        kernel,
        out_shape=jax.ShapeDtypeStruct((rows, wide), jnp.bfloat16),
        in_specs=[vmem] * (4 + len(extras)),
        out_specs=vmem,
        compiler_params=pltpu.CompilerParams(vmem_limit_bytes=16 * MIB),
        cost_estimate=pl.CostEstimate(
            flops=2 * rows * width * weights.shape[1],
            bytes_accessed=2 * width * weights.shape[1],
            transcendentals=0,
        ),
    )(normed, cosine, sine, weights, *extras)


def attended(starts_ref, query_ref, query_pos_ref, state, held):
    peak_ref, total_ref, accum_ref = state
    heads, size, rows = accum_ref.shape
    block = rows // 2
    rate = 1.4426950408889634 / size**0.5
    query_pos = query_pos_ref[...]
    within = lax.broadcasted_iota(jnp.int32, (block, rows), 0)
    key = jnp.concatenate([ref[:, :size] for ref in held], axis=0)
    value = jnp.concatenate([ref[:, size : 2 * size] for ref in held], axis=0).T
    allowed = jnp.concatenate(
        [within + starts_ref[i] <= query_pos for i in range(2 * len(held))], axis=0
    )
    scores = [
        jnp.where(
            allowed,
            lax.dot_general(
                key,
                query_ref[:, (head + 2) * size : (head + 3) * size],
                (((1,), (1,)), ((), ())),
                preferred_element_type=jnp.float32,
            ),
            MASKED,
        )
        for head in range(heads)
    ]
    results = []
    for head in range(heads):
        peak = peak_ref[head]
        new_peak = jnp.maximum(peak, jnp.max(scores[head], axis=0, keepdims=True))
        probs = jnp.exp2((scores[head] - new_peak) * rate)
        fade = jnp.exp2((peak - new_peak) * rate)
        mixed = jnp.dot(value, probs.astype(jnp.bfloat16), preferred_element_type=jnp.float32)
        total = total_ref[head] * fade + jnp.sum(probs, axis=0, keepdims=True)
        results.append((new_peak, total, accum_ref[head] * fade + mixed))
    return results


def attend_kernel(starts_ref, query_ref, query_pos_ref, peak_ref, total_ref, accum_ref, *refs):
    new_peak_ref, new_total_ref, new_accum_ref = refs[-3:]
    results = attended(
        starts_ref, query_ref, query_pos_ref, (peak_ref, total_ref, accum_ref), refs[:-3]
    )
    for head, (peak, total, accum) in enumerate(results):
        new_peak_ref[head] = peak
        new_total_ref[head] = total
        new_accum_ref[head] = accum


def attend(starts, query, query_pos, state, held):
    heads, _, rows = state[2].shape
    keys = rows * len(held)
    vmem = pl.BlockSpec(memory_space=pltpu.VMEM)
    return pl.pallas_call(
        attend_kernel,
        out_shape=[jax.ShapeDtypeStruct(part.shape, part.dtype) for part in state],
        in_specs=[pl.BlockSpec(memory_space=pltpu.SMEM)] + [vmem] * (5 + len(held)),
        out_specs=[vmem] * 3,
        compiler_params=pltpu.CompilerParams(vmem_limit_bytes=16 * MIB),
        cost_estimate=pl.CostEstimate(
            flops=4 * heads * rows * HD * keys,
            bytes_accessed=4 * HD * keys,
            transcendentals=heads * rows * keys,
        ),
    )(starts, query, query_pos, *state, *held)


def finish_kernel(starts_ref, query_ref, query_pos_ref, peak_ref, total_ref, accum_ref, *refs):
    weights_ref, out_ref, context_ref = refs[-3:]
    blocks, depth, packed = weights_ref.shape
    size = accum_ref.shape[1]
    per = out_ref.shape[0] * out_ref.shape[2] // blocks
    share = out_ref.shape[2] // per

    @pl.when(pl.program_id(0) == 0)
    def _():
        results = attended(
            starts_ref, query_ref, query_pos_ref, (peak_ref, total_ref, accum_ref), refs[:-3]
        )
        for head, (_, total, accum) in enumerate(results):
            context = (accum / total).T
            context_ref[:, head * size : (head + 1) * size] = context.astype(context_ref.dtype)

    for at in range(blocks):
        total = None
        for i in range(packed // per):
            term = jnp.dot(
                context_ref[:, i * depth : (i + 1) * depth],
                weights_ref[at, :, i * per : (i + 1) * per],
                preferred_element_type=jnp.float32,
            )
            total = term if total is None else total + term
        column = (at % share) * per
        out_ref[at // share, :, column : column + per] = total.astype(out_ref.dtype)


def finish(starts, query, query_pos, state, held, packed, n_tp):
    heads, size, rows = state[2].shape
    n_ctx, deep, wide = packed.shape
    part = heads * size
    steps = 4
    whole = [query, query_pos, *state, *held]
    return pl.pallas_call(
        finish_kernel,
        grid=(steps,),
        out_shape=jax.ShapeDtypeStruct((n_tp, rows, part), jnp.bfloat16),
        in_specs=[pl.BlockSpec(memory_space=pltpu.SMEM)]
        + [pl.BlockSpec(memory_space=pltpu.VMEM)] * len(whole)
        + [pl.BlockSpec((n_ctx // steps, deep, wide), lambda k: (k, 0, 0))],
        out_specs=pl.BlockSpec((n_tp // steps, rows, part), lambda k: (k, 0, 0)),
        scratch_shapes=[pltpu.VMEM((rows, part), jnp.bfloat16)],
        compiler_params=pltpu.CompilerParams(
            dimension_semantics=("arbitrary",), vmem_limit_bytes=16 * MIB
        ),
        cost_estimate=pl.CostEstimate(
            flops=2 * rows * part * part * n_tp,
            bytes_accessed=4 * part * part * n_tp,
            transcendentals=0,
        ),
    )(starts, *whole, packed)


def shards(section_in, stretch_order, norm_gain, w_query, w_key, w_value, w_out):
    hidden = section_in[0]
    rows, part = hidden.shape
    block = rows // 2
    n_ctx = lax.axis_size("ctx")
    n_tp = lax.axis_size("tp")
    me = lax.axis_index("ctx")
    heads = w_query.shape[2] // HD
    depth = w_query.shape[1]
    span = w_out.shape[2]
    w_mine = jnp.concatenate([w_query[0], w_key[0], w_value[0]], axis=1)
    w_all = lax.all_gather(w_mine, "ctx", axis=0, tiled=True)
    folded = [w_out[0, i * depth : (i + 1) * depth] for i in range(part // span)]
    ahead = jnp.concatenate([hidden, jnp.concatenate(folded, axis=1)], axis=0)
    ahead = passed_along(ahead, "pipe", 1)
    residual = ahead[:rows]
    packed = lax.all_gather(ahead[rows:], "ctx", axis=0, tiled=False)
    gain = norm_gain[0]
    high = lax.reduce_precision(gain, 8, 7)
    middle = lax.reduce_precision(gain - high, 8, 7)
    low = gain - high - middle
    extra = jnp.zeros((16, part), jnp.float32)
    extra = extra.at[0].set(high).at[1].set(middle).at[2].set(low)
    payload = jnp.concatenate([hidden, extra.astype(jnp.bfloat16)], axis=0)
    spread = lax.all_to_all(
        jnp.broadcast_to(payload[None], (n_tp,) + payload.shape), "tp", 0, 0
    )
    normed = normalise(spread, rows)
    local_rows = jnp.arange(rows, dtype=jnp.int32)
    query_pos = positions_of(me * rows + local_rows, stretch_order, block)
    cosine, sine = turning(query_pos)
    query_pos = query_pos[None, :]

    def starts_of(turns):
        stored = jnp.stack(
            [2 * ((me - turn) % n_ctx) + i for turn in turns for i in range(2)]
        )
        return positions_of(stored * block, stretch_order, block)

    keys_values = project(key_value_kernel, 2 * HD, normed, cosine, sine, w_all[:, part:])
    w_all, _ = lax.optimization_barrier((w_all, keys_values))
    own = project(
        query_kernel, 2 * HD + part, normed, cosine, sine, w_all[:, :part], keys_values
    )
    state = (
        jnp.full((heads, 1, rows), LOW, jnp.float32),
        jnp.zeros((heads, 1, rows), jnp.float32),
        jnp.zeros((heads, HD, rows), jnp.float32),
    )
    half = n_ctx // 2
    arrived = {}
    waiting = []
    for turn in range(1, half + 1):
        if turn == 1:
            up, down = passed_on(keys_values, 1), passed_on(keys_values, -1)
        else:
            up = passed_along(up, "ctx", 1)
            if turn < half:
                down = passed_along(down, "ctx", -1)
        if turn == 1:
            own, down = lax.optimization_barrier((own, down))
            own = passed_along(own, "pipe", 1)
            arrived[0] = own
            waiting.append(0)
        if turn in ATTENDED:
            state = attend(
                starts_of(waiting), own, query_pos, state, [arrived[t] for t in waiting]
            )
            up, state = lax.optimization_barrier((up, state))
            waiting = []
        arrived[turn], arrived[-turn] = up, down
        waiting += [turn, -turn] if turn < half else [turn]
    terms = finish(
        starts_of(waiting), own, query_pos, state, [arrived[t] for t in waiting], packed, n_tp
    )
    parts = lax.all_to_all(terms, "tp", 0, 0)
    summed = jnp.sum(parts.astype(jnp.float32), axis=0)
    return (residual.astype(jnp.float32) + summed).astype(jnp.bfloat16)[None]


def solution(mesh):
    in_specs = (
        P("pipe", "ctx", "tp"),
        P(),
        P("pipe", "tp"),
        P("pipe", "ctx", "tp"),
        P("pipe", "ctx", "tp"),
        P("pipe", "ctx", "tp"),
        P("pipe", "tp", "ctx"),
    )
    out_specs = P("pipe", "ctx", "tp")
    return jax.shard_map(shards, mesh=mesh, in_specs=in_specs, out_specs=out_specs, check_vma=False)
```

time: 237 us -> 233 us (0.983)
  Pallas kernels: 21.1 us -> 17 us
    ppermute x16 -> x15, waiting for transfers between devices: 17.8 us -> 29.5 us  [passed_along(): lax.ppermute(value, axis, [(i, (i + by) % length) for i in range(length)])]
    all_gather x1, waiting for transfers between devices: 48.7 us -> 38.7 us  [shards(): w_all = lax.all_gather(w_mine, 'ctx', axis=0, tiled=True)]
    ppermute x0 -> x2, starting transfers between devices: none -> 6.75 us  [passed_on(): return lax.ppermute(value, ('pipe', 'ctx'), pairs)]
    ppermute x16 -> x15, starting transfers between devices: 54.4 us -> 48.3 us  [passed_along(): lax.ppermute(value, axis, [(i, (i + by) % length) for i in range(length)])]
    unnamed x13 -> x14, local copies, waits for them, and re-layouts: 8.71 us -> 5.23 us
    pallas_call x9 -> x6, Pallas kernels: 14.1 us -> 10.7 us  [attend(): pl.pallas_call(attend_kernel, out_shape=[jax.ShapeDtypeStruct(part.shape,...]
    slice x0 -> x3, local copies, waits for them, and re-layouts: none -> 2.92 us  [the longest x1 1.88 us: shards(): w_all[:, part:]]
  transfers between devices with their start and end apart: 19 -> 20, of which waited for: 13 -> 10; matrix products, arithmetic and copies ran while one was open for 3% -> 4% of each run, Pallas kernels for 8% -> 6%
where the time goes in v4:
time: 233 us; the launch traced here: 231 us
  waiting for transfers between devices  90.6 us (39%)
  starting transfers between devices  64.6 us (28%)
  blocking collectives  28.1 us (12%)
  Pallas kernels  17 us (7%)
  between operations  14.1 us (6%)
  local copies, waits for them, and re-layouts  10.9 us (5%)
  other arithmetic  5.86 us (3%)
    ppermute x15, starting transfers between devices, passed_along(): lax.ppermute(value, axis, [(i, (i + by) % length) for i in range(length)])  48.3 us
    all_gather x1, waiting for transfers between devices, shards(): w_all = lax.all_gather(w_mine, 'ctx', axis=0, tiled=True)  38.7 us
    ppermute x15, waiting for transfers between devices, passed_along(): lax.ppermute(value, axis, [(i, (i + by) % length) for i in range(length)])  29.5 us
    all_to_all x1, blocking collectives, shards(): parts = lax.all_to_all(terms, 'tp', 0, 0)  28.1 us
    all_to_all x1, waiting for transfers between devices, shards(): lax.all_to_all(jnp.broadcast_to(payload[None], (n_tp,) + payload.shape),...  22.3 us
    pallas_call x6, Pallas kernels, attend(): pl.pallas_call(attend_kernel, out_shape=[jax.ShapeDtypeStruct(part.shape,...  10.7 us
    all_to_all x1, starting transfers between devices, shards(): lax.all_to_all(jnp.broadcast_to(payload[None], (n_tp,) + payload.shape),...  9.53 us
    ppermute x2, starting transfers between devices, passed_on(): return lax.ppermute(value, ('pipe', 'ctx'), pairs)  6.75 us
  transfers between devices with their start and end apart: 20, of which 10 were waited for; matrix products, arithmetic and copies ran while one was open for 4% of the time, Pallas kernels for 6%

profile of v4, /device:TPU:6, one launch (start us, length us, event | category | flops | bytes accessed | tf_op | source)
XLA Modules:
  0.0 231.3 jit_solution(13216427206363534843)
XLA Ops:
  10.5 1.9 collective-permute-start
  12.4 8.6 %collective-permute-done = bf16[512,512]{1,0:T(8,128)(2,1)S(1)} collective-permute-done((bf16[512,512]{1,0:T(8,128)(2,1)S(1)}, bf16[512,512]{1,0:T(8,128)(2,1)S(1)}, u32[]{:S(2)}, u32[]{:S(2)}) %collective-permute-start) | collective-permute-done | bytes 524320 | tf_op jit(solution)/shard_map/ppermute | solution.py:19
  23.5 9.5 %all-to-all-start = ((bf16[8,272,512]{2,1,0:T(8,128)(2,1)}), bf16[8,272,512]{2,1,0:T(8,128)(2,1)S(1)}, u32[]{:S(2)}, u32[]{:S(2)}) async-start(bf16[8,272,512]{2,1,0:T(8,128)(2,1)} %broadcast_in_dim.112), calls=%async_computation | async-start | bytes 4456448 | tf_op jit(solution)/shard_map/all_to_all | solution.py:271
  35.0 22.3 %all-to-all-done.spread_ref = bf16[8,272,512]{2,1,0:T(8,128)(2,1)S(1)} async-done(((bf16[8,272,512]{2,1,0:T(8,128)(2,1)}), bf16[8,272,512]{2,1,0:T(8,128)(2,1)S(1)}, u32[]{:S(2)}, u32[]{:S(2)}) %all-to-all-start) | async-done | bytes 2228256 | tf_op jit(solution)/shard_map/all_to_all | solution.py:271
  61.3 38.7 %all-gather.4.cloned.1.call-done = bf16[4096,768]{1,0:T(8,128)(2,1)} async-done(((bf16[256,768]{1,0:T(8,128)(2,1)}), bf16[4096,768]{1,0:T(8,128)(2,1)}) %all-gather.4.cloned.1.call-update) | async-done | bytes 6291472 | tf_op jit(solution)/shard_map/all_gather | solution.py:258
  102.8 1.9 collective-permute-start.1
  104.7 4.8 %collective-permute-start.3 = (bf16[256,256]{1,0:T(8,128)(2,1)S(1)}, bf16[256,256]{1,0:T(8,128)(2,1)S(1)}, u32[]{:S(2)}, u32[]{:S(2)}) collective-permute-start(bf16[256,256]{1,0:T(8,128)(2,1)S(1)} %shard_map.74.keys_values_ref), channel_id=1, source_target_pairs={{0,136},{8,144},{16,152},{24,160},{32,168},{40,176},{48,184},{56,1... | collective-permute-start | bytes 393224 | tf_op jit(solution)/shard_map/ppermute | solution.py:39
  111.3 2.2 collective-permute-start.2
  113.5 3.5 %collective-permute-start.4 = (bf16[256,256]{1,0:T(8,128)(2,1)S(1)}, bf16[256,256]{1,0:T(8,128)(2,1)S(1)}, u32[]{:S(2)}, u32[]{:S(2)}) collective-permute-start(bf16[256,256]{1,0:T(8,128)(2,1)S(1)} %collective-permute-done.3.refs_1_), channel_id=1, source_target_pairs={{0,8},{8,16},{16,24},{24,32},{32,40},{40,48},{48,56},{56,64},{64,7... | collective-permute-start | bytes 393224 | tf_op jit(solution)/shard_map/ppermute | solution.py:19
  117.1 3.5 %collective-permute-start.6 = (bf16[256,256]{1,0:T(8,128)(2,1)S(1)}, bf16[256,256]{1,0:T(8,128)(2,1)S(1)}, u32[]{:S(2)}, u32[]{:S(2)}) collective-permute-start(bf16[256,256]{1,0:T(8,128)(2,1)S(1)} %collective-permute-done.1.refs_2_), channel_id=1, source_target_pairs={{0,120},{8,0},{16,8},{24,16},{32,24},{40,32},{48,40},{56,48},{64,5... | collective-permute-start | bytes 393224 | tf_op jit(solution)/shard_map/ppermute | solution.py:19
  120.6 4.4 %collective-permute-done.4.refs_3_ = bf16[256,256]{1,0:T(8,128)(2,1)S(1)} collective-permute-done((bf16[256,256]{1,0:T(8,128)(2,1)S(1)}, bf16[256,256]{1,0:T(8,128)(2,1)S(1)}, u32[]{:S(2)}, u32[]{:S(2)}) %collective-permute-start.4) | collective-permute-done | bytes 131104 | tf_op jit(solution)/shard_map/ppermute | solution.py:19
  125.0 1.9 collective-permute-start.5
  127.0 5.1 %collective-permute-start.8 = (bf16[256,256]{1,0:T(8,128)(2,1)S(1)}, bf16[256,256]{1,0:T(8,128)(2,1)S(1)}, u32[]{:S(2)}, u32[]{:S(2)}) collective-permute-start(bf16[256,256]{1,0:T(8,128)(2,1)S(1)} %collective-permute-done.6.refs_4_), channel_id=1, source_target_pairs={{0,120},{8,0},{16,8},{24,16},{32,24},{40,32},{48,40},{56,48},{64,5... | collective-permute-start | bytes 393224 | tf_op jit(solution)/shard_map/ppermute | solution.py:19
  132.2 2.7 %shard_map.76 = (f32[4,1,256]{2,1,0:T(1,128)S(1)}, f32[4,1,256]{2,1,0:T(1,128)S(1)}, f32[4,128,256]{2,1,0:T(8,128)S(1)}) custom-call(s32[10]{0:T(128)S(1)} %fusion.9.starts_ref, bf16[256,768]{1,0:T(8,128)(2,1)S(1)} %collective-permute-done.2.query_ref.refs_0_, s32[1,256]{1,0:T(1,128)S(1)} %fusion.2.query_pos_ref, ...), custom_call_target="tpu_custom_call" | custom-call | flops 671088640 | bytes 655360 | tf_op jit(solution)/shard_map/pallas_call | solution.py:178
  134.9 2.1 collective-permute-done.5.refs_0_
  137.0 1.9 collective-permute-start.7
  138.9 5.1 %collective-permute-start.10 = (bf16[256,256]{1,0:T(8,128)(2,1)S(1)}, bf16[256,256]{1,0:T(8,128)(2,1)S(1)}, u32[]{:S(2)}, u32[]{:S(2)}) collective-permute-start(bf16[256,256]{1,0:T(8,128)(2,1)S(1)} %collective-permute-done.8.refs_1_), channel_id=1, source_target_pairs={{0,120},{8,0},{16,8},{24,16},{32,24},{40,32},{48,40},{56,48},{64,5... | collective-permute-start | bytes 393224 | tf_op jit(solution)/shard_map/ppermute | solution.py:19
  145.7 2.1 collective-permute-done.7.refs_0_
  147.7 1.9 collective-permute-start.9
  149.7 5.1 %collective-permute-start.12 = (bf16[256,256]{1,0:T(8,128)(2,1)S(1)}, bf16[256,256]{1,0:T(8,128)(2,1)S(1)}, u32[]{:S(2)}, u32[]{:S(2)}) collective-permute-start(bf16[256,256]{1,0:T(8,128)(2,1)S(1)} %collective-permute-done.10.refs_1_), channel_id=1, source_target_pairs={{0,120},{8,0},{16,8},{24,16},{32,24},{40,32},{48,40},{56,48},{64,5... | collective-permute-start | bytes 393224 | tf_op jit(solution)/shard_map/ppermute | solution.py:19
  156.4 2.8 %collective-permute-done.9.refs_0_ = bf16[256,256]{1,0:T(8,128)(2,1)S(1)} collective-permute-done((bf16[256,256]{1,0:T(8,128)(2,1)S(1)}, bf16[256,256]{1,0:T(8,128)(2,1)S(1)}, u32[]{:S(2)}, u32[]{:S(2)}) %collective-permute-start.9) | collective-permute-done | bytes 131104 | tf_op jit(solution)/shard_map/ppermute | solution.py:19
  159.3 1.9 collective-permute-start.11
  161.3 5.1 %collective-permute-start.14 = (bf16[256,256]{1,0:T(8,128)(2,1)S(1)}, bf16[256,256]{1,0:T(8,128)(2,1)S(1)}, u32[]{:S(2)}, u32[]{:S(2)}) collective-permute-start(bf16[256,256]{1,0:T(8,128)(2,1)S(1)} %collective-permute-done.12.refs_1_), channel_id=1, source_target_pairs={{0,120},{8,0},{16,8},{24,16},{32,24},{40,32},{48,40},{56,48},{64,5... | collective-permute-start | bytes 393224 | tf_op jit(solution)/shard_map/ppermute | solution.py:19
  168.0 3.1 %collective-permute-done.11.refs_0_ = bf16[256,256]{1,0:T(8,128)(2,1)S(1)} collective-permute-done((bf16[256,256]{1,0:T(8,128)(2,1)S(1)}, bf16[256,256]{1,0:T(8,128)(2,1)S(1)}, u32[]{:S(2)}, u32[]{:S(2)}) %collective-permute-start.11) | collective-permute-done | bytes 131104 | tf_op jit(solution)/shard_map/ppermute | solution.py:19
  171.1 1.9 collective-permute-start.13
  173.2 5.1 %collective-permute-start.16 = (bf16[256,256]{1,0:T(8,128)(2,1)S(1)}, bf16[256,256]{1,0:T(8,128)(2,1)S(1)}, u32[]{:S(2)}, u32[]{:S(2)}) collective-permute-start(bf16[256,256]{1,0:T(8,128)(2,1)S(1)} %collective-permute-done.14.refs_1_), channel_id=1, source_target_pairs={{0,120},{8,0},{16,8},{24,16},{32,24},{40,32},{48,40},{56,48},{64,5... | collective-permute-start | bytes 393224 | tf_op jit(solution)/shard_map/ppermute | solution.py:19
  180.0 1.9 collective-permute-done.13.refs_0_
  181.9 1.9 collective-permute-start.15
  185.4 4.5 %collective-permute-done.15.refs_0_ = bf16[256,256]{1,0:T(8,128)(2,1)S(1)} collective-permute-done((bf16[256,256]{1,0:T(8,128)(2,1)S(1)}, bf16[256,256]{1,0:T(8,128)(2,1)S(1)}, u32[]{:S(2)}, u32[]{:S(2)}) %collective-permute-start.15) | collective-permute-done | bytes 131104 | tf_op jit(solution)/shard_map/ppermute | solution.py:19
  189.9 2.2 copy-done.2
  192.1 3.1 %shard_map.82 = bf16[8,256,512]{2,1,0:T(8,128)(2,1)S(1)} custom-call(s32[2]{0:T(128)S(1)} %fusion.8.starts_ref, bf16[256,768]{1,0:T(8,128)(2,1)S(1)} %collective-permute-done.2.query_ref.refs_0_, s32[1,256]{1,0:T(1,128)S(1)} %fusion.2.query_pos_ref, f32[4,1,256]{2,1,0:T(1,128)S(1)} %get-tuple-element.127.peak_ref, ...), custom_call_target="tpu_custom_call" | custom-call | flops 1073741824 | bytes 8388608 | tf_op jit(solution)/shard_map/pallas_call | solution.py:227
  195.2 28.1 %all_to_all.10 = bf16[8,256,512]{2,1,0:T(8,128)(2,1)S(1)} all-to-all(bf16[8,256,512]{2,1,0:T(8,128)(2,1)S(1)} %shard_map.82), channel_id=1, replica_groups=mesh['pipe'=4,'ctx'=16,'tp'=8] {'tp'}, dimensions={0} | all-to-all | bytes 4194304 | tf_op jit(solution)/shard_map/all_to_all | solution.py:322
  (75 shorter events, 25.9 us)
Async XLA Ops:
  6.5 15.3 %copy-start.4 = (bf16[1,256,512]{2,1,0:T(8,128)(2,1)S(1)}, bf16[1,256,512]{2,1,0:T(8,128)(2,1)}, u32[]{:S(2)}) copy-start(bf16[1,256,512]{2,1,0:T(8,128)(2,1)} %param.13) | copy-start | bytes 786436
  6.5 15.2 %copy-start.5 = (f32[1,512]{1,0:T(1,128)S(1)}, f32[1,512]{1,0:T(1,128)}, u32[]{:S(2)}) copy-start(f32[1,512]{1,0:T(1,128)} %param.15) | copy-start | bytes 6148
  6.5 93.5 %all-gather.4.cloned.1.call-start = ((), (), s32[]{:S(2)}) async-start(), calls=%async_computation.2 | async-start | bytes 6684672 | tf_op jit(solution)/shard_map/all_gather | solution.py:258
  8.5 181.5 %all-gather.6.cloned.1.call-start = ((), (), s32[]{:S(2)}) async-start(), calls=%async_computation.3 | async-start | bytes 4456448 | tf_op jit(solution)/shard_map/all_gather | solution.py:263
  10.5 10.5 %collective-permute-start = (bf16[512,512]{1,0:T(8,128)(2,1)S(1)}, bf16[512,512]{1,0:T(8,128)(2,1)S(1)}, u32[]{:S(2)}, u32[]{:S(2)}) collective-permute-start(bf16[512,512]{1,0:T(8,128)(2,1)S(1)} %maximum_maximum_fusion), channel_id=1, source_target_pairs={{0,128},{128,256},{256,384},{384,0},{1,129},{129,257},{257,385},{3... | collective-permute-start | bytes 1572872 | tf_op jit(solution)/shard_map/ppermute | solution.py:19
  23.5 10.2 %copy-start.6 = (s32[32]{0:T(128)S(1)}, s32[32]{0:T(128)}, u32[]{:S(2)}) copy-start(s32[32]{0:T(128)} %param.14) | copy-start | bytes 388
  23.5 33.8 %all-to-all-start = ((bf16[8,272,512]{2,1,0:T(8,128)(2,1)}), bf16[8,272,512]{2,1,0:T(8,128)(2,1)S(1)}, u32[]{:S(2)}, u32[]{:S(2)}) async-start(bf16[8,272,512]{2,1,0:T(8,128)(2,1)} %broadcast_in_dim.112), calls=%async_computation | async-start | bytes 4456448 | tf_op jit(solution)/shard_map/all_to_all | solution.py:271
  57.3 1.4 copy-start
  58.7 1.6 copy-start.1
  100.1 9.5 %copy-start.3 = (bf16[4096,768]{1,0:T(8,128)(2,1)S(1)}, bf16[4096,768]{1,0:T(8,128)(2,1)}, u32[]{:S(2)}) copy-start(bf16[4096,768]{1,0:T(8,128)(2,1)} %all-gather.4.cloned.1.call-done) | copy-start | bytes 18874372
  102.8 8.5 %collective-permute-start.1 = (bf16[256,256]{1,0:T(8,128)(2,1)S(1)}, bf16[256,256]{1,0:T(8,128)(2,1)S(1)}, u32[]{:S(2)}, u32[]{:S(2)}) collective-permute-start(bf16[256,256]{1,0:T(8,128)(2,1)S(1)} %shard_map.74.keys_values_ref), channel_id=1, source_target_pairs={{0,248},{8,128},{16,136},{24,144},{32,152},{40,160},{48,168},{56,1... | collective-permute-start | bytes 393224 | tf_op jit(solution)/shard_map/ppermute | solution.py:39
  104.7 8.8 %collective-permute-start.3 = (bf16[256,256]{1,0:T(8,128)(2,1)S(1)}, bf16[256,256]{1,0:T(8,128)(2,1)S(1)}, u32[]{:S(2)}, u32[]{:S(2)}) collective-permute-start(bf16[256,256]{1,0:T(8,128)(2,1)S(1)} %shard_map.74.keys_values_ref), channel_id=1, source_target_pairs={{0,136},{8,144},{16,152},{24,160},{32,168},{40,176},{48,184},{56,1... | collective-permute-start | bytes 393224 | tf_op jit(solution)/shard_map/ppermute | solution.py:39
  111.3 20.8 %collective-permute-start.2 = (bf16[256,768]{1,0:T(8,128)(2,1)S(1)}, bf16[256,768]{1,0:T(8,128)(2,1)S(1)}, u32[]{:S(2)}, u32[]{:S(2)}) collective-permute-start(bf16[256,768]{1,0:T(8,128)(2,1)S(1)} %shard_map.75), channel_id=1, source_target_pairs={{0,128},{128,256},{256,384},{384,0},{1,129},{129,257},{257,385},{3... | collective-permute-start | bytes 1179656 | tf_op jit(solution)/shard_map/ppermute | solution.py:19
  113.5 11.5 %collective-permute-start.4 = (bf16[256,256]{1,0:T(8,128)(2,1)S(1)}, bf16[256,256]{1,0:T(8,128)(2,1)S(1)}, u32[]{:S(2)}, u32[]{:S(2)}) collective-permute-start(bf16[256,256]{1,0:T(8,128)(2,1)S(1)} %collective-permute-done.3.refs_1_), channel_id=1, source_target_pairs={{0,8},{8,16},{16,24},{24,32},{32,40},{40,48},{48,56},{56,64},{64,7... | collective-permute-start | bytes 393224 | tf_op jit(solution)/shard_map/ppermute | solution.py:19
  117.1 9.9 %collective-permute-start.6 = (bf16[256,256]{1,0:T(8,128)(2,1)S(1)}, bf16[256,256]{1,0:T(8,128)(2,1)S(1)}, u32[]{:S(2)}, u32[]{:S(2)}) collective-permute-start(bf16[256,256]{1,0:T(8,128)(2,1)S(1)} %collective-permute-done.1.refs_2_), channel_id=1, source_target_pairs={{0,120},{8,0},{16,8},{24,16},{32,24},{40,32},{48,40},{56,48},{64,5... | collective-permute-start | bytes 393224 | tf_op jit(solution)/shard_map/ppermute | solution.py:19
  125.0 12.0 %collective-permute-start.5 = (bf16[256,256]{1,0:T(8,128)(2,1)S(1)}, bf16[256,256]{1,0:T(8,128)(2,1)S(1)}, u32[]{:S(2)}, u32[]{:S(2)}) collective-permute-start(bf16[256,256]{1,0:T(8,128)(2,1)S(1)} %collective-permute-done.4.refs_3_), channel_id=1, source_target_pairs={{0,8},{8,16},{16,24},{24,32},{32,40},{40,48},{48,56},{56,64},{64,7... | collective-permute-start | bytes 393224 | tf_op jit(solution)/shard_map/ppermute | solution.py:19
  127.0 12.0 %collective-permute-start.8 = (bf16[256,256]{1,0:T(8,128)(2,1)S(1)}, bf16[256,256]{1,0:T(8,128)(2,1)S(1)}, u32[]{:S(2)}, u32[]{:S(2)}) collective-permute-start(bf16[256,256]{1,0:T(8,128)(2,1)S(1)} %collective-permute-done.6.refs_4_), channel_id=1, source_target_pairs={{0,120},{8,0},{16,8},{24,16},{32,24},{40,32},{48,40},{56,48},{64,5... | collective-permute-start | bytes 393224 | tf_op jit(solution)/shard_map/ppermute | solution.py:19
  137.0 10.7 %collective-permute-start.7 = (bf16[256,256]{1,0:T(8,128)(2,1)S(1)}, bf16[256,256]{1,0:T(8,128)(2,1)S(1)}, u32[]{:S(2)}, u32[]{:S(2)}) collective-permute-start(bf16[256,256]{1,0:T(8,128)(2,1)S(1)} %collective-permute-done.5.refs_0_), channel_id=1, source_target_pairs={{0,8},{8,16},{16,24},{24,32},{32,40},{40,48},{48,56},{56,64},{64,7... | collective-permute-start | bytes 393224 | tf_op jit(solution)/shard_map/ppermute | solution.py:19
  138.9 10.8 %collective-permute-start.10 = (bf16[256,256]{1,0:T(8,128)(2,1)S(1)}, bf16[256,256]{1,0:T(8,128)(2,1)S(1)}, u32[]{:S(2)}, u32[]{:S(2)}) collective-permute-start(bf16[256,256]{1,0:T(8,128)(2,1)S(1)} %collective-permute-done.8.refs_1_), channel_id=1, source_target_pairs={{0,120},{8,0},{16,8},{24,16},{32,24},{40,32},{48,40},{56,48},{64,5... | collective-permute-start | bytes 393224 | tf_op jit(solution)/shard_map/ppermute | solution.py:19
  147.7 11.5 %collective-permute-start.9 = (bf16[256,256]{1,0:T(8,128)(2,1)S(1)}, bf16[256,256]{1,0:T(8,128)(2,1)S(1)}, u32[]{:S(2)}, u32[]{:S(2)}) collective-permute-start(bf16[256,256]{1,0:T(8,128)(2,1)S(1)} %collective-permute-done.7.refs_0_), channel_id=1, source_target_pairs={{0,8},{8,16},{16,24},{24,32},{32,40},{40,48},{48,56},{56,64},{64,7... | collective-permute-start | bytes 393224 | tf_op jit(solution)/shard_map/ppermute | solution.py:19
  149.7 11.6 %collective-permute-start.12 = (bf16[256,256]{1,0:T(8,128)(2,1)S(1)}, bf16[256,256]{1,0:T(8,128)(2,1)S(1)}, u32[]{:S(2)}, u32[]{:S(2)}) collective-permute-start(bf16[256,256]{1,0:T(8,128)(2,1)S(1)} %collective-permute-done.10.refs_1_), channel_id=1, source_target_pairs={{0,120},{8,0},{16,8},{24,16},{32,24},{40,32},{48,40},{56,48},{64,5... | collective-permute-start | bytes 393224 | tf_op jit(solution)/shard_map/ppermute | solution.py:19
  159.3 11.8 %collective-permute-start.11 = (bf16[256,256]{1,0:T(8,128)(2,1)S(1)}, bf16[256,256]{1,0:T(8,128)(2,1)S(1)}, u32[]{:S(2)}, u32[]{:S(2)}) collective-permute-start(bf16[256,256]{1,0:T(8,128)(2,1)S(1)} %collective-permute-done.9.refs_0_), channel_id=1, source_target_pairs={{0,8},{8,16},{16,24},{24,32},{32,40},{40,48},{48,56},{56,64},{64,7... | collective-permute-start | bytes 393224 | tf_op jit(solution)/shard_map/ppermute | solution.py:19
  161.3 11.9 %collective-permute-start.14 = (bf16[256,256]{1,0:T(8,128)(2,1)S(1)}, bf16[256,256]{1,0:T(8,128)(2,1)S(1)}, u32[]{:S(2)}, u32[]{:S(2)}) collective-permute-start(bf16[256,256]{1,0:T(8,128)(2,1)S(1)} %collective-permute-done.12.refs_1_), channel_id=1, source_target_pairs={{0,120},{8,0},{16,8},{24,16},{32,24},{40,32},{48,40},{56,48},{64,5... | collective-permute-start | bytes 393224 | tf_op jit(solution)/shard_map/ppermute | solution.py:19
  171.1 10.7 %collective-permute-start.13 = (bf16[256,256]{1,0:T(8,128)(2,1)S(1)}, bf16[256,256]{1,0:T(8,128)(2,1)S(1)}, u32[]{:S(2)}, u32[]{:S(2)}) collective-permute-start(bf16[256,256]{1,0:T(8,128)(2,1)S(1)} %collective-permute-done.11.refs_0_), channel_id=1, source_target_pairs={{0,8},{8,16},{16,24},{24,32},{32,40},{40,48},{48,56},{56,64},{64,7... | collective-permute-start | bytes 393224 | tf_op jit(solution)/shard_map/ppermute | solution.py:19
  173.2 10.6 %collective-permute-start.16 = (bf16[256,256]{1,0:T(8,128)(2,1)S(1)}, bf16[256,256]{1,0:T(8,128)(2,1)S(1)}, u32[]{:S(2)}, u32[]{:S(2)}) collective-permute-start(bf16[256,256]{1,0:T(8,128)(2,1)S(1)} %collective-permute-done.14.refs_1_), channel_id=1, source_target_pairs={{0,120},{8,0},{16,8},{24,16},{32,24},{40,32},{48,40},{56,48},{64,5... | collective-permute-start | bytes 393224 | tf_op jit(solution)/shard_map/ppermute | solution.py:19
  181.9 8.1 %collective-permute-start.15 = (bf16[256,256]{1,0:T(8,128)(2,1)S(1)}, bf16[256,256]{1,0:T(8,128)(2,1)S(1)}, u32[]{:S(2)}, u32[]{:S(2)}) collective-permute-start(bf16[256,256]{1,0:T(8,128)(2,1)S(1)} %collective-permute-done.13.refs_0_), channel_id=1, source_target_pairs={{0,8},{8,16},{16,24},{24,32},{32,40},{40,48},{48,56},{56,64},{64,7... | collective-permute-start | bytes 393224 | tf_op jit(solution)/shard_map/ppermute | solution.py:19
  189.9 2.2 copy-start.2
Sparse Core Ops, SparseCore 0:
  9.4 90.5 all-gather.3
  102.1 86.1 all-gather.5

commit v5 on v4

--- a/solution.py
+++ b/solution.py
@@ -29,13 +29,17 @@
     return jnp.concatenate([cosine, cosine], axis=1), jnp.concatenate([-sine, sine], axis=1)
 
 
-def passed_on(value, by):
+def way(pipe):
+    return 1 - 2 * (pipe % 2)
+
+
+def round_ctx(value, by, hop):
     n_pipe, n_ctx = lax.axis_size("pipe"), lax.axis_size("ctx")
-    pairs = [
-        (p * n_ctx + c, (p + 1) % n_pipe * n_ctx + (c + by) % n_ctx)
-        for p in range(n_pipe)
-        for c in range(n_ctx)
-    ]
+    pairs = []
+    for pipe in range(n_pipe):
+        to = (pipe + hop) % n_pipe
+        for ctx in range(n_ctx):
+            pairs.append((pipe * n_ctx + ctx, to * n_ctx + (ctx + by * way(to)) % n_ctx))
     return lax.ppermute(value, ("pipe", "ctx"), pairs)
 
 
@@ -277,9 +281,11 @@
     cosine, sine = turning(query_pos)
     query_pos = query_pos[None, :]
 
+    sense = way(lax.axis_index("pipe"))
+
     def starts_of(turns):
         stored = jnp.stack(
-            [2 * ((me - turn) % n_ctx) + i for turn in turns for i in range(2)]
+            [2 * ((me - turn * sense) % n_ctx) + i for turn in turns for i in range(2)]
         )
         return positions_of(stored * block, stretch_order, block)
 
@@ -298,11 +304,11 @@
     waiting = []
     for turn in range(1, half + 1):
         if turn == 1:
-            up, down = passed_on(keys_values, 1), passed_on(keys_values, -1)
+            up, down = round_ctx(keys_values, 1, 1), round_ctx(keys_values, -1, 1)
         else:
-            up = passed_along(up, "ctx", 1)
+            up = round_ctx(up, 1, 0)
             if turn < half:
-                down = passed_along(down, "ctx", -1)
+                down = round_ctx(down, -1, 0)
         if turn == 1:
             own, down = lax.optimization_barrier((own, down))
             own = passed_along(own, "pipe", 1)

time: 233 us -> 233 us (level)
  local copies, waits for them, and re-layouts: 10.9 us -> 14.6 us
  waiting for transfers between devices: 90.6 us -> 87.8 us
    ppermute x2 -> x15, starting transfers between devices: 6.75 us -> 51.7 us  [round_ctx(): return lax.ppermute(value, ('pipe', 'ctx'), pairs)]
    ppermute x15 -> x2, starting transfers between devices: 48.3 us -> 3.84 us  [passed_along(): lax.ppermute(value, axis, [(i, (i + by) % length) for i in range(length)])]
    ppermute x15 -> x2, waiting for transfers between devices: 29.5 us -> 8.57 us  [passed_along(): lax.ppermute(value, axis, [(i, (i + by) % length) for i in range(length)])]
    ppermute x2 -> x15, waiting for transfers between devices: 0.01 us -> 18.8 us  [round_ctx(): return lax.ppermute(value, ('pipe', 'ctx'), pairs)]
    unnamed x14 -> x16, local copies, waits for them, and re-layouts: 5.23 us -> 6.85 us
  transfers between devices with their start and end apart: 20 -> 20, of which waited for: 10 -> 10; matrix products, arithmetic and copies ran while one was open for 4% -> 5% of each run, Pallas kernels for 6% -> 6%
where the time goes in v5:
time: 233 us; the launch traced here: 231 us
  waiting for transfers between devices  87.8 us (38%)
  starting transfers between devices  65.1 us (28%)
  blocking collectives  26.9 us (12%)
  Pallas kernels  17 us (7%)
  local copies, waits for them, and re-layouts  14.6 us (6%)
  between operations  14.1 us (6%)
  other arithmetic  5.8 us (2%)
    ppermute x15, starting transfers between devices, round_ctx(): return lax.ppermute(value, ('pipe', 'ctx'), pairs)  51.7 us
    all_gather x1, waiting for transfers between devices, shards(): w_all = lax.all_gather(w_mine, 'ctx', axis=0, tiled=True)  37.6 us
    all_to_all x1, blocking collectives, shards(): parts = lax.all_to_all(terms, 'tp', 0, 0)  26.9 us
    all_to_all x1, waiting for transfers between devices, shards(): lax.all_to_all(jnp.broadcast_to(payload[None], (n_tp,) + payload.shape),...  22.9 us
    ppermute x15, waiting for transfers between devices, round_ctx(): return lax.ppermute(value, ('pipe', 'ctx'), pairs)  18.8 us
    pallas_call x6, Pallas kernels, attend(): pl.pallas_call(attend_kernel, out_shape=[jax.ShapeDtypeStruct(part.shape,...  10.7 us
    all_to_all x1, starting transfers between devices, shards(): lax.all_to_all(jnp.broadcast_to(payload[None], (n_tp,) + payload.shape),...  9.51 us
    ppermute x2, waiting for transfers between devices, passed_along(): lax.ppermute(value, axis, [(i, (i + by) % length) for i in range(length)])  8.57 us
  transfers between devices with their start and end apart: 20, of which 10 were waited for; matrix products, arithmetic and copies ran while one was open for 5% of the time, Pallas kernels for 6%

profile of v5, /device:TPU:6, one launch (start us, length us, event | category | flops | bytes accessed | tf_op | source)
XLA Modules:
  0.0 231.3 jit_solution(4962306658171248645)
XLA Ops:
  6.5 1.8 pad_maximum_fusion
  10.4 1.9 collective-permute-start
  12.4 8.6 %collective-permute-done = bf16[512,512]{1,0:T(8,128)(2,1)S(1)} collective-permute-done((bf16[512,512]{1,0:T(8,128)(2,1)S(1)}, bf16[512,512]{1,0:T(8,128)(2,1)S(1)}, u32[]{:S(2)}, u32[]{:S(2)}) %collective-permute-start) | collective-permute-done | bytes 524320 | tf_op jit(solution)/shard_map/ppermute | solution.py:19
  24.3 9.5 %all-to-all-start = ((bf16[8,272,512]{2,1,0:T(8,128)(2,1)}), bf16[8,272,512]{2,1,0:T(8,128)(2,1)S(1)}, u32[]{:S(2)}, u32[]{:S(2)}) async-start(bf16[8,272,512]{2,1,0:T(8,128)(2,1)} %broadcast_in_dim.112), calls=%async_computation | async-start | bytes 4456448 | tf_op jit(solution)/shard_map/all_to_all | solution.py:275
  35.2 22.9 %all-to-all-done.spread_ref = bf16[8,272,512]{2,1,0:T(8,128)(2,1)S(1)} async-done(((bf16[8,272,512]{2,1,0:T(8,128)(2,1)}), bf16[8,272,512]{2,1,0:T(8,128)(2,1)S(1)}, u32[]{:S(2)}, u32[]{:S(2)}) %all-to-all-start) | async-done | bytes 2228256 | tf_op jit(solution)/shard_map/all_to_all | solution.py:275
  62.2 37.6 %all-gather.4.cloned.1.call-done = bf16[4096,768]{1,0:T(8,128)(2,1)} async-done(((bf16[256,768]{1,0:T(8,128)(2,1)}), bf16[4096,768]{1,0:T(8,128)(2,1)}) %all-gather.4.cloned.1.call-update) | async-done | bytes 6291472 | tf_op jit(solution)/shard_map/all_gather | solution.py:262
  102.3 1.9 collective-permute-start.1
  104.3 5.6 %collective-permute-start.3 = (bf16[256,256]{1,0:T(8,128)(2,1)S(1)}, bf16[256,256]{1,0:T(8,128)(2,1)S(1)}, u32[]{:S(2)}, u32[]{:S(2)}) collective-permute-start(bf16[256,256]{1,0:T(8,128)(2,1)S(1)} %shard_map.74.keys_values_ref), channel_id=1, source_target_pairs={{0,248},{8,128},{16,136},{24,144},{32,152},{40,160},{48,168},{56,1... | collective-permute-start | bytes 393224 | tf_op jit(solution)/shard_map/ppermute | solution.py:43
  109.9 2.5 %slice.66.weights_ref = bf16[4096,512]{1,0:T(8,128)(2,1)S(1)} slice(bf16[4096,768]{1,0:T(8,128)(2,1)} %all-gather.4.cloned.1.call-done), slice={[0:4096], [0:512]} | slice | bytes 8388608 | tf_op jit(solution)/shard_map/slice | solution.py:295
  113.8 1.9 collective-permute-start.2
  115.9 3.2 %collective-permute-start.4 = (bf16[256,256]{1,0:T(8,128)(2,1)S(1)}, bf16[256,256]{1,0:T(8,128)(2,1)S(1)}, u32[]{:S(2)}, u32[]{:S(2)}) collective-permute-start(bf16[256,256]{1,0:T(8,128)(2,1)S(1)} %collective-permute-done.3.refs_1_), channel_id=1, source_target_pairs={{0,8},{8,16},{16,24},{24,32},{32,40},{40,48},{48,56},{56,64},{64,7... | collective-permute-start | bytes 393224 | tf_op jit(solution)/shard_map/ppermute | solution.py:43
  119.2 3.9 %collective-permute-start.6 = (bf16[256,256]{1,0:T(8,128)(2,1)S(1)}, bf16[256,256]{1,0:T(8,128)(2,1)S(1)}, u32[]{:S(2)}, u32[]{:S(2)}) collective-permute-start(bf16[256,256]{1,0:T(8,128)(2,1)S(1)} %collective-permute-done.1.refs_2_), channel_id=1, source_target_pairs={{0,120},{8,0},{16,8},{24,16},{32,24},{40,32},{48,40},{56,48},{64,5... | collective-permute-start | bytes 393224 | tf_op jit(solution)/shard_map/ppermute | solution.py:43
  123.2 3.2 %collective-permute-done.4.refs_3_ = bf16[256,256]{1,0:T(8,128)(2,1)S(1)} collective-permute-done((bf16[256,256]{1,0:T(8,128)(2,1)S(1)}, bf16[256,256]{1,0:T(8,128)(2,1)S(1)}, u32[]{:S(2)}, u32[]{:S(2)}) %collective-permute-start.4) | collective-permute-done | bytes 131104 | tf_op jit(solution)/shard_map/ppermute | solution.py:43
  126.4 1.9 collective-permute-start.5
  128.6 5.1 %collective-permute-start.8 = (bf16[256,256]{1,0:T(8,128)(2,1)S(1)}, bf16[256,256]{1,0:T(8,128)(2,1)S(1)}, u32[]{:S(2)}, u32[]{:S(2)}) collective-permute-start(bf16[256,256]{1,0:T(8,128)(2,1)S(1)} %collective-permute-done.6.refs_4_), channel_id=1, source_target_pairs={{0,120},{8,0},{16,8},{24,16},{32,24},{40,32},{48,40},{56,48},{64,5... | collective-permute-start | bytes 393224 | tf_op jit(solution)/shard_map/ppermute | solution.py:43
  133.8 2.7 %shard_map.76 = (f32[4,1,256]{2,1,0:T(1,128)S(1)}, f32[4,1,256]{2,1,0:T(1,128)S(1)}, f32[4,128,256]{2,1,0:T(8,128)S(1)}) custom-call(s32[10]{0:T(128)S(1)} %fusion.9.starts_ref, bf16[256,768]{1,0:T(8,128)(2,1)S(1)} %collective-permute-done.2.query_ref.refs_0_, s32[1,256]{1,0:T(1,128)S(1)} %fusion.2.query_pos_ref, ...), custom_call_target="tpu_custom_call" | custom-call | flops 671088640 | bytes 655360 | tf_op jit(solution)/shard_map/pallas_call | solution.py:182
  137.7 1.9 collective-permute-start.7
  139.7 5.1 %collective-permute-start.10 = (bf16[256,256]{1,0:T(8,128)(2,1)S(1)}, bf16[256,256]{1,0:T(8,128)(2,1)S(1)}, u32[]{:S(2)}, u32[]{:S(2)}) collective-permute-start(bf16[256,256]{1,0:T(8,128)(2,1)S(1)} %collective-permute-done.8.refs_1_), channel_id=1, source_target_pairs={{0,120},{8,0},{16,8},{24,16},{32,24},{40,32},{48,40},{56,48},{64,5... | collective-permute-start | bytes 393224 | tf_op jit(solution)/shard_map/ppermute | solution.py:43
  146.4 2.7 %collective-permute-done.7.refs_0_ = bf16[256,256]{1,0:T(8,128)(2,1)S(1)} collective-permute-done((bf16[256,256]{1,0:T(8,128)(2,1)S(1)}, bf16[256,256]{1,0:T(8,128)(2,1)S(1)}, u32[]{:S(2)}, u32[]{:S(2)}) %collective-permute-start.7) | collective-permute-done | bytes 131104 | tf_op jit(solution)/shard_map/ppermute | solution.py:43
  149.2 1.9 collective-permute-start.9
  151.1 5.1 %collective-permute-start.12 = (bf16[256,256]{1,0:T(8,128)(2,1)S(1)}, bf16[256,256]{1,0:T(8,128)(2,1)S(1)}, u32[]{:S(2)}, u32[]{:S(2)}) collective-permute-start(bf16[256,256]{1,0:T(8,128)(2,1)S(1)} %collective-permute-done.10.refs_1_), channel_id=1, source_target_pairs={{0,120},{8,0},{16,8},{24,16},{32,24},{40,32},{48,40},{56,48},{64,5... | collective-permute-start | bytes 393224 | tf_op jit(solution)/shard_map/ppermute | solution.py:43
  157.8 3.1 %collective-permute-done.9.refs_0_ = bf16[256,256]{1,0:T(8,128)(2,1)S(1)} collective-permute-done((bf16[256,256]{1,0:T(8,128)(2,1)S(1)}, bf16[256,256]{1,0:T(8,128)(2,1)S(1)}, u32[]{:S(2)}, u32[]{:S(2)}) %collective-permute-start.9) | collective-permute-done | bytes 131104 | tf_op jit(solution)/shard_map/ppermute | solution.py:43
  160.9 1.9 collective-permute-start.11
  162.9 5.1 %collective-permute-start.14 = (bf16[256,256]{1,0:T(8,128)(2,1)S(1)}, bf16[256,256]{1,0:T(8,128)(2,1)S(1)}, u32[]{:S(2)}, u32[]{:S(2)}) collective-permute-start(bf16[256,256]{1,0:T(8,128)(2,1)S(1)} %collective-permute-done.12.refs_1_), channel_id=1, source_target_pairs={{0,120},{8,0},{16,8},{24,16},{32,24},{40,32},{48,40},{56,48},{64,5... | collective-permute-start | bytes 393224 | tf_op jit(solution)/shard_map/ppermute | solution.py:43
  169.6 2.3 collective-permute-done.11.refs_0_
  171.9 1.9 collective-permute-start.13
  173.8 5.2 %collective-permute-start.16 = (bf16[256,256]{1,0:T(8,128)(2,1)S(1)}, bf16[256,256]{1,0:T(8,128)(2,1)S(1)}, u32[]{:S(2)}, u32[]{:S(2)}) collective-permute-start(bf16[256,256]{1,0:T(8,128)(2,1)S(1)} %collective-permute-done.14.refs_1_), channel_id=1, source_target_pairs={{0,120},{8,0},{16,8},{24,16},{32,24},{40,32},{48,40},{56,48},{64,5... | collective-permute-start | bytes 393224 | tf_op jit(solution)/shard_map/ppermute | solution.py:43
  182.4 1.9 collective-permute-start.15
  185.9 4.5 %collective-permute-done.15.refs_0_ = bf16[256,256]{1,0:T(8,128)(2,1)S(1)} collective-permute-done((bf16[256,256]{1,0:T(8,128)(2,1)S(1)}, bf16[256,256]{1,0:T(8,128)(2,1)S(1)}, u32[]{:S(2)}, u32[]{:S(2)}) %collective-permute-start.15) | collective-permute-done | bytes 131104 | tf_op jit(solution)/shard_map/ppermute | solution.py:43
  190.4 2.2 copy-done.2
  192.6 3.1 %shard_map.82 = bf16[8,256,512]{2,1,0:T(8,128)(2,1)S(1)} custom-call(s32[2]{0:T(128)S(1)} %fusion.8.starts_ref, bf16[256,768]{1,0:T(8,128)(2,1)S(1)} %collective-permute-done.2.query_ref.refs_0_, s32[1,256]{1,0:T(1,128)S(1)} %fusion.2.query_pos_ref, f32[4,1,256]{2,1,0:T(1,128)S(1)} %get-tuple-element.127.peak_ref, ...), custom_call_target="tpu_custom_call" | custom-call | flops 1073741824 | bytes 8388608 | tf_op jit(solution)/shard_map/pallas_call | solution.py:231
  195.7 26.9 %all_to_all.10 = bf16[8,256,512]{2,1,0:T(8,128)(2,1)S(1)} all-to-all(bf16[8,256,512]{2,1,0:T(8,128)(2,1)S(1)} %shard_map.82), channel_id=1, replica_groups=mesh['pipe'=4,'ctx'=16,'tp'=8] {'tp'}, dimensions={0} | all-to-all | bytes 4194304 | tf_op jit(solution)/shard_map/all_to_all | solution.py:328
  (77 shorter events, 28.1 us)
Async XLA Ops:
  6.5 16.2 %copy-start.3 = (bf16[1,256,512]{2,1,0:T(8,128)(2,1)S(1)}, bf16[1,256,512]{2,1,0:T(8,128)(2,1)}, u32[]{:S(2)}) copy-start(bf16[1,256,512]{2,1,0:T(8,128)(2,1)} %param.13) | copy-start | bytes 786436
  6.5 16.0 %copy-start.6 = (f32[1,512]{1,0:T(1,128)S(1)}, f32[1,512]{1,0:T(1,128)}, u32[]{:S(2)}) copy-start(f32[1,512]{1,0:T(1,128)} %param.15) | copy-start | bytes 6148
  6.5 93.2 %all-gather.4.cloned.1.call-start = ((), (), s32[]{:S(2)}) async-start(), calls=%async_computation.2 | async-start | bytes 6684672 | tf_op jit(solution)/shard_map/all_gather | solution.py:262
  8.4 182.0 %all-gather.6.cloned.1.call-start = ((), (), s32[]{:S(2)}) async-start(), calls=%async_computation.3 | async-start | bytes 4456448 | tf_op jit(solution)/shard_map/all_gather | solution.py:267
  10.4 10.5 %collective-permute-start = (bf16[512,512]{1,0:T(8,128)(2,1)S(1)}, bf16[512,512]{1,0:T(8,128)(2,1)S(1)}, u32[]{:S(2)}, u32[]{:S(2)}) collective-permute-start(bf16[512,512]{1,0:T(8,128)(2,1)S(1)} %maximum_maximum_fusion), channel_id=1, source_target_pairs={{0,128},{128,256},{256,384},{384,0},{1,129},{129,257},{257,385},{3... | collective-permute-start | bytes 1572872 | tf_op jit(solution)/shard_map/ppermute | solution.py:19
  20.9 0.9 copy-start.4
  24.3 9.7 %copy-start.7 = (s32[32]{0:T(128)S(1)}, s32[32]{0:T(128)}, u32[]{:S(2)}) copy-start(s32[32]{0:T(128)} %param.14) | copy-start | bytes 388
  24.3 33.8 %all-to-all-start = ((bf16[8,272,512]{2,1,0:T(8,128)(2,1)}), bf16[8,272,512]{2,1,0:T(8,128)(2,1)S(1)}, u32[]{:S(2)}, u32[]{:S(2)}) async-start(bf16[8,272,512]{2,1,0:T(8,128)(2,1)} %broadcast_in_dim.112), calls=%async_computation | async-start | bytes 4456448 | tf_op jit(solution)/shard_map/all_to_all | solution.py:275
  58.1 1.4 copy-start
  59.5 1.7 copy-start.1
  102.3 11.5 %collective-permute-start.1 = (bf16[256,256]{1,0:T(8,128)(2,1)S(1)}, bf16[256,256]{1,0:T(8,128)(2,1)S(1)}, u32[]{:S(2)}, u32[]{:S(2)}) collective-permute-start(bf16[256,256]{1,0:T(8,128)(2,1)S(1)} %shard_map.74.keys_values_ref), channel_id=1, source_target_pairs={{0,136},{8,144},{16,152},{24,160},{32,168},{40,176},{48,184},{56,1... | collective-permute-start | bytes 393224 | tf_op jit(solution)/shard_map/ppermute | solution.py:43
  104.3 11.6 %collective-permute-start.3 = (bf16[256,256]{1,0:T(8,128)(2,1)S(1)}, bf16[256,256]{1,0:T(8,128)(2,1)S(1)}, u32[]{:S(2)}, u32[]{:S(2)}) collective-permute-start(bf16[256,256]{1,0:T(8,128)(2,1)S(1)} %shard_map.74.keys_values_ref), channel_id=1, source_target_pairs={{0,248},{8,128},{16,136},{24,144},{32,152},{40,160},{48,168},{56,1... | collective-permute-start | bytes 393224 | tf_op jit(solution)/shard_map/ppermute | solution.py:43
  113.8 19.9 %collective-permute-start.2 = (bf16[256,768]{1,0:T(8,128)(2,1)S(1)}, bf16[256,768]{1,0:T(8,128)(2,1)S(1)}, u32[]{:S(2)}, u32[]{:S(2)}) collective-permute-start(bf16[256,768]{1,0:T(8,128)(2,1)S(1)} %shard_map.75), channel_id=1, source_target_pairs={{0,128},{128,256},{256,384},{384,0},{1,129},{129,257},{257,385},{3... | collective-permute-start | bytes 1179656 | tf_op jit(solution)/shard_map/ppermute | solution.py:19
  115.9 10.5 %collective-permute-start.4 = (bf16[256,256]{1,0:T(8,128)(2,1)S(1)}, bf16[256,256]{1,0:T(8,128)(2,1)S(1)}, u32[]{:S(2)}, u32[]{:S(2)}) collective-permute-start(bf16[256,256]{1,0:T(8,128)(2,1)S(1)} %collective-permute-done.3.refs_1_), channel_id=1, source_target_pairs={{0,8},{8,16},{16,24},{24,32},{32,40},{40,48},{48,56},{56,64},{64,7... | collective-permute-start | bytes 393224 | tf_op jit(solution)/shard_map/ppermute | solution.py:43
  119.2 9.3 %collective-permute-start.6 = (bf16[256,256]{1,0:T(8,128)(2,1)S(1)}, bf16[256,256]{1,0:T(8,128)(2,1)S(1)}, u32[]{:S(2)}, u32[]{:S(2)}) collective-permute-start(bf16[256,256]{1,0:T(8,128)(2,1)S(1)} %collective-permute-done.1.refs_2_), channel_id=1, source_target_pairs={{0,120},{8,0},{16,8},{24,16},{32,24},{40,32},{48,40},{56,48},{64,5... | collective-permute-start | bytes 393224 | tf_op jit(solution)/shard_map/ppermute | solution.py:43
  126.4 11.3 %collective-permute-start.5 = (bf16[256,256]{1,0:T(8,128)(2,1)S(1)}, bf16[256,256]{1,0:T(8,128)(2,1)S(1)}, u32[]{:S(2)}, u32[]{:S(2)}) collective-permute-start(bf16[256,256]{1,0:T(8,128)(2,1)S(1)} %collective-permute-done.4.refs_3_), channel_id=1, source_target_pairs={{0,8},{8,16},{16,24},{24,32},{32,40},{40,48},{48,56},{56,64},{64,7... | collective-permute-start | bytes 393224 | tf_op jit(solution)/shard_map/ppermute | solution.py:43
  128.6 11.1 %collective-permute-start.8 = (bf16[256,256]{1,0:T(8,128)(2,1)S(1)}, bf16[256,256]{1,0:T(8,128)(2,1)S(1)}, u32[]{:S(2)}, u32[]{:S(2)}) collective-permute-start(bf16[256,256]{1,0:T(8,128)(2,1)S(1)} %collective-permute-done.6.refs_4_), channel_id=1, source_target_pairs={{0,120},{8,0},{16,8},{24,16},{32,24},{40,32},{48,40},{56,48},{64,5... | collective-permute-start | bytes 393224 | tf_op jit(solution)/shard_map/ppermute | solution.py:43
  137.7 11.4 %collective-permute-start.7 = (bf16[256,256]{1,0:T(8,128)(2,1)S(1)}, bf16[256,256]{1,0:T(8,128)(2,1)S(1)}, u32[]{:S(2)}, u32[]{:S(2)}) collective-permute-start(bf16[256,256]{1,0:T(8,128)(2,1)S(1)} %collective-permute-done.5.refs_0_), channel_id=1, source_target_pairs={{0,8},{8,16},{16,24},{24,32},{32,40},{40,48},{48,56},{56,64},{64,7... | collective-permute-start | bytes 393224 | tf_op jit(solution)/shard_map/ppermute | solution.py:43
  139.7 11.4 %collective-permute-start.10 = (bf16[256,256]{1,0:T(8,128)(2,1)S(1)}, bf16[256,256]{1,0:T(8,128)(2,1)S(1)}, u32[]{:S(2)}, u32[]{:S(2)}) collective-permute-start(bf16[256,256]{1,0:T(8,128)(2,1)S(1)} %collective-permute-done.8.refs_1_), channel_id=1, source_target_pairs={{0,120},{8,0},{16,8},{24,16},{32,24},{40,32},{48,40},{56,48},{64,5... | collective-permute-start | bytes 393224 | tf_op jit(solution)/shard_map/ppermute | solution.py:43
  149.2 11.8 %collective-permute-start.9 = (bf16[256,256]{1,0:T(8,128)(2,1)S(1)}, bf16[256,256]{1,0:T(8,128)(2,1)S(1)}, u32[]{:S(2)}, u32[]{:S(2)}) collective-permute-start(bf16[256,256]{1,0:T(8,128)(2,1)S(1)} %collective-permute-done.7.refs_0_), channel_id=1, source_target_pairs={{0,8},{8,16},{16,24},{24,32},{32,40},{40,48},{48,56},{56,64},{64,7... | collective-permute-start | bytes 393224 | tf_op jit(solution)/shard_map/ppermute | solution.py:43
  151.1 11.8 %collective-permute-start.12 = (bf16[256,256]{1,0:T(8,128)(2,1)S(1)}, bf16[256,256]{1,0:T(8,128)(2,1)S(1)}, u32[]{:S(2)}, u32[]{:S(2)}) collective-permute-start(bf16[256,256]{1,0:T(8,128)(2,1)S(1)} %collective-permute-done.10.refs_1_), channel_id=1, source_target_pairs={{0,120},{8,0},{16,8},{24,16},{32,24},{40,32},{48,40},{56,48},{64,5... | collective-permute-start | bytes 393224 | tf_op jit(solution)/shard_map/ppermute | solution.py:43
  160.9 10.9 %collective-permute-start.11 = (bf16[256,256]{1,0:T(8,128)(2,1)S(1)}, bf16[256,256]{1,0:T(8,128)(2,1)S(1)}, u32[]{:S(2)}, u32[]{:S(2)}) collective-permute-start(bf16[256,256]{1,0:T(8,128)(2,1)S(1)} %collective-permute-done.9.refs_0_), channel_id=1, source_target_pairs={{0,8},{8,16},{16,24},{24,32},{32,40},{40,48},{48,56},{56,64},{64,7... | collective-permute-start | bytes 393224 | tf_op jit(solution)/shard_map/ppermute | solution.py:43
  162.9 10.9 %collective-permute-start.14 = (bf16[256,256]{1,0:T(8,128)(2,1)S(1)}, bf16[256,256]{1,0:T(8,128)(2,1)S(1)}, u32[]{:S(2)}, u32[]{:S(2)}) collective-permute-start(bf16[256,256]{1,0:T(8,128)(2,1)S(1)} %collective-permute-done.12.refs_1_), channel_id=1, source_target_pairs={{0,120},{8,0},{16,8},{24,16},{32,24},{40,32},{48,40},{56,48},{64,5... | collective-permute-start | bytes 393224 | tf_op jit(solution)/shard_map/ppermute | solution.py:43
  171.9 10.5 %collective-permute-start.13 = (bf16[256,256]{1,0:T(8,128)(2,1)S(1)}, bf16[256,256]{1,0:T(8,128)(2,1)S(1)}, u32[]{:S(2)}, u32[]{:S(2)}) collective-permute-start(bf16[256,256]{1,0:T(8,128)(2,1)S(1)} %collective-permute-done.11.refs_0_), channel_id=1, source_target_pairs={{0,8},{8,16},{16,24},{24,32},{32,40},{40,48},{48,56},{56,64},{64,7... | collective-permute-start | bytes 393224 | tf_op jit(solution)/shard_map/ppermute | solution.py:43
  173.8 10.5 %collective-permute-start.16 = (bf16[256,256]{1,0:T(8,128)(2,1)S(1)}, bf16[256,256]{1,0:T(8,128)(2,1)S(1)}, u32[]{:S(2)}, u32[]{:S(2)}) collective-permute-start(bf16[256,256]{1,0:T(8,128)(2,1)S(1)} %collective-permute-done.14.refs_1_), channel_id=1, source_target_pairs={{0,120},{8,0},{16,8},{24,16},{32,24},{40,32},{48,40},{56,48},{64,5... | collective-permute-start | bytes 393224 | tf_op jit(solution)/shard_map/ppermute | solution.py:43
  182.4 8.1 %collective-permute-start.15 = (bf16[256,256]{1,0:T(8,128)(2,1)S(1)}, bf16[256,256]{1,0:T(8,128)(2,1)S(1)}, u32[]{:S(2)}, u32[]{:S(2)}) collective-permute-start(bf16[256,256]{1,0:T(8,128)(2,1)S(1)} %collective-permute-done.13.refs_0_), channel_id=1, source_target_pairs={{0,8},{8,16},{16,24},{24,32},{32,40},{40,48},{48,56},{56,64},{64,7... | collective-permute-start | bytes 393224 | tf_op jit(solution)/shard_map/ppermute | solution.py:43
  190.4 2.2 copy-start.2
  222.7 1.0 copy-start.5
Sparse Core Ops, SparseCore 0:
  9.4 90.2 all-gather.3
  101.8 85.1 all-gather.5

commit v6 on v5

--- a/solution.py
+++ b/solution.py
@@ -194,16 +194,15 @@
 
 
 def finish_kernel(starts_ref, query_ref, query_pos_ref, peak_ref, total_ref, accum_ref, *refs):
-    weights_ref, out_ref, context_ref = refs[-3:]
+    weights_ref, even_ref, odd_ref, context_ref = refs[-4:]
     blocks, depth, packed = weights_ref.shape
     size = accum_ref.shape[1]
-    per = out_ref.shape[0] * out_ref.shape[2] // blocks
-    share = out_ref.shape[2] // per
+    per = even_ref.shape[2]
 
     @pl.when(pl.program_id(0) == 0)
     def _():
         results = attended(
-            starts_ref, query_ref, query_pos_ref, (peak_ref, total_ref, accum_ref), refs[:-3]
+            starts_ref, query_ref, query_pos_ref, (peak_ref, total_ref, accum_ref), refs[:-4]
         )
         for head, (_, total, accum) in enumerate(results):
             context = (accum / total).T
@@ -218,8 +217,8 @@
                 preferred_element_type=jnp.float32,
             )
             total = term if total is None else total + term
-        column = (at % share) * per
-        out_ref[at // share, :, column : column + per] = total.astype(out_ref.dtype)
+        out_ref = odd_ref if at % 2 else even_ref
+        out_ref[at // 2] = total.astype(out_ref.dtype)
 
 
 def finish(starts, query, query_pos, state, held, packed, n_tp):
@@ -231,11 +230,11 @@
     return pl.pallas_call(
         finish_kernel,
         grid=(steps,),
-        out_shape=jax.ShapeDtypeStruct((n_tp, rows, part), jnp.bfloat16),
+        out_shape=[jax.ShapeDtypeStruct((n_tp, rows, part // 2), jnp.bfloat16)] * 2,
         in_specs=[pl.BlockSpec(memory_space=pltpu.SMEM)]
         + [pl.BlockSpec(memory_space=pltpu.VMEM)] * len(whole)
         + [pl.BlockSpec((n_ctx // steps, deep, wide), lambda k: (k, 0, 0))],
-        out_specs=pl.BlockSpec((n_tp // steps, rows, part), lambda k: (k, 0, 0)),
+        out_specs=[pl.BlockSpec((n_tp // steps, rows, part // 2), lambda k: (k, 0, 0))] * 2,
         scratch_shapes=[pltpu.VMEM((rows, part), jnp.bfloat16)],
         compiler_params=pltpu.CompilerParams(
             dimension_semantics=("arbitrary",), vmem_limit_bytes=16 * MIB
@@ -325,8 +324,8 @@
     terms = finish(
         starts_of(waiting), own, query_pos, state, [arrived[t] for t in waiting], packed, n_tp
     )
-    parts = lax.all_to_all(terms, "tp", 0, 0)
-    summed = jnp.sum(parts.astype(jnp.float32), axis=0)
+    parts = [lax.all_to_all(term, "tp", 0, 0) for term in terms]
+    summed = jnp.concatenate([jnp.sum(p.astype(jnp.float32), axis=0) for p in parts], axis=1)
     return (residual.astype(jnp.float32) + summed).astype(jnp.bfloat16)[None]
 
 

time: 233 us -> 241 us (1.034)
  waiting for transfers between devices: 87.8 us -> 98.1 us
  blocking collectives: 26.9 us -> 17.7 us
  starting transfers between devices: 65.1 us -> 71 us
    all_to_all x0 -> x1, waiting for transfers between devices: none -> 10.6 us  [shards(): parts = [lax.all_to_all(term, 'tp', 0, 0) for term in terms]]
    all_to_all x1, blocking collectives: 26.9 us -> 17.7 us  [shards(): parts = [lax.all_to_all(term, 'tp', 0, 0) for term in terms]]
    all_to_all x0 -> x1, starting transfers between devices: none -> 5.73 us  [shards(): parts = [lax.all_to_all(term, 'tp', 0, 0) for term in terms]]
  transfers between devices with their start and end apart: 20 -> 21, of which waited for: 10 -> 11; matrix products, arithmetic and copies ran while one was open for 5% -> 5% of each run, Pallas kernels for 6% -> 6%
where the time goes in v6:
time: 241 us; the launch traced here: 238 us
  waiting for transfers between devices  98.1 us (41%)
  starting transfers between devices  71 us (29%)
  Pallas kernels  18 us (7%)
  blocking collectives  17.7 us (7%)
  between operations  14.1 us (6%)
  local copies, waits for them, and re-layouts  13.8 us (6%)
  other arithmetic  5.76 us (2%)
    ppermute x15, starting transfers between devices, round_ctx(): return lax.ppermute(value, ('pipe', 'ctx'), pairs)  51.9 us
    all_gather x1, waiting for transfers between devices, shards(): w_all = lax.all_gather(w_mine, 'ctx', axis=0, tiled=True)  37.6 us
    all_to_all x1, waiting for transfers between devices, shards(): lax.all_to_all(jnp.broadcast_to(payload[None], (n_tp,) + payload.shape),...  22.9 us
    ppermute x15, waiting for transfers between devices, round_ctx(): return lax.ppermute(value, ('pipe', 'ctx'), pairs)  18.5 us
    all_to_all x1, blocking collectives, shards(): parts = [lax.all_to_all(term, 'tp', 0, 0) for term in terms]  17.7 us
    pallas_call x6, Pallas kernels, attend(): pl.pallas_call(attend_kernel, out_shape=[jax.ShapeDtypeStruct(part.shape,...  10.7 us
    all_to_all x1, waiting for transfers between devices, shards(): parts = [lax.all_to_all(term, 'tp', 0, 0) for term in terms]  10.6 us
    all_to_all x1, starting transfers between devices, shards(): lax.all_to_all(jnp.broadcast_to(payload[None], (n_tp,) + payload.shape),...  9.51 us
  transfers between devices with their start and end apart: 21, of which 11 were waited for; matrix products, arithmetic and copies ran while one was open for 5% of the time, Pallas kernels for 6%

profile of v6, /device:TPU:6, one launch (start us, length us, event | category | flops | bytes accessed | tf_op | source)
XLA Modules:
  0.0 238.4 jit_solution(15965613763044778830)
XLA Ops:
  10.4 1.9 collective-permute-start
  12.4 8.6 %collective-permute-done = bf16[512,512]{1,0:T(8,128)(2,1)S(1)} collective-permute-done((bf16[512,512]{1,0:T(8,128)(2,1)S(1)}, bf16[512,512]{1,0:T(8,128)(2,1)S(1)}, u32[]{:S(2)}, u32[]{:S(2)}) %collective-permute-start) | collective-permute-done | bytes 524320 | tf_op jit(solution)/shard_map/ppermute | solution.py:19
  24.3 9.5 %all-to-all-start = ((bf16[8,272,512]{2,1,0:T(8,128)(2,1)}), bf16[8,272,512]{2,1,0:T(8,128)(2,1)S(1)}, u32[]{:S(2)}, u32[]{:S(2)}) async-start(bf16[8,272,512]{2,1,0:T(8,128)(2,1)} %broadcast_in_dim.112), calls=%async_computation | async-start | bytes 4456448 | tf_op jit(solution)/shard_map/all_to_all | solution.py:274
  35.2 22.9 %all-to-all-done.spread_ref = bf16[8,272,512]{2,1,0:T(8,128)(2,1)S(1)} async-done(((bf16[8,272,512]{2,1,0:T(8,128)(2,1)}), bf16[8,272,512]{2,1,0:T(8,128)(2,1)S(1)}, u32[]{:S(2)}, u32[]{:S(2)}) %all-to-all-start) | async-done | bytes 2228256 | tf_op jit(solution)/shard_map/all_to_all | solution.py:274
  62.2 37.6 %all-gather.4.cloned.1.call-done = bf16[4096,768]{1,0:T(8,128)(2,1)} async-done(((bf16[256,768]{1,0:T(8,128)(2,1)}), bf16[4096,768]{1,0:T(8,128)(2,1)}) %all-gather.4.cloned.1.call-update) | async-done | bytes 6291472 | tf_op jit(solution)/shard_map/all_gather | solution.py:261
  102.3 1.9 collective-permute-start.1
  104.3 5.6 %collective-permute-start.3 = (bf16[256,256]{1,0:T(8,128)(2,1)S(1)}, bf16[256,256]{1,0:T(8,128)(2,1)S(1)}, u32[]{:S(2)}, u32[]{:S(2)}) collective-permute-start(bf16[256,256]{1,0:T(8,128)(2,1)S(1)} %shard_map.74.keys_values_ref), channel_id=1, source_target_pairs={{0,248},{8,128},{16,136},{24,144},{32,152},{40,160},{48,168},{56,1... | collective-permute-start | bytes 393224 | tf_op jit(solution)/shard_map/ppermute | solution.py:43
  109.9 2.5 %slice.66.weights_ref = bf16[4096,512]{1,0:T(8,128)(2,1)S(1)} slice(bf16[4096,768]{1,0:T(8,128)(2,1)} %all-gather.4.cloned.1.call-done), slice={[0:4096], [0:512]} | slice | bytes 8388608 | tf_op jit(solution)/shard_map/slice | solution.py:294
  113.8 1.9 collective-permute-start.2
  115.9 3.2 %collective-permute-start.4 = (bf16[256,256]{1,0:T(8,128)(2,1)S(1)}, bf16[256,256]{1,0:T(8,128)(2,1)S(1)}, u32[]{:S(2)}, u32[]{:S(2)}) collective-permute-start(bf16[256,256]{1,0:T(8,128)(2,1)S(1)} %collective-permute-done.3.refs_1_), channel_id=1, source_target_pairs={{0,8},{8,16},{16,24},{24,32},{32,40},{40,48},{48,56},{56,64},{64,7... | collective-permute-start | bytes 393224 | tf_op jit(solution)/shard_map/ppermute | solution.py:43
  119.2 3.9 %collective-permute-start.6 = (bf16[256,256]{1,0:T(8,128)(2,1)S(1)}, bf16[256,256]{1,0:T(8,128)(2,1)S(1)}, u32[]{:S(2)}, u32[]{:S(2)}) collective-permute-start(bf16[256,256]{1,0:T(8,128)(2,1)S(1)} %collective-permute-done.1.refs_2_), channel_id=1, source_target_pairs={{0,120},{8,0},{16,8},{24,16},{32,24},{40,32},{48,40},{56,48},{64,5... | collective-permute-start | bytes 393224 | tf_op jit(solution)/shard_map/ppermute | solution.py:43
  123.2 3.2 %collective-permute-done.4.refs_3_ = bf16[256,256]{1,0:T(8,128)(2,1)S(1)} collective-permute-done((bf16[256,256]{1,0:T(8,128)(2,1)S(1)}, bf16[256,256]{1,0:T(8,128)(2,1)S(1)}, u32[]{:S(2)}, u32[]{:S(2)}) %collective-permute-start.4) | collective-permute-done | bytes 131104 | tf_op jit(solution)/shard_map/ppermute | solution.py:43
  126.4 1.9 collective-permute-start.5
  128.6 5.1 %collective-permute-start.8 = (bf16[256,256]{1,0:T(8,128)(2,1)S(1)}, bf16[256,256]{1,0:T(8,128)(2,1)S(1)}, u32[]{:S(2)}, u32[]{:S(2)}) collective-permute-start(bf16[256,256]{1,0:T(8,128)(2,1)S(1)} %collective-permute-done.6.refs_4_), channel_id=1, source_target_pairs={{0,120},{8,0},{16,8},{24,16},{32,24},{40,32},{48,40},{56,48},{64,5... | collective-permute-start | bytes 393224 | tf_op jit(solution)/shard_map/ppermute | solution.py:43
  133.8 2.7 %shard_map.76 = (f32[4,1,256]{2,1,0:T(1,128)S(1)}, f32[4,1,256]{2,1,0:T(1,128)S(1)}, f32[4,128,256]{2,1,0:T(8,128)S(1)}) custom-call(s32[10]{0:T(128)S(1)} %fusion.10.starts_ref, bf16[256,768]{1,0:T(8,128)(2,1)S(1)} %collective-permute-done.2.query_ref.refs_0_, s32[1,256]{1,0:T(1,128)S(1)} %fusion.3.query_pos_ref, ...), custom_call_target="tpu_custom_call" | custom-call | flops 671088640 | bytes 655360 | tf_op jit(solution)/shard_map/pallas_call | solution.py:182
  137.7 1.9 collective-permute-start.7
  139.7 5.1 %collective-permute-start.10 = (bf16[256,256]{1,0:T(8,128)(2,1)S(1)}, bf16[256,256]{1,0:T(8,128)(2,1)S(1)}, u32[]{:S(2)}, u32[]{:S(2)}) collective-permute-start(bf16[256,256]{1,0:T(8,128)(2,1)S(1)} %collective-permute-done.8.refs_1_), channel_id=1, source_target_pairs={{0,120},{8,0},{16,8},{24,16},{32,24},{40,32},{48,40},{56,48},{64,5... | collective-permute-start | bytes 393224 | tf_op jit(solution)/shard_map/ppermute | solution.py:43
  146.4 2.5 %collective-permute-done.7.refs_0_ = bf16[256,256]{1,0:T(8,128)(2,1)S(1)} collective-permute-done((bf16[256,256]{1,0:T(8,128)(2,1)S(1)}, bf16[256,256]{1,0:T(8,128)(2,1)S(1)}, u32[]{:S(2)}, u32[]{:S(2)}) %collective-permute-start.7) | collective-permute-done | bytes 131104 | tf_op jit(solution)/shard_map/ppermute | solution.py:43
  148.9 1.9 collective-permute-start.9
  150.8 5.1 %collective-permute-start.12 = (bf16[256,256]{1,0:T(8,128)(2,1)S(1)}, bf16[256,256]{1,0:T(8,128)(2,1)S(1)}, u32[]{:S(2)}, u32[]{:S(2)}) collective-permute-start(bf16[256,256]{1,0:T(8,128)(2,1)S(1)} %collective-permute-done.10.refs_1_), channel_id=1, source_target_pairs={{0,120},{8,0},{16,8},{24,16},{32,24},{40,32},{48,40},{56,48},{64,5... | collective-permute-start | bytes 393224 | tf_op jit(solution)/shard_map/ppermute | solution.py:43
  157.6 2.1 collective-permute-done.9.refs_0_
  161.6 5.1 %collective-permute-start.14 = (bf16[256,256]{1,0:T(8,128)(2,1)S(1)}, bf16[256,256]{1,0:T(8,128)(2,1)S(1)}, u32[]{:S(2)}, u32[]{:S(2)}) collective-permute-start(bf16[256,256]{1,0:T(8,128)(2,1)S(1)} %collective-permute-done.12.refs_1_), channel_id=1, source_target_pairs={{0,120},{8,0},{16,8},{24,16},{32,24},{40,32},{48,40},{56,48},{64,5... | collective-permute-start | bytes 393224 | tf_op jit(solution)/shard_map/ppermute | solution.py:43
  168.4 2.9 %collective-permute-done.11.refs_0_ = bf16[256,256]{1,0:T(8,128)(2,1)S(1)} collective-permute-done((bf16[256,256]{1,0:T(8,128)(2,1)S(1)}, bf16[256,256]{1,0:T(8,128)(2,1)S(1)}, u32[]{:S(2)}, u32[]{:S(2)}) %collective-permute-start.11) | collective-permute-done | bytes 131104 | tf_op jit(solution)/shard_map/ppermute | solution.py:43
  173.2 5.1 %collective-permute-start.16 = (bf16[256,256]{1,0:T(8,128)(2,1)S(1)}, bf16[256,256]{1,0:T(8,128)(2,1)S(1)}, u32[]{:S(2)}, u32[]{:S(2)}) collective-permute-start(bf16[256,256]{1,0:T(8,128)(2,1)S(1)} %collective-permute-done.14.refs_1_), channel_id=1, source_target_pairs={{0,120},{8,0},{16,8},{24,16},{32,24},{40,32},{48,40},{56,48},{64,5... | collective-permute-start | bytes 393224 | tf_op jit(solution)/shard_map/ppermute | solution.py:43
  180.0 2.2 collective-permute-done.13.refs_0_
  182.2 2.1 collective-permute-start.15
  185.9 4.3 %collective-permute-done.15.refs_0_ = bf16[256,256]{1,0:T(8,128)(2,1)S(1)} collective-permute-done((bf16[256,256]{1,0:T(8,128)(2,1)S(1)}, bf16[256,256]{1,0:T(8,128)(2,1)S(1)}, u32[]{:S(2)}, u32[]{:S(2)}) %collective-permute-start.15) | collective-permute-done | bytes 131104 | tf_op jit(solution)/shard_map/ppermute | solution.py:43
  190.3 2.2 copy-done.2
  192.5 4.1 %shard_map.82 = (bf16[8,256,256]{2,1,0:T(8,128)(2,1)}, bf16[8,256,256]{2,1,0:T(8,128)(2,1)S(1)}) custom-call(s32[2]{0:T(128)S(1)} %fusion.9.starts_ref, bf16[256,768]{1,0:T(8,128)(2,1)S(1)} %collective-permute-done.2.query_ref.refs_0_, s32[1,256]{1,0:T(1,128)S(1)} %fusion.3.query_pos_ref, f32[4,1,256]{2,1,0:T(1,128)S(1)} %get-tuple-element.129.peak_ref, ...), custom_call_target="tpu_custom_call" | custom-call | flops 1073741824 | bytes 8388608 | tf_op jit(solution)/shard_map/pallas_call | solution.py:230
  196.5 17.7 %all_to_all.15 = bf16[8,256,256]{2,1,0:T(8,128)(2,1)S(1)} all-to-all(bf16[8,256,256]{2,1,0:T(8,128)(2,1)S(1)} %get-tuple-element.134), channel_id=1, replica_groups=mesh['pipe'=4,'ctx'=16,'tp'=8] {'tp'}, dimensions={0} | all-to-all | bytes 2097152 | tf_op jit(solution)/shard_map/all_to_all | solution.py:327
  214.2 5.7 %all-to-all-start.1 = ((bf16[8,256,256]{2,1,0:T(8,128)(2,1)}), bf16[8,256,256]{2,1,0:T(8,128)(2,1)S(1)}, u32[]{:S(2)}, u32[]{:S(2)}) async-start(bf16[8,256,256]{2,1,0:T(8,128)(2,1)} %get-tuple-element.133), calls=%async_computation.1 | async-start | bytes 2097152 | tf_op jit(solution)/shard_map/all_to_all | solution.py:327
  220.1 10.6 %all-to-all-done.1 = bf16[8,256,256]{2,1,0:T(8,128)(2,1)S(1)} async-done(((bf16[8,256,256]{2,1,0:T(8,128)(2,1)}), bf16[8,256,256]{2,1,0:T(8,128)(2,1)S(1)}, u32[]{:S(2)}, u32[]{:S(2)}) %all-to-all-start.1) | async-done | bytes 1048608 | tf_op jit(solution)/shard_map/all_to_all | solution.py:327
  (80 shorter events, 31.3 us)
Async XLA Ops:
  6.5 16.2 %copy-start.3 = (bf16[1,256,512]{2,1,0:T(8,128)(2,1)S(1)}, bf16[1,256,512]{2,1,0:T(8,128)(2,1)}, u32[]{:S(2)}) copy-start(bf16[1,256,512]{2,1,0:T(8,128)(2,1)} %param.13) | copy-start | bytes 786436
  6.5 16.0 %copy-start.6 = (f32[1,512]{1,0:T(1,128)S(1)}, f32[1,512]{1,0:T(1,128)}, u32[]{:S(2)}) copy-start(f32[1,512]{1,0:T(1,128)} %param.15) | copy-start | bytes 6148
  6.5 93.2 %all-gather.4.cloned.1.call-start = ((), (), s32[]{:S(2)}) async-start(), calls=%async_computation.3 | async-start | bytes 6684672 | tf_op jit(solution)/shard_map/all_gather | solution.py:261
  8.4 181.9 %all-gather.6.cloned.1.call-start = ((), (), s32[]{:S(2)}) async-start(), calls=%async_computation.4 | async-start | bytes 4456448 | tf_op jit(solution)/shard_map/all_gather | solution.py:266
  10.4 10.5 %collective-permute-start = (bf16[512,512]{1,0:T(8,128)(2,1)S(1)}, bf16[512,512]{1,0:T(8,128)(2,1)S(1)}, u32[]{:S(2)}, u32[]{:S(2)}) collective-permute-start(bf16[512,512]{1,0:T(8,128)(2,1)S(1)} %maximum_maximum_fusion), channel_id=1, source_target_pairs={{0,128},{128,256},{256,384},{384,0},{1,129},{129,257},{257,385},{3... | collective-permute-start | bytes 1572872 | tf_op jit(solution)/shard_map/ppermute | solution.py:19
  20.9 0.9 copy-start.4
  24.3 9.7 %copy-start.7 = (s32[32]{0:T(128)S(1)}, s32[32]{0:T(128)}, u32[]{:S(2)}) copy-start(s32[32]{0:T(128)} %param.14) | copy-start | bytes 388
  24.3 33.8 %all-to-all-start = ((bf16[8,272,512]{2,1,0:T(8,128)(2,1)}), bf16[8,272,512]{2,1,0:T(8,128)(2,1)S(1)}, u32[]{:S(2)}, u32[]{:S(2)}) async-start(bf16[8,272,512]{2,1,0:T(8,128)(2,1)} %broadcast_in_dim.112), calls=%async_computation | async-start | bytes 4456448 | tf_op jit(solution)/shard_map/all_to_all | solution.py:274
  58.1 1.4 copy-start
  59.5 1.7 copy-start.1
  102.3 11.5 %collective-permute-start.1 = (bf16[256,256]{1,0:T(8,128)(2,1)S(1)}, bf16[256,256]{1,0:T(8,128)(2,1)S(1)}, u32[]{:S(2)}, u32[]{:S(2)}) collective-permute-start(bf16[256,256]{1,0:T(8,128)(2,1)S(1)} %shard_map.74.keys_values_ref), channel_id=1, source_target_pairs={{0,136},{8,144},{16,152},{24,160},{32,168},{40,176},{48,184},{56,1... | collective-permute-start | bytes 393224 | tf_op jit(solution)/shard_map/ppermute | solution.py:43
  104.3 11.6 %collective-permute-start.3 = (bf16[256,256]{1,0:T(8,128)(2,1)S(1)}, bf16[256,256]{1,0:T(8,128)(2,1)S(1)}, u32[]{:S(2)}, u32[]{:S(2)}) collective-permute-start(bf16[256,256]{1,0:T(8,128)(2,1)S(1)} %shard_map.74.keys_values_ref), channel_id=1, source_target_pairs={{0,248},{8,128},{16,136},{24,144},{32,152},{40,160},{48,168},{56,1... | collective-permute-start | bytes 393224 | tf_op jit(solution)/shard_map/ppermute | solution.py:43
  113.8 19.9 %collective-permute-start.2 = (bf16[256,768]{1,0:T(8,128)(2,1)S(1)}, bf16[256,768]{1,0:T(8,128)(2,1)S(1)}, u32[]{:S(2)}, u32[]{:S(2)}) collective-permute-start(bf16[256,768]{1,0:T(8,128)(2,1)S(1)} %shard_map.75), channel_id=1, source_target_pairs={{0,128},{128,256},{256,384},{384,0},{1,129},{129,257},{257,385},{3... | collective-permute-start | bytes 1179656 | tf_op jit(solution)/shard_map/ppermute | solution.py:19
  115.9 10.5 %collective-permute-start.4 = (bf16[256,256]{1,0:T(8,128)(2,1)S(1)}, bf16[256,256]{1,0:T(8,128)(2,1)S(1)}, u32[]{:S(2)}, u32[]{:S(2)}) collective-permute-start(bf16[256,256]{1,0:T(8,128)(2,1)S(1)} %collective-permute-done.3.refs_1_), channel_id=1, source_target_pairs={{0,8},{8,16},{16,24},{24,32},{32,40},{40,48},{48,56},{56,64},{64,7... | collective-permute-start | bytes 393224 | tf_op jit(solution)/shard_map/ppermute | solution.py:43
  119.2 9.3 %collective-permute-start.6 = (bf16[256,256]{1,0:T(8,128)(2,1)S(1)}, bf16[256,256]{1,0:T(8,128)(2,1)S(1)}, u32[]{:S(2)}, u32[]{:S(2)}) collective-permute-start(bf16[256,256]{1,0:T(8,128)(2,1)S(1)} %collective-permute-done.1.refs_2_), channel_id=1, source_target_pairs={{0,120},{8,0},{16,8},{24,16},{32,24},{40,32},{48,40},{56,48},{64,5... | collective-permute-start | bytes 393224 | tf_op jit(solution)/shard_map/ppermute | solution.py:43
  126.4 11.3 %collective-permute-start.5 = (bf16[256,256]{1,0:T(8,128)(2,1)S(1)}, bf16[256,256]{1,0:T(8,128)(2,1)S(1)}, u32[]{:S(2)}, u32[]{:S(2)}) collective-permute-start(bf16[256,256]{1,0:T(8,128)(2,1)S(1)} %collective-permute-done.4.refs_3_), channel_id=1, source_target_pairs={{0,8},{8,16},{16,24},{24,32},{32,40},{40,48},{48,56},{56,64},{64,7... | collective-permute-start | bytes 393224 | tf_op jit(solution)/shard_map/ppermute | solution.py:43
  128.6 11.1 %collective-permute-start.8 = (bf16[256,256]{1,0:T(8,128)(2,1)S(1)}, bf16[256,256]{1,0:T(8,128)(2,1)S(1)}, u32[]{:S(2)}, u32[]{:S(2)}) collective-permute-start(bf16[256,256]{1,0:T(8,128)(2,1)S(1)} %collective-permute-done.6.refs_4_), channel_id=1, source_target_pairs={{0,120},{8,0},{16,8},{24,16},{32,24},{40,32},{48,40},{56,48},{64,5... | collective-permute-start | bytes 393224 | tf_op jit(solution)/shard_map/ppermute | solution.py:43
  137.7 11.2 %collective-permute-start.7 = (bf16[256,256]{1,0:T(8,128)(2,1)S(1)}, bf16[256,256]{1,0:T(8,128)(2,1)S(1)}, u32[]{:S(2)}, u32[]{:S(2)}) collective-permute-start(bf16[256,256]{1,0:T(8,128)(2,1)S(1)} %collective-permute-done.5.refs_0_), channel_id=1, source_target_pairs={{0,8},{8,16},{16,24},{24,32},{32,40},{40,48},{48,56},{56,64},{64,7... | collective-permute-start | bytes 393224 | tf_op jit(solution)/shard_map/ppermute | solution.py:43
  139.7 11.1 %collective-permute-start.10 = (bf16[256,256]{1,0:T(8,128)(2,1)S(1)}, bf16[256,256]{1,0:T(8,128)(2,1)S(1)}, u32[]{:S(2)}, u32[]{:S(2)}) collective-permute-start(bf16[256,256]{1,0:T(8,128)(2,1)S(1)} %collective-permute-done.8.refs_1_), channel_id=1, source_target_pairs={{0,120},{8,0},{16,8},{24,16},{32,24},{40,32},{48,40},{56,48},{64,5... | collective-permute-start | bytes 393224 | tf_op jit(solution)/shard_map/ppermute | solution.py:43
  148.9 10.8 %collective-permute-start.9 = (bf16[256,256]{1,0:T(8,128)(2,1)S(1)}, bf16[256,256]{1,0:T(8,128)(2,1)S(1)}, u32[]{:S(2)}, u32[]{:S(2)}) collective-permute-start(bf16[256,256]{1,0:T(8,128)(2,1)S(1)} %collective-permute-done.7.refs_0_), channel_id=1, source_target_pairs={{0,8},{8,16},{16,24},{24,32},{32,40},{40,48},{48,56},{56,64},{64,7... | collective-permute-start | bytes 393224 | tf_op jit(solution)/shard_map/ppermute | solution.py:43
  150.8 10.8 %collective-permute-start.12 = (bf16[256,256]{1,0:T(8,128)(2,1)S(1)}, bf16[256,256]{1,0:T(8,128)(2,1)S(1)}, u32[]{:S(2)}, u32[]{:S(2)}) collective-permute-start(bf16[256,256]{1,0:T(8,128)(2,1)S(1)} %collective-permute-done.10.refs_1_), channel_id=1, source_target_pairs={{0,120},{8,0},{16,8},{24,16},{32,24},{40,32},{48,40},{56,48},{64,5... | collective-permute-start | bytes 393224 | tf_op jit(solution)/shard_map/ppermute | solution.py:43
  159.7 11.6 %collective-permute-start.11 = (bf16[256,256]{1,0:T(8,128)(2,1)S(1)}, bf16[256,256]{1,0:T(8,128)(2,1)S(1)}, u32[]{:S(2)}, u32[]{:S(2)}) collective-permute-start(bf16[256,256]{1,0:T(8,128)(2,1)S(1)} %collective-permute-done.9.refs_0_), channel_id=1, source_target_pairs={{0,8},{8,16},{16,24},{24,32},{32,40},{40,48},{48,56},{56,64},{64,7... | collective-permute-start | bytes 393224 | tf_op jit(solution)/shard_map/ppermute | solution.py:43
  161.6 11.6 %collective-permute-start.14 = (bf16[256,256]{1,0:T(8,128)(2,1)S(1)}, bf16[256,256]{1,0:T(8,128)(2,1)S(1)}, u32[]{:S(2)}, u32[]{:S(2)}) collective-permute-start(bf16[256,256]{1,0:T(8,128)(2,1)S(1)} %collective-permute-done.12.refs_1_), channel_id=1, source_target_pairs={{0,120},{8,0},{16,8},{24,16},{32,24},{40,32},{48,40},{56,48},{64,5... | collective-permute-start | bytes 393224 | tf_op jit(solution)/shard_map/ppermute | solution.py:43
  171.3 10.9 %collective-permute-start.13 = (bf16[256,256]{1,0:T(8,128)(2,1)S(1)}, bf16[256,256]{1,0:T(8,128)(2,1)S(1)}, u32[]{:S(2)}, u32[]{:S(2)}) collective-permute-start(bf16[256,256]{1,0:T(8,128)(2,1)S(1)} %collective-permute-done.11.refs_0_), channel_id=1, source_target_pairs={{0,8},{8,16},{16,24},{24,32},{32,40},{40,48},{48,56},{56,64},{64,7... | collective-permute-start | bytes 393224 | tf_op jit(solution)/shard_map/ppermute | solution.py:43
  173.2 11.1 %collective-permute-start.16 = (bf16[256,256]{1,0:T(8,128)(2,1)S(1)}, bf16[256,256]{1,0:T(8,128)(2,1)S(1)}, u32[]{:S(2)}, u32[]{:S(2)}) collective-permute-start(bf16[256,256]{1,0:T(8,128)(2,1)S(1)} %collective-permute-done.14.refs_1_), channel_id=1, source_target_pairs={{0,120},{8,0},{16,8},{24,16},{32,24},{40,32},{48,40},{56,48},{64,5... | collective-permute-start | bytes 393224 | tf_op jit(solution)/shard_map/ppermute | solution.py:43
  182.2 8.1 %collective-permute-start.15 = (bf16[256,256]{1,0:T(8,128)(2,1)S(1)}, bf16[256,256]{1,0:T(8,128)(2,1)S(1)}, u32[]{:S(2)}, u32[]{:S(2)}) collective-permute-start(bf16[256,256]{1,0:T(8,128)(2,1)S(1)} %collective-permute-done.13.refs_0_), channel_id=1, source_target_pairs={{0,8},{8,16},{16,24},{24,32},{32,40},{40,48},{48,56},{56,64},{64,7... | collective-permute-start | bytes 393224 | tf_op jit(solution)/shard_map/ppermute | solution.py:43
  190.3 2.2 copy-start.2
  214.2 16.6 %copy-start.5 = (bf16[512,512]{1,0:T(8,128)(2,1)S(1)}, bf16[512,512]{1,0:T(8,128)(2,1)}, u32[]{:S(2)}) copy-start(bf16[512,512]{1,0:T(8,128)(2,1)} %copy-done.4) | copy-start | bytes 1572868
  214.2 16.4 %all-to-all-start.1 = ((bf16[8,256,256]{2,1,0:T(8,128)(2,1)}), bf16[8,256,256]{2,1,0:T(8,128)(2,1)S(1)}, u32[]{:S(2)}, u32[]{:S(2)}) async-start(bf16[8,256,256]{2,1,0:T(8,128)(2,1)} %get-tuple-element.133), calls=%async_computation.1 | async-start | bytes 2097152 | tf_op jit(solution)/shard_map/all_to_all | solution.py:327
Sparse Core Ops, SparseCore 0:
  9.4 90.2 all-gather.3
  101.8 85.2 all-gather.5
